TPU v7x, 32 devices: a whole 2x2x4 slice. The times are simulated.
32 devices in a mesh: dp: 16 (over z, y, core), mp: 2 (over x).
Axes of the slice: x: 2, y: 2, z: 4, core: 2. Of those that a mesh axis runs over, the one named last changes fastest.
Arguments:
- tokens: bfloat16 [2048, 1024], P('dp'), may hold values from -6 to 6
- memory: bfloat16 [16384, 1024], P('dp'), may hold values from -6 to 6
- mem_len: int32 [16], P('dp'), may hold values from 128 to 1024, as said below
- dec_len: int32 [16], P('dp'), may hold values from 16 to 128, as said below
- cotangent: bfloat16 [2048, 1024], P('dp'), may hold values from -6 to 6
- self_qkv: bfloat16 [1024, 3, 1024], P(None, None, 'mp'), may hold values from -0.1875 to 0.1875
- self_qv_bias: float32 [2, 1024], P(None, 'mp'), may hold values from -3 to 3
- self_out: bfloat16 [1024, 1024], P('mp'), may hold values from -0.75 to 0.75
- cross_q: bfloat16 [1024, 1024], P(None, 'mp'), may hold values from -0.1875 to 0.1875
- cross_kv: bfloat16 [1024, 2, 1024], P(None, None, 'mp'), may hold values from -0.1875 to 0.1875
- cross_qv_bias: float32 [2, 1024], P(None, 'mp'), may hold values from -3 to 3
- cross_out: bfloat16 [1024, 1024], P('mp'), may hold values from -1 to 1
- fc_in: bfloat16 [1024, 4096], P(None, 'mp'), may hold values from -0.1875 to 0.1875
- fc_in_bias: float32 [4096], P('mp'), may hold values from -3 to 3
- fc_out: bfloat16 [4096, 1024], P('mp'), may hold values from -0.09375 to 0.09375
- out_bias: float32 [3, 1024], replicated, may hold values from -3 to 3
- norm_gain: float32 [3, 1024], replicated, may hold values from 0.5 to 1.5
- norm_bias: float32 [3, 1024], replicated, may hold values from -3 to 3
Outputs:
- layer_out: bfloat16 [2048, 1024], P('dp')
- grad_tokens: bfloat16 [2048, 1024], P('dp')
- grad_memory: bfloat16 [16384, 1024], P(('dp', 'mp'))
- grad_self_qkv: float32 [1024, 3, 1024], P('dp', None, 'mp')
- grad_self_qv_bias: float32 [2, 1024], P(None, 'mp')
- grad_self_out: float32 [1024, 1024], P('mp', 'dp')
- grad_cross_q: float32 [1024, 1024], P('dp', 'mp')
- grad_cross_kv: float32 [1024, 2, 1024], P('dp', None, 'mp')
- grad_cross_qv_bias: float32 [2, 1024], P(None, 'mp')
- grad_cross_out: float32 [1024, 1024], P('mp', 'dp')
- grad_fc_in: float32 [1024, 4096], P('dp', 'mp')
- grad_fc_in_bias: float32 [4096], P('mp')
- grad_fc_out: float32 [4096, 1024], P('mp', 'dp')
- grad_out_bias: float32 [3, 1024], replicated
- grad_norm_gain: float32 [3, 1024], replicated
- grad_norm_bias: float32 [3, 1024], replicated
Inputs may be any that keep to these rules, and one draw needn't show every extreme that they name: `mem_len`: an item's memory rows past its length are padding; some item has exactly 1024. `dec_len`: an item's decoder rows past its length are padding; some item has exactly 128.
All inputs are finite; a program needn't handle non-finite values.
Results may differ from a plain program's by a relative error of at most 0.023.
The roundings to bfloat16 on the way count: a program that leaves them out, or rounds other values in their place, can miss the bound.
Values may be sent and summed in bfloat16 or wider, within the bound.
A program may use at most 192 MiB of HBM per device.

v0:
```python
import jax
import jax.numpy as jnp
from jax import lax
from jax.sharding import PartitionSpec as P

HEAD = 64
TLEN = 128
MLEN = 1024


epsilon = 1e-05


def normalize(inputs, gain_row, shift_row):
    row_mean = jnp.mean(inputs, axis=-1, keepdims=True)
    centred = inputs - row_mean
    inv_std = lax.rsqrt(jnp.mean(centred * centred, axis=-1, keepdims=True) + epsilon)
    unit_rows = centred * inv_std
    return (unit_rows * gain_row + shift_row, unit_rows, inv_std)


def normalize_back(upstream, unit_rows, inv_std, gain_row):
    scaled = upstream * gain_row
    inputs_grad = inv_std * (
        scaled
        - jnp.mean(scaled, axis=-1, keepdims=True)
        - unit_rows * jnp.mean(scaled * unit_rows, axis=-1, keepdims=True)
    )
    return (inputs_grad, jnp.sum(upstream * unit_rows, axis=0), jnp.sum(upstream, axis=0))


def gelu(inputs):
    return 0.5 * inputs * (1.0 + lax.erf(inputs * 0.7071067811865476))


def gelu_slope(inputs):
    return (
        0.5 * (1.0 + lax.erf(inputs * 0.7071067811865476))
        + inputs * jnp.exp(-0.5 * inputs * inputs) * 0.3989422804014327
    )


def contract_rows(operand, other):
    return lax.dot_general(
        operand, other, (((0,), (0,)), ((), ())), preferred_element_type=jnp.float32
    )


def contract_tail(operand, weight):
    tail_dims = tuple(range(1, operand.ndim))
    return lax.dot_general(
        operand, weight, ((tail_dims, tail_dims), ((), ())), preferred_element_type=jnp.float32
    )


def forward_term(operand, weight):

    def partial_term(first_index, row_count):
        return jnp.dot(operand, weight, preferred_element_type=jnp.float32)

    return partial_term


def backward_term(operand, weight):

    def partial_term(first_index, row_count):
        return contract_tail(operand, weight)

    return partial_term


def attend(query_in, key_in, value_in, allowed):
    score_scale = query_in.shape[-1] ** (-0.5)
    scores = (
        jnp.einsum("iqhd,ikhd->ihqk", query_in, key_in, preferred_element_type=jnp.float32)
        * score_scale
    )
    scores = jnp.where(allowed[:, None], scores, -1e30)
    row_top = jnp.max(scores, axis=-1, keepdims=True)
    weights = jnp.exp(scores - row_top)
    row_total = jnp.sum(weights, axis=-1, keepdims=True)
    softmax_low = (weights / row_total).astype(jnp.bfloat16)
    mixed = jnp.einsum("ihqk,ikhd->iqhd", softmax_low, value_in, preferred_element_type=jnp.float32)
    return (mixed.astype(jnp.bfloat16), row_top + jnp.log(row_total))


def attend_back(query_in, key_in, value_in, allowed, logsum, mixed_grad):
    score_scale = query_in.shape[-1] ** (-0.5)
    scores = (
        jnp.einsum("iqhd,ikhd->ihqk", query_in, key_in, preferred_element_type=jnp.float32)
        * score_scale
    )
    scores = jnp.where(allowed[:, None], scores, -1e30)
    weights = jnp.exp(scores - logsum)
    value_grad = jnp.einsum(
        "ihqk,iqhd->ikhd",
        weights.astype(jnp.bfloat16),
        mixed_grad,
        preferred_element_type=jnp.float32,
    )
    weight_grad = jnp.einsum(
        "iqhd,ikhd->ihqk", mixed_grad, value_in, preferred_element_type=jnp.float32
    )
    score_grad = (
        weights * (weight_grad - jnp.sum(weights * weight_grad, axis=-1, keepdims=True))
    ).astype(jnp.bfloat16)
    query_grad = (
        jnp.einsum("ihqk,ikhd->iqhd", score_grad, key_in, preferred_element_type=jnp.float32)
        * score_scale
    )
    key_grad = (
        jnp.einsum("ihqk,iqhd->ikhd", score_grad, query_in, preferred_element_type=jnp.float32)
        * score_scale
    )
    return (query_grad, key_grad, value_grad)


def per_device(
    tokens,
    memory,
    mem_len,
    dec_len,
    cotangent,
    self_qkv,
    self_qv_bias,
    self_out,
    cross_q,
    cross_kv,
    cross_qv_bias,
    cross_out,
    fc_in,
    fc_in_bias,
    fc_out,
    out_bias,
    norm_gain,
    norm_bias,
):
    all_rows = tokens.shape[0]
    memory_rows = memory.shape[0]
    item_count = all_rows // TLEN
    local_width = self_out.shape[0]

    def reduce_forward(partial_term):
        return lax.psum(partial_term(0, all_rows), "mp")

    def reduce_backward(partial_term):
        return lax.psum(partial_term(0, all_rows), "mp")

    def heads_of(values, length):
        return values.reshape(item_count, length, -1, HEAD)

    position = jnp.arange(TLEN, dtype=jnp.int32)
    causal = (position[None, None, :] <= position[None, :, None]) & (
        position[None, None, :] < dec_len[:, None, None]
    )
    memory_mask = jnp.arange(MLEN, dtype=jnp.int32)[None, None, :] < mem_len[:, None, None]
    live_rows = (position[None, :] < dec_len[:, None]).reshape(all_rows, 1)
    zero_row = jnp.zeros((1, local_width), jnp.float32)
    packed = jnp.einsum("td,dcf->tcf", tokens, self_qkv, preferred_element_type=jnp.float32)
    packed = (
        packed + jnp.concatenate([self_qv_bias[:1], zero_row, self_qv_bias[1:]], axis=0)[None]
    ).astype(jnp.bfloat16)
    self_query = heads_of(packed[:, 0], TLEN)
    self_key = heads_of(packed[:, 1], TLEN)
    self_value = heads_of(packed[:, 2], TLEN)
    self_mixed, self_logsum = attend(self_query, self_key, self_value, causal)
    self_mixed = self_mixed.reshape(all_rows, local_width)
    branch = reduce_forward(forward_term(self_mixed, self_out)) + out_bias[0]
    first_norm, first_unit, first_inv = normalize(
        tokens.astype(jnp.float32) + branch, norm_gain[0], norm_bias[0]
    )
    first_full = first_norm.astype(jnp.bfloat16)
    cross_query = (
        jnp.dot(first_full, cross_q, preferred_element_type=jnp.float32) + cross_qv_bias[0]
    ).astype(jnp.bfloat16)
    cross_pair = jnp.einsum("md,dcf->mcf", memory, cross_kv, preferred_element_type=jnp.float32)
    cross_pair = (cross_pair + jnp.concatenate([zero_row, cross_qv_bias[1:]], axis=0)[None]).astype(
        jnp.bfloat16
    )
    cross_heads = heads_of(cross_query, TLEN)
    memory_key = heads_of(cross_pair[:, 0], MLEN)
    memory_value = heads_of(cross_pair[:, 1], MLEN)
    cross_mixed, cross_logsum = attend(cross_heads, memory_key, memory_value, memory_mask)
    cross_mixed = cross_mixed.reshape(all_rows, local_width)
    branch = reduce_forward(forward_term(cross_mixed, cross_out)) + out_bias[1]
    second_norm, second_unit, second_inv = normalize(
        first_norm + branch, norm_gain[1], norm_bias[1]
    )
    second_full = second_norm.astype(jnp.bfloat16)
    hidden = jnp.dot(second_full, fc_in, preferred_element_type=jnp.float32) + fc_in_bias
    active = gelu(hidden).astype(jnp.bfloat16)
    branch = reduce_forward(forward_term(active, fc_out)) + out_bias[2]
    output_norm, output_unit, output_inv = normalize(
        second_norm + branch, norm_gain[2], norm_bias[2]
    )
    layer_out = output_norm.astype(jnp.bfloat16)
    upstream = jnp.where(live_rows, cotangent.astype(jnp.float32), 0.0)
    ffn_grad, gain_output, shift_output = normalize_back(
        upstream, output_unit, output_inv, norm_gain[2]
    )
    ffn_low = ffn_grad.astype(jnp.bfloat16)
    bias_ffn = jnp.sum(ffn_low.astype(jnp.float32), axis=0)
    grad_fc_out = contract_rows(active, ffn_low)
    active_grad = contract_tail(ffn_low, fc_out)
    hidden_grad = (active_grad * gelu_slope(hidden)).astype(jnp.bfloat16)
    grad_fc_in_bias = jnp.sum(hidden_grad.astype(jnp.float32), axis=0)
    grad_fc_in = contract_rows(second_full, hidden_grad)
    second_grad = ffn_grad + reduce_backward(backward_term(hidden_grad, fc_in))
    cross_grad, gain_second, shift_second = normalize_back(
        second_grad, second_unit, second_inv, norm_gain[1]
    )
    cross_low = cross_grad.astype(jnp.bfloat16)
    bias_cross = jnp.sum(cross_low.astype(jnp.float32), axis=0)
    grad_cross_out = contract_rows(cross_mixed, cross_low)
    mixed_grad = contract_tail(cross_low, cross_out).astype(jnp.bfloat16)
    query_grad, key_grad, value_grad = attend_back(
        cross_heads, memory_key, memory_value, memory_mask, cross_logsum, heads_of(mixed_grad, TLEN)
    )
    query_grad = query_grad.reshape(all_rows, local_width).astype(jnp.bfloat16)
    pair_grad = jnp.stack(
        [key_grad.reshape(memory_rows, local_width), value_grad.reshape(memory_rows, local_width)],
        axis=1,
    ).astype(jnp.bfloat16)
    grad_cross_qv_bias = jnp.stack(
        [
            jnp.sum(query_grad.astype(jnp.float32), axis=0),
            jnp.sum(pair_grad[:, 1].astype(jnp.float32), axis=0),
        ]
    )
    grad_cross_q = contract_rows(first_full, query_grad)
    grad_cross_kv = contract_rows(memory, pair_grad)
    grad_memory = lax.psum_scatter(
        backward_term(pair_grad, cross_kv)(
            jnp.int32(0), memory_rows // lax.axis_size("mp") * lax.axis_size("mp")
        ).astype(jnp.bfloat16),
        "mp",
        scatter_dimension=0,
        tiled=True,
    )
    first_grad = cross_grad + reduce_backward(backward_term(query_grad, cross_q))
    self_grad, gain_first, shift_first = normalize_back(
        first_grad, first_unit, first_inv, norm_gain[0]
    )
    self_low = self_grad.astype(jnp.bfloat16)
    bias_self = jnp.sum(self_low.astype(jnp.float32), axis=0)
    grad_self_out = contract_rows(self_mixed, self_low)
    self_mixed_grad = contract_tail(self_low, self_out).astype(jnp.bfloat16)
    query_grad, key_grad, value_grad = attend_back(
        self_query, self_key, self_value, causal, self_logsum, heads_of(self_mixed_grad, TLEN)
    )
    packed_grad = jnp.stack(
        [
            query_grad.reshape(all_rows, local_width),
            key_grad.reshape(all_rows, local_width),
            value_grad.reshape(all_rows, local_width),
        ],
        axis=1,
    ).astype(jnp.bfloat16)
    grad_self_qv_bias = jnp.stack(
        [
            jnp.sum(packed_grad[:, 0].astype(jnp.float32), axis=0),
            jnp.sum(packed_grad[:, 2].astype(jnp.float32), axis=0),
        ]
    )
    grad_self_qkv = contract_rows(tokens, packed_grad)
    tokens_grad = self_grad + reduce_backward(backward_term(packed_grad, self_qkv))
    grad_tokens = tokens_grad.astype(jnp.bfloat16)
    bias_grads = jnp.stack([bias_self, bias_cross, bias_ffn])
    gain_grads = jnp.stack([gain_first, gain_second, gain_output])
    shift_grads = jnp.stack([shift_first, shift_second, shift_output])
    (
        grad_self_qkv,
        grad_self_out,
        grad_cross_q,
        grad_cross_kv,
        grad_cross_out,
        grad_fc_in,
        grad_fc_out,
    ) = (
        lax.psum_scatter(grad_self_qkv, "dp", scatter_dimension=0, tiled=True),
        lax.psum_scatter(grad_self_out, "dp", scatter_dimension=1, tiled=True),
        lax.psum_scatter(grad_cross_q, "dp", scatter_dimension=0, tiled=True),
        lax.psum_scatter(grad_cross_kv, "dp", scatter_dimension=0, tiled=True),
        lax.psum_scatter(grad_cross_out, "dp", scatter_dimension=1, tiled=True),
        lax.psum_scatter(grad_fc_in, "dp", scatter_dimension=0, tiled=True),
        lax.psum_scatter(grad_fc_out, "dp", scatter_dimension=1, tiled=True),
    )
    grad_self_qv_bias, grad_cross_qv_bias, grad_fc_in_bias, bias_grads, gain_grads, shift_grads = (
        lax.psum(
            (
                grad_self_qv_bias,
                grad_cross_qv_bias,
                grad_fc_in_bias,
                bias_grads,
                gain_grads,
                shift_grads,
            ),
            "dp",
        )
    )
    return (
        layer_out,
        grad_tokens,
        grad_memory,
        grad_self_qkv,
        grad_self_qv_bias,
        grad_self_out,
        grad_cross_q,
        grad_cross_kv,
        grad_cross_qv_bias,
        grad_cross_out,
        grad_fc_in,
        grad_fc_in_bias,
        grad_fc_out,
        bias_grads,
        gain_grads,
        shift_grads,
    )


def solution(mesh):
    placed = (
        P("dp", None),
        P("dp", None),
        P("dp"),
        P("dp"),
        P("dp", None),
        P(None, None, "mp"),
        P(None, "mp"),
        P("mp", None),
        P(None, "mp"),
        P(None, None, "mp"),
        P(None, "mp"),
        P("mp", None),
        P(None, "mp"),
        P("mp"),
        P("mp", None),
        P(),
        P(),
        P(),
    )
    return jax.shard_map(
        per_device,
        mesh=mesh,
        in_specs=placed,
        out_specs=(
            P("dp", None),
            P("dp", None),
            P(("dp", "mp"), None),
            P("dp", None, "mp"),
            P(None, "mp"),
            P("mp", "dp"),
            P("dp", "mp"),
            P("dp", None, "mp"),
            P(None, "mp"),
            P("mp", "dp"),
            P("dp", "mp"),
            P("mp"),
            P("mp", "dp"),
            P(),
            P(),
            P(),
        ),
        check_vma=False,
    )
```

profile of v0, /device:TPU:0, one launch (start us, length us, event | category | flops | bytes accessed | tf_op | source)
XLA Modules:
  0.0 960.0 jit_solution(5997729488443684576)
XLA Ops:
  14.7 2.4 fusion.74
  21.7 4.6 add_convert_fusion
  28.5 20.0 %all-reduce.13.cloned.1.call-done = f32[128,1024]{1,0:T(8,128)} async-done(((f32[128,1024]{1,0:T(8,128)}), f32[128,1024]{1,0:T(8,128)}) %all-reduce.13.cloned.1.call-update) | async-done | bytes 524304 | tf_op jit(solution)/shard_map/psum | solution.py:144
  60.2 28.7 %all-reduce.15.cloned.1.call-done = f32[128,1024]{1,0:T(8,128)} async-done(((f32[128,1024]{1,0:T(8,128)}), f32[128,1024]{1,0:T(8,128)}) %all-reduce.15.cloned.1.call-update) | async-done | bytes 524304 | tf_op jit(solution)/shard_map/psum | solution.py:144
  91.4 3.0 convolution_add_fusion
  97.2 28.5 %all-reduce.17.cloned.1.call-done = f32[128,1024]{1,0:T(8,128)} async-done(((f32[128,1024]{1,0:T(8,128)}), f32[128,1024]{1,0:T(8,128)}) %all-reduce.17.cloned.1.call-update) | async-done | bytes 524304 | tf_op jit(solution)/shard_map/psum | solution.py:144
  129.4 2.7 convert_reduce_fusion.2
  132.1 4.6 convert_reduce_fusion.1
  137.5 2.3 fusion.76
  140.6 28.0 %all-reduce.19.cloned.1.call-done = f32[128,1024]{1,0:T(8,128)} async-done(((f32[128,1024]{1,0:T(8,128)}), f32[128,1024]{1,0:T(8,128)}) %all-reduce.19.cloned.1.call-update) | async-done | bytes 524304 | tf_op jit(solution)/shard_map/psum | solution.py:147
  173.5 2.4 convolution_convert_fusion.3
  176.9 3.9 multiply_reduce_fusion
  186.6 4.1 fusion.16
  192.9 3.1 multiply_convert_fusion.1
  198.3 17.0 %all-reduce.21.cloned.1.call-done = f32[128,1024]{1,0:T(8,128)} async-done(((f32[128,1024]{1,0:T(8,128)}), f32[128,1024]{1,0:T(8,128)}) %all-reduce.21.cloned.1.call-update) | async-done | bytes 524304 | tf_op jit(solution)/shard_map/psum | solution.py:147
  220.2 2.4 convolution_convert_fusion.2
  236.0 2.9 convolution_bitcast_fusion.2
  239.2 6.6 convolution_bitcast_fusion.1
  245.8 7.3 copy.102
  253.1 3.7 convolution_bitcast_fusion
  256.8 9.5 copy.100
  273.2 5.7 bitcast_convert_fusion
  279.0 4.5 fusion.52
  284.8 4.6 fusion.55
  293.3 65.8 %all-reduce.3 = (f32[2,512]{1,0:T(2,128)}, f32[2,512]{1,0:T(2,128)}, f32[2048]{0:T(1024)}, f32[3,1024]{1,0:T(4,128)}, f32[3,1024]{1,0:T(4,128)}, /*index=5*/f32[3,1024]{1,0:T(4,128)}) all-reduce(f32[2,512]{1,0:T(2,128)S(1)} %pad_maximum_fusion.10, f32[2,512]{1,0:T(2,128)S(1)} %pad_maximum_fusion.11, ...), channel_id=1, replica_groups=mesh['dp'=16,'mp'=2] {'dp'}, use_global_device_ids=true, to_apply=%region_28.29 | all-reduce | flops 13312 | bytes 106496 | tf_op jit(solution)/shard_map/psum | solution.py:289
  361.1 144.5 %all-reduce.25.cloned.1.call-done = (f32[1024,3,512]{2,1,0:T(4,128)}, f32[1024,2,512]{2,1,0:T(2,128)}) async-done(((f32[1024,3,512]{2,1,0:T(4,128)}, f32[1024,2,512]{2,1,0:T(2,128)}), (f32[1024,3,512]{2,1,0:T(4,128)}, f32[1024,2,512]{2,1,0:T(2,128)})) %all-reduce.25.cloned.1.call-update) | async-done | bytes 10485776
  509.3 62.2 %reduce-scatter.13.cloned.1.call-done = f32[512,64]{0,1:T(8,128)} async-done(((f32[512,1024]{0,1:T(8,128)}), f32[512,64]{0,1:T(8,128)}) %reduce-scatter.13.cloned.1.call-update) | async-done | bytes 131088 | tf_op jit(solution)/shard_map/reduce_scatter | solution.py:284
  571.5 65.3 %reduce-scatter.11.cloned.1.call-done = f32[64,512]{1,0:T(8,128)} async-done(((f32[1024,512]{1,0:T(8,128)}), f32[64,512]{1,0:T(8,128)}) %reduce-scatter.11.cloned.1.call-update) | async-done | bytes 131088 | tf_op jit(solution)/shard_map/reduce_scatter | solution.py:282
  636.8 64.7 %reduce-scatter.9.cloned.1.call-done = f32[512,64]{0,1:T(8,128)} async-done(((f32[512,1024]{0,1:T(8,128)}), f32[512,64]{0,1:T(8,128)}) %reduce-scatter.9.cloned.1.call-update) | async-done | bytes 131088 | tf_op jit(solution)/shard_map/reduce_scatter | solution.py:281
  701.5 33.8 %reduce-scatter.7.cloned.1.call-done = bf16[512,1024]{1,0:T(8,128)(2,1)} async-done(((bf16[1024,1024]{1,0:T(8,128)(2,1)}), bf16[512,1024]{1,0:T(8,128)(2,1)}) %reduce-scatter.7.cloned.1.call-update) | async-done | bytes 1048592 | tf_op jit(solution)/shard_map/reduce_scatter | solution.py:232
  735.3 109.1 %reduce-scatter.17.cloned.1.call-done = f32[2048,64]{0,1:T(8,128)} async-done(((f32[2048,1024]{0,1:T(8,128)}), f32[2048,64]{0,1:T(8,128)}) %reduce-scatter.17.cloned.1.call-update) | async-done | bytes 524304 | tf_op jit(solution)/shard_map/reduce_scatter | solution.py:286
  844.5 109.0 %reduce-scatter.15.cloned.1.call-done = f32[64,2048]{1,0:T(8,128)} async-done(((f32[1024,2048]{1,0:T(8,128)}), f32[64,2048]{1,0:T(8,128)}) %reduce-scatter.15.cloned.1.call-update) | async-done | bytes 524304 | tf_op jit(solution)/shard_map/reduce_scatter | solution.py:285
  (286 shorter events, 85.9 us)
Async XLA Ops:
  7.2 41.3 %all-reduce.13.cloned.1.call-start = ((), (), s32[]{:S(2)}) async-start(), calls=%async_computation.6 | async-start | bytes 1048576 | tf_op jit(solution)/shard_map/psum | solution.py:144
  11.5 10.3 %copy-start.31 = (bf16[128,1,512]{0,2,1:T(8,128)(2,1)}, bf16[128,1,512]{0,2,1:T(8,128)(2,1)S(1)}, u32[]{:S(2)}) copy-start(bf16[128,1,512]{0,2,1:T(8,128)(2,1)S(1)} %copy.84) | copy-start | bytes 393220
  11.6 10.1 %copy-start.33 = (bf16[128,1,512]{0,2,1:T(8,128)(2,1)}, bf16[128,1,512]{0,2,1:T(8,128)(2,1)S(1)}, u32[]{:S(2)}) copy-start(bf16[128,1,512]{0,2,1:T(8,128)(2,1)S(1)} %copy.83) | copy-start | bytes 393220
  12.7 13.7 %copy-start.39 = (bf16[128,1,512]{0,2,1:T(8,128)(2,1)}, bf16[128,1,512]{0,2,1:T(8,128)(2,1)S(1)}, u32[]{:S(2)}) copy-start(bf16[128,1,512]{0,2,1:T(8,128)(2,1)S(1)} %copy.82) | copy-start | bytes 393220
  17.1 71.8 %all-reduce.15.cloned.1.call-start = ((), (), s32[]{:S(2)}) async-start(), calls=%async_computation.7 | async-start | bytes 1048576 | tf_op jit(solution)/shard_map/psum | solution.py:144
  26.4 22.1 %copy-start.25 = (bf16[128,1024]{1,0:T(8,128)(2,1)S(1)}, bf16[128,1024]{1,0:T(8,128)(2,1)}, u32[]{:S(2)}) copy-start(bf16[128,1024]{1,0:T(8,128)(2,1)} %param.18) | copy-start | bytes 786436
  27.0 61.9 %copy-start.45 = (f32[1,1024]{1,0:T(1,128)}, f32[1,1024]{1,0:T(1,128)S(1)}, u32[]{:S(2)}) copy-start(f32[1,1024]{1,0:T(1,128)S(1)} %get-tuple-element.108) | copy-start | bytes 12292
  27.0 21.5 %copy-start.74 = (f32[1,1024]{1,0:T(1,128)S(1)}, f32[1,1024]{1,0:T(1,128)}, u32[]{:S(2)}) copy-start(f32[1,1024]{1,0:T(1,128)} %get-tuple-element.111) | copy-start | bytes 12292
  27.0 23.5 %copy-start.83 = (f32[1,512]{1,0:T(1,128)S(1)}, f32[1,512]{1,0:T(1,128)}, u32[]{:S(2)}) copy-start(f32[1,512]{1,0:T(1,128)} %get-tuple-element.115) | copy-start | bytes 6148
  57.2 31.7 %copy-start.57 = (f32[128]{0:T(128)S(1)}, f32[128]{0:T(128)}, u32[]{:S(2)}) copy-start(f32[128]{0:T(128)} %copy-done.56) | copy-start | bytes 1540
  57.2 31.7 %copy-start.73 = (f32[1,1024]{1,0:T(1,128)S(1)}, f32[1,1024]{1,0:T(1,128)}, u32[]{:S(2)}) copy-start(f32[1,1024]{1,0:T(1,128)} %get-tuple-element.112) | copy-start | bytes 12292
  57.2 31.7 %copy-start.78 = (f32[128]{0:T(128)S(1)}, f32[128]{0:T(128)}, u32[]{:S(2)}) copy-start(f32[128]{0:T(128)} %copy-done.77) | copy-start | bytes 1540
  58.3 33.0 %copy-start.82 = (f32[2048]{0:T(1024)S(1)}, f32[2048]{0:T(1024)}, u32[]{:S(2)}) copy-start(f32[2048]{0:T(1024)} %param.31) | copy-start | bytes 24580
  60.1 65.6 %all-reduce.17.cloned.1.call-start = ((), (), s32[]{:S(2)}) async-start(), calls=%async_computation.8 | async-start | bytes 1048576 | tf_op jit(solution)/shard_map/psum | solution.py:144
  90.5 80.3 %copy-start.52 = (f32[128]{0:T(128)}, f32[128]{0:T(128)S(1)}, u32[]{:S(2)}) copy-start(f32[128]{0:T(128)S(1)} %broadcast_multiply_fusion.7) | copy-start | bytes 1540
  90.7 80.1 %copy-start.54 = (f32[128]{0:T(128)}, f32[128]{0:T(128)S(1)}, u32[]{:S(2)}) copy-start(f32[128]{0:T(128)S(1)} %add_rsqrt_fusion.1) | copy-start | bytes 1540
  95.3 30.4 %copy-start.72 = (f32[1,1024]{1,0:T(1,128)S(1)}, f32[1,1024]{1,0:T(1,128)}, u32[]{:S(2)}) copy-start(f32[1,1024]{1,0:T(1,128)} %get-tuple-element.110) | copy-start | bytes 12292
  95.3 32.2 %copy-start.49 = (f32[1,1024]{1,0:T(1,128)S(1)}, f32[1,1024]{1,0:T(1,128)}, u32[]{:S(2)}) copy-start(f32[1,1024]{1,0:T(1,128)} %get-tuple-element.104) | copy-start | bytes 12292
  95.3 32.2 %copy-start.86 = (pred[128]{0:T(512)(128)(4,1)S(1)}, pred[128]{0:T(512)(128)(4,1)}, u32[]{:S(2)}) copy-start(pred[128]{0:T(512)(128)(4,1)} %copy-done.85) | copy-start | bytes 388
  95.3 34.1 %copy-start.71 = (f32[1,1024]{1,0:T(1,128)S(1)}, f32[1,1024]{1,0:T(1,128)}, u32[]{:S(2)}) copy-start(f32[1,1024]{1,0:T(1,128)} %get-tuple-element.107) | copy-start | bytes 12292
  97.0 71.6 %all-reduce.19.cloned.1.call-start = ((), (), s32[]{:S(2)}) async-start(), calls=%async_computation.9 | async-start | bytes 1048576 | tf_op jit(solution)/shard_map/psum | solution.py:147
  139.8 75.4 %all-reduce.21.cloned.1.call-start = ((), (), s32[]{:S(2)}) async-start(), calls=%async_computation.10 | async-start | bytes 1048576 | tf_op jit(solution)/shard_map/psum | solution.py:147
  186.5 172.6 %all-reduce.23.cloned.1.call-start = ((), (), s32[]{:S(2)}) async-start(), calls=%async_computation.11 | async-start | bytes 1048576 | tf_op jit(solution)/shard_map/psum | solution.py:147
  198.3 30.6 %copy-start.32 = (bf16[128,1,512]{0,2,1:T(8,128)(2,1)S(1)}, bf16[128,1,512]{0,2,1:T(8,128)(2,1)}, u32[]{:S(2)}) copy-start(bf16[128,1,512]{0,2,1:T(8,128)(2,1)} %copy-done.31) | copy-start | bytes 393220
  238.9 266.7 %all-reduce.25.cloned.1.call-start = ((), (), s32[]{:S(2)}) async-start(), calls=%async_computation.18 | async-start | bytes 25165824
  266.4 305.1 %reduce-scatter.13.cloned.1.call-start = ((), (), s32[]{:S(2)}) async-start(), calls=%async_computation.15 | async-start | bytes 2228224 | tf_op jit(solution)/shard_map/reduce_scatter | solution.py:284
  269.2 367.6 %reduce-scatter.11.cloned.1.call-start = ((), (), s32[]{:S(2)}) async-start(), calls=%async_computation.14 | async-start | bytes 2228224 | tf_op jit(solution)/shard_map/reduce_scatter | solution.py:282
  271.2 430.3 %reduce-scatter.9.cloned.1.call-start = ((), (), s32[]{:S(2)}) async-start(), calls=%async_computation.13 | async-start | bytes 2228224 | tf_op jit(solution)/shard_map/reduce_scatter | solution.py:281
  273.1 462.2 %reduce-scatter.7.cloned.1.call-start = ((), (), s32[]{:S(2)}) async-start(), calls=%async_computation.12 | async-start | bytes 3145728 | tf_op jit(solution)/shard_map/reduce_scatter | solution.py:232
  278.9 565.5 %reduce-scatter.17.cloned.1.call-start = ((), (), s32[]{:S(2)}) async-start(), calls=%async_computation.17 | async-start | bytes 8912896 | tf_op jit(solution)/shard_map/reduce_scatter | solution.py:286
  283.6 669.9 %reduce-scatter.15.cloned.1.call-start = ((), (), s32[]{:S(2)}) async-start(), calls=%async_computation.16 | async-start | bytes 8912896 | tf_op jit(solution)/shard_map/reduce_scatter | solution.py:285
  289.5 664.0 %copy-start.1 = (bf16[1024,3,512]{2,0,1:T(8,128)(2,1)S(1)}, bf16[1024,3,512]{2,0,1:T(8,128)(2,1)}, u32[]{:S(2)}) copy-start(bf16[1024,3,512]{2,0,1:T(8,128)(2,1)} %param.23) | copy-start | bytes 9437188
  (69 other events, 203.0 us)
Sparse Core Ops, SparseCore 0:
  17.2 31.2 all-reduce.12
  60.2 28.5 all-reduce.14
  97.1 28.5 all-reduce.16
  140.0 28.5 all-reduce.18
  186.6 28.5 all-reduce.20
  239.0 28.5 all-reduce.22
  271.7 233.8 all-reduce.24
  509.9 61.5 reduce-scatter.12
  576.3 60.4 reduce-scatter.10
  641.0 60.5 reduce-scatter.8
  704.4 30.8 reduce-scatter.6
  739.8 104.6 reduce-scatter.16
  849.1 104.3 reduce-scatter.14
where the time goes:
time: 962 us; the launch traced here: 960 us
  waiting for transfers between devices  711 us (74%)
  matrix products  85.5 us (9%)
  blocking collectives  65.8 us (7%)
  local copies, waits for them, and re-layouts  53.4 us (6%)
  other arithmetic  26.1 us (3%)
  between operations  17.1 us (2%)
    unnamed x14, waiting for transfers between devices  145 us
    reduce_scatter x1, waiting for transfers between devices, per_device(): lax.psum_scatter(grad_fc_out, 'dp', scatter_dimension=1, tiled=True)  109 us
    reduce_scatter x1, waiting for transfers between devices, per_device(): lax.psum_scatter(grad_fc_in, 'dp', scatter_dimension=0, tiled=True)  109 us
    psum x3, waiting for transfers between devices, reduce_forward(): return lax.psum(partial_term(0, all_rows), 'mp')  77.2 us
    psum x1, blocking collectives, per_device(): lax.psum((grad_self_qv_bias, grad_cross_qv_bias, grad_fc_in_bias, bias_gr...  65.8 us
    reduce_scatter x1, waiting for transfers between devices, per_device(): lax.psum_scatter(grad_cross_q, 'dp', scatter_dimension=0, tiled=True)  65.3 us
    reduce_scatter x1, waiting for transfers between devices, per_device(): lax.psum_scatter(grad_self_out, 'dp', scatter_dimension=1, tiled=True)  64.7 us
    reduce_scatter x1, waiting for transfers between devices, per_device(): lax.psum_scatter(grad_cross_out, 'dp', scatter_dimension=1, tiled=True)  62.2 us
  transfers between devices with their start and end apart: 13, of which 12 were waited for; matrix products, arithmetic and copies ran while one was open for 8% of the time, Pallas kernels for 0%

commit v1 on v0

v1 whole, which is shorter than its diff:
```python
import functools
import types

import jax
import jax.numpy as jnp
from jax import lax
from jax.experimental import pallas as pl
from jax.experimental.pallas import tpu as pltpu
from jax.sharding import PartitionSpec as P

HEAD = 64
GROUP = 16
epsilon = 1e-05
MESH = pl.DeviceIdType.MESH
f32, bf16 = jnp.float32, jnp.bfloat16

FC_OUT, FC_IN, CROSS_OUT, CROSS_Q, SELF_OUT, QKV, KV = 0, 4, 8, 9, 10, 11, 14
UNITS = 16
X_TOKENS, X_FIRST, X_SECOND, X_FFN, X_CROSS, X_SELF = range(6)


def nn(a, b):
    return lax.dot_general(a, b, (((1,), (0,)), ((), ())), preferred_element_type=f32)


def nt(a, b):
    return lax.dot_general(a, b, (((1,), (1,)), ((), ())), preferred_element_type=f32)


def loop(count, body):
    def step(i, carry):
        body(i)
        return carry

    lax.fori_loop(0, count, step, 0)


def at(index, size):
    return pl.ds(pl.multiple_of(index * size, size), size)


def kernel(names, refs_at, *refs):
    r = types.SimpleNamespace(**dict(zip(names, refs)))
    T, D = r.tokens.shape
    ML = r.memory.shape[0]
    HL = r.self_out.shape[0]
    FL = r.fc_out.shape[0]
    W = 512
    PAIRS = HL // 128
    CH = 128
    scale = HEAD**-0.5

    d, m = lax.axis_index("dp"), lax.axis_index("mp")
    c, y = lax.rem(d, 2), lax.rem(d // 2, 2)
    zl, zh = lax.rem(d // 4, 2), lax.rem(d // 8, 2)
    to_mp = (d, 1 - m)
    to_c = (d + 1 - 2 * c, m)
    to_y = (d + 2 - 4 * y, m)
    to_z1 = (d + 4 - 8 * zl, m)
    to_z2 = (d + 8 - 16 * zh, m)

    barrier = pltpu.get_barrier_semaphore()
    for partner in (to_mp, to_c, to_y, to_z1, to_z2):
        pl.semaphore_signal(barrier, inc=1, device_id=partner, device_id_type=MESH)

    given = {}
    local_given = {}

    def slot(key, count=1):
        if key not in given:
            given[key] = sum(n for _, n in given.values()), count
        return given[key][0]

    def remote(key, index, count, src, dst, partner):
        base = slot(key, count) + index
        return pltpu.make_async_remote_copy(
            src_ref=src,
            dst_ref=dst,
            send_sem=r.send_sem.at[base],
            recv_sem=r.recv_sem.at[base],
            device_id=partner,
            device_id_type=MESH,
        )

    def local(key, src, dst, index=0, count=1):
        if key not in local_given:
            local_given[key] = sum(n for _, n in local_given.values()), count
        return pltpu.make_async_copy(src, dst, r.local_sem.at[local_given[key][0] + index])

    def load(src):
        name = next(k for k, v in vars(r).items() if v is src)
        return local(name, src, getattr(r, name + "_v"))

    for src in (r.tokens, r.wqkv, r.self_out, r.memory, r.wkv, r.cross_q, r.cross_out, r.fc_in, r.fc_out, r.cotangent):
        load(src).start()
    pl.semaphore_wait(barrier, 5)

    dec_len = r.dec_len[0]
    mem_len = r.mem_len[0]
    gain, shift, out_bias = r.norm_gain, r.norm_bias, r.out_bias
    sm = r.sm
    ycat, xcat, xsend = r.ycat, r.xcat, r.xsend
    low = r.low
    lane_low = lax.broadcasted_iota(jnp.int32, (T, 128), 1) < HEAD

    def stacked(pair):
        wide = pair.astype(f32)
        return jnp.concatenate(
            [jnp.where(lane_low, wide, 0.0).astype(bf16), jnp.where(lane_low, 0.0, wide).astype(bf16)], axis=0
        )

    def unstacked(wide):
        return jnp.concatenate([wide[:HEAD, :T], wide[HEAD:, T:]], axis=0).T

    def col_sum(x):
        return jnp.sum(x, axis=0, keepdims=True)

    def send_x(w, src):
        def block(q):
            row = lax.rem(q, 2) * 128 + (q // 2) * 64
            for own in (True, False):
                side = y if own else 1 - y
                t = src[:, at(q * 2 + side, 128)].astype(f32).T.astype(bf16)
                for half in range(2):
                    rows = pl.ds(pl.multiple_of(half * 256 + row, 64), 64)
                    piece = t[half * 64 : (half + 1) * 64]
                    if own:
                        xcat[w, rows, 0:128] = piece
                    else:
                        xsend[w, rows, :] = piece

        loop(4, block)
        copy_x(w).start()

    def copy_x(w):
        return remote(("x", w), 0, 1, xsend.at[w], xcat.at[w, :, pl.ds(128, 128)], to_y)

    def copy_y(u):
        return remote("yunit", u, KV, ycat.at[u, pl.ds(0, T), :], ycat.at[u, pl.ds(T, T), :], to_y)

    def exchange_copy(k, j):
        s = k % 2
        return remote(("ex", k), j, 4, r.ex_out.at[s, j], r.ex_in.at[s, j], to_mp)

    def exchange_start(k, term):
        def step(j):
            r.ex_out[k % 2, j] = term(j).astype(bf16)
            exchange_copy(k, j).start()

        loop(4, step)

    def exchange_wait(k):
        def step(j):
            exchange_copy(k, j).wait()

        loop(4, step)

    def exchanged(k, rows):
        s = k % 2
        return jnp.concatenate(
            [r.ex_out[s, j, rows, :].astype(f32) + r.ex_in[s, j, rows, :].astype(f32) for j in range(4)], axis=1
        )

    def kept(u):
        return r.fc_out_v.at[at(lax.rem(u, 8), 256), at(u // 8, W)]

    def core_out(u):
        return r.fc_in_v.at[at(lax.rem(u, 4), 256), at(u // 4, W)]

    def copy_core(u):
        return remote("core", u, KV, core_out(u), r.core_in.at[u], to_c)

    def stage_a(w, u0, count):
        def step(i):
            u = u0 + i
            if w >= 0:
                copy_y(u).wait_recv()
            out = core_out(u)
            keep = kept(u)
            for h in range(2):
                cols = pl.ds(h * 256, 256)
                rhs = ycat[u, :, cols]
                out[:, cols] = nn(xcat[w, at(1 - c, 256), :], rhs).astype(bf16)
                keep[:, cols] = nn(xcat[w, at(c, 256), :], rhs).astype(bf16)
            copy_core(u).start()

        copy_x_once(w)
        loop(count, step)

    x_waited = set()

    def copy_x_once(w):
        if w not in x_waited:
            x_waited.add(w)
            copy_x(w).wait_recv()

    def copy_z1(u):
        return remote("z1", u, UNITS, r.z1_out.at[u], r.z1_in.at[u], to_z1)

    def copy_z2(u):
        return remote("z2", u, UNITS, r.z2_out.at[u], r.z2_in.at[u], to_z2)

    def chunk_sum(u, rows):
        return kept(u)[rows, :].astype(f32) + r.core_in[u, rows, :].astype(f32)

    def kv_sum(v, rows):
        low_rows = pl.ds(pl.multiple_of(y * 256 + rows.start, 64), rows.size)
        return (
            r.memory_v[pl.ds(pl.multiple_of(y * 256 + rows.start, 64), rows.size), at(v, W)].astype(f32)
            + r.kvc_in[v, low_rows, :].astype(f32)
            + r.kvy_in[v, rows, :].astype(f32)
        )

    def stage_b(u0, count, total=chunk_sum, shift_u=0, before=None):
        def step(i):
            u = u0 + i
            if before is None:
                copy_core(u).wait_recv()
            else:
                before(i)
            r.z1_out[u] = total(u - shift_u, at(1 - zl, 128)).astype(bf16)
            copy_z1(u).start()

        loop(count, step)

    def stage_c(u0, count, total=chunk_sum, shift_u=0):
        def step(i):
            u = u0 + i
            copy_z1(u).wait_recv()
            rows = pl.ds(pl.multiple_of(zl * 128 + (1 - zh) * 64, 64), 64)
            got = r.z1_in[u, at(1 - zh, 64), :].astype(f32)
            r.z2_out[u] = (total(u - shift_u, rows) + got).astype(bf16)
            copy_z2(u).start()

        loop(count, step)

    def out_copy(u0, i):
        u = u0 + i
        fin = r.fin.at[u]
        if u0 == FC_OUT:
            return local(u0, fin, r.g_fc_out.at[:, at(i, W)], i, 4)
        if u0 == FC_IN:
            return local(u0, fin, r.g_fc_in.at[:, at(i, W)], i, 4)
        if u0 == QKV:
            return local(u0, fin, r.g_qkv.at[i], i, 3)
        if u0 == KV:
            return local(u0, fin, r.g_kv.at[i], i, 2)
        return local(u0, fin, {CROSS_OUT: r.g_cross_out, CROSS_Q: r.g_cross_q, SELF_OUT: r.g_self_out}[u0])

    def stage_d(u0, count, total=chunk_sum, shift_u=0):
        def step(i):
            u = u0 + i
            copy_z2(u).wait_recv()
            rows = pl.ds(pl.multiple_of(zl * 128 + zh * 64, 64), 64)
            got = r.z1_in[u, at(zh, 64), :].astype(f32) + r.z2_in[u].astype(f32)
            r.fin[u] = total(u - shift_u, rows) + got
            out_copy(u0, i).start()

        loop(count, step)

    load(r.tokens).wait()
    load(r.wqkv).wait()
    for part in range(3):

        def packed(j, part=part):
            cols = at(j, 256)
            x = nn(r.tokens_v[...], r.wqkv_v[part, :, cols])
            if part == 0:
                x = x + r.self_qv_bias[0:1, cols]
            if part == 2:
                x = x + r.self_qv_bias[1:2, cols]
            r.packed[part, :, cols] = x.astype(bf16)

        loop(HL // 256, packed)

    key_row = lax.broadcasted_iota(jnp.int32, (T, 2 * T), 0)
    query_row = lax.rem(lax.broadcasted_iota(jnp.int32, (T, 2 * T), 1), T)

    def self_pair(p):
        cols = at(p, 128)
        q, k, v = (r.packed[i, :, cols] for i in range(3))
        s = nt(k, stacked(q)) * scale
        s = jnp.where((key_row <= query_row) & (key_row < dec_len), s, -1e30)
        w = jnp.exp(s - jnp.max(s, axis=0, keepdims=True))
        probs = w / jnp.sum(w, axis=0, keepdims=True)
        r.self_probs[p] = probs
        mixed = nn(v.astype(f32).T.astype(bf16), probs.astype(bf16))
        ycat[SELF_OUT, 0:T, cols] = unstacked(mixed).astype(bf16)

    loop(PAIRS, self_pair)
    load(r.self_out).wait()
    exchange_start(0, lambda j: nn(ycat[SELF_OUT, 0:T, :], r.self_out_v[:, at(j, 256)]))
    copy_y(SELF_OUT).start()
    send_x(X_TOKENS, r.tokens_v)

    load(r.memory).wait()
    load(r.wkv).wait()
    key, value, turned = r.key, r.value, r.turned

    def pair_rows(i):
        rows = at(i, CH)
        x = r.memory_v[rows, :]
        for j in range(HL // 256):
            cols = pl.ds(j * 256, 256)
            key[rows, cols] = nn(x, r.wkv_v[0, :, cols]).astype(bf16)
            val = (nn(x, r.wkv_v[1, :, cols]) + r.cross_qv_bias[1:2, cols]).astype(bf16)
            value[rows, cols] = val

    loop(ML // CH, pair_rows)

    def turn(src):
        def step(i):
            rows = at(i, CH)
            for j in range(HL // 128):
                turned[pl.ds(j * 128, 128), rows] = src[rows, pl.ds(j * 128, 128)].astype(f32).T.astype(bf16)

        loop(ML // CH, step)

    turn(value)

    def normalize(v, k):
        mean = jnp.mean(v, axis=-1, keepdims=True)
        centred = v - mean
        inv = lax.rsqrt(jnp.mean(centred * centred, axis=-1, keepdims=True) + epsilon)
        unit = centred * inv
        return unit * gain[k : k + 1, :] + shift[k : k + 1, :], unit, inv

    def norm_back(g, unit, inv, k):
        w = g * gain[k : k + 1, :]
        return inv * (w - jnp.mean(w, axis=-1, keepdims=True) - unit * jnp.mean(w * unit, axis=-1, keepdims=True))

    exchange_wait(0)

    def first_rows(i):
        rows = at(i, 16)
        v = r.tokens_v[rows, :].astype(f32) + (exchanged(0, rows) + out_bias[0:1, :])
        norm, unit, inv = normalize(v, 0)
        r.norm[rows, :] = norm
        r.unit0[rows, :] = unit
        r.inv[0, rows, :] = jnp.broadcast_to(inv, (16, 128))
        low[rows, :] = norm.astype(bf16)

    loop(T // 16, first_rows)

    load(r.cross_q).wait()

    def cross_query(j):
        cols = at(j, 256)
        x = nn(low[...], r.cross_q_v[:, cols]) + r.cross_qv_bias[0:1, cols]
        r.query[:, cols] = x.astype(bf16)

    loop(HL // 256, cross_query)

    probs_ref = r.probs
    low_probs = r.low_probs
    mem_row = lax.broadcasted_iota(jnp.int32, (CH, 2 * T), 0)
    chunks = ML // CH

    def fold(x, op):
        total = x[0:8]
        for i in range(1, x.shape[0] // 8):
            total = op(total, x[8 * i : 8 * i + 8])
        return total

    def cross_pair(p):
        cols = at(p, 128)
        q = stacked(r.query[:, cols])

        def scores(i, top):
            rows = at(i, CH)
            s = nt(key[rows, cols], q) * scale
            s = jnp.where(mem_row + i * CH < mem_len, s, -1e30)
            probs_ref[p, rows, :] = s
            return jnp.maximum(top, fold(s, jnp.maximum))

        top = lax.fori_loop(0, chunks, scores, jnp.full((8, 2 * T), -1e30, f32))
        top = jnp.max(top, axis=0, keepdims=True)

        def weigh(i, total):
            rows = at(i, CH)
            w = jnp.exp(probs_ref[p, rows, :] - top)
            probs_ref[p, rows, :] = w
            return total + fold(w, jnp.add)

        total = lax.fori_loop(0, chunks, weigh, jnp.zeros((8, 2 * T), f32))
        part = 1.0 / jnp.sum(total, axis=0, keepdims=True)

        def share(i):
            rows = at(i, CH)
            w = probs_ref[p, rows, :] * part
            probs_ref[p, rows, :] = w
            low_probs[rows, :] = w.astype(bf16)

        loop(chunks, share)
        mixed = nn(turned[cols, :], low_probs[...])
        ycat[CROSS_OUT, 0:T, cols] = unstacked(mixed).astype(bf16)

    loop(PAIRS, cross_pair)
    load(r.cross_out).wait()
    exchange_start(1, lambda j: nn(ycat[CROSS_OUT, 0:T, :], r.cross_out_v[:, at(j, 256)]))
    copy_y(CROSS_OUT).start()
    send_x(X_FIRST, low)
    turn(key)

    def turn_memory(i):
        rows = at(i, CH)

        def block(b):
            t = r.memory_v[rows, at(b, 128)].astype(f32).T.astype(bf16)
            side, zlow, zhigh = lax.rem(b, 2), lax.rem(b // 2, 2), b // 4
            for half in range(2):
                to = half * 512 + side * 256 + zlow * 128 + zhigh * 64
                r.memory_t[pl.ds(pl.multiple_of(to, 64), 64), rows] = t[half * 64 : (half + 1) * 64]

        loop(D // 128, block)

    exchange_wait(1)

    def second_rows(i):
        rows = at(i, 16)
        v = r.norm[rows, :] + (exchanged(1, rows) + out_bias[1:2, :])
        norm, unit, inv = normalize(v, 1)
        r.norm[rows, :] = norm
        r.unit1[rows, :] = unit
        r.inv[1, rows, :] = jnp.broadcast_to(inv, (16, 128))
        low[rows, :] = norm.astype(bf16)

    loop(T // 16, second_rows)
    load(r.fc_in).wait()

    def ffn(j):
        cols = at(j, 256)
        h = nn(low[...], r.fc_in_v[:, cols]) + r.fc_in_bias[:, cols]
        phi = 0.5 * (1.0 + lax.erf(h * 0.7071067811865476))
        slope = phi + h * jnp.exp(-0.5 * h * h) * 0.3989422804014327
        r.slope[:, cols] = slope
        ycat[FC_OUT + j // 2, 0:T, at(lax.rem(j, 2), 256)] = (h * phi).astype(bf16)

    loop(FL // 256, ffn)
    load(r.fc_out).wait()

    def ffn_term(j):
        cols = at(j, 256)
        total = nn(ycat[FC_OUT, 0:T, :], r.fc_out_v[pl.ds(0, W), cols])
        for b in range(1, FL // W):
            total = total + nn(ycat[FC_OUT + b, 0:T, :], r.fc_out_v[pl.ds(b * W, W), cols])
        return total

    exchange_start(2, ffn_term)
    for b in range(4):
        copy_y(FC_OUT + b).start()
    send_x(X_SECOND, low)
    loop(ML // CH, turn_memory)
    load(r.cotangent).wait()
    exchange_wait(2)

    row16 = lax.broadcasted_iota(jnp.int32, (16, D), 0)
    zero8 = jnp.zeros((8, D), f32)

    def sums_of(body, k):
        def step(i, carry):
            g, unit, rounded = body(i)
            return (
                carry[0] + fold(rounded, jnp.add),
                carry[1] + fold(g * unit, jnp.add),
                carry[2] + fold(g, jnp.add),
            )

        bias, gains, shifts = lax.fori_loop(0, T // 16, step, (zero8, zero8, zero8))
        sm[0, k : k + 1, :] = col_sum(bias)
        sm[0, 3 + k : 4 + k, :] = col_sum(gains)
        sm[0, 6 + k : 7 + k, :] = col_sum(shifts)

    def output_rows(i):
        rows = at(i, 16)
        v = r.norm[rows, :] + (exchanged(2, rows) + out_bias[2:3, :])
        norm, unit, inv = normalize(v, 2)
        r.layer_v[rows, :] = norm.astype(bf16)
        g = jnp.where(row16 + i * 16 < dec_len, r.cotangent_v[rows, :].astype(f32), 0.0)
        grad = norm_back(g, unit, inv, 2)
        r.grad[rows, :] = grad
        rounded = grad.astype(bf16)
        low[rows, :] = rounded
        return g, unit, rounded.astype(f32)

    copy_x(X_SECOND).wait_send()
    sums_of(output_rows, 2)
    layer_copy = local("layer", r.layer_v, r.layer_out)
    layer_copy.start()
    send_x(X_FFN, low)

    def hidden_grad(j):
        cols = at(j, 256)
        g = nt(low[...], r.fc_out_v[at(j, 256), :]) * r.slope[:, cols]
        rounded = g.astype(bf16)
        ycat[FC_IN + j // 2, 0:T, at(lax.rem(j, 2), 256)] = rounded
        sm[0, pl.ds(11 + j // 4, 1), at(lax.rem(j, 4), 256)] = col_sum(rounded.astype(f32))

    loop(FL // 256, hidden_grad)

    def hidden_term(j):
        rows = at(j, 256)
        total = nt(ycat[FC_IN, 0:T, :], r.fc_in_v[rows, pl.ds(0, W)])
        for b in range(1, FL // W):
            total = total + nt(ycat[FC_IN + b, 0:T, :], r.fc_in_v[rows, pl.ds(b * W, W)])
        return total

    exchange_start(3, hidden_term)
    for b in range(4):
        copy_y(FC_IN + b).start()
    stage_a(X_FFN, FC_OUT, 4)
    stage_b(FC_OUT, 4)
    exchange_wait(3)

    def grad_rows(k, e, unit_ref):
        def body(i):
            rows = at(i, 16)
            g = r.grad[rows, :] + exchanged(e, rows)
            unit = unit_ref[rows, :]
            grad = norm_back(g, unit, r.inv[k, rows, 0:1], k)
            r.grad[rows, :] = grad
            rounded = grad.astype(bf16)
            low[rows, :] = rounded
            return g, unit, rounded.astype(f32)

        sums_of(body, k)

    grad_rows(1, 3, r.unit1)
    send_x(X_CROSS, low)

    load_mixed = r.mixed_grad

    def cross_mixed_grad(j):
        load_mixed[:, at(j, 256)] = nt(low[...], r.cross_out_v[at(j, 256), :]).astype(bf16)

    loop(HL // 256, cross_mixed_grad)

    dp_ref = r.dp

    def cross_back(p):
        cols = at(p, 128)
        q = stacked(r.query[:, cols])
        g = stacked(load_mixed[:, cols])

        def first(i, total):
            rows = at(i, CH)
            probs = probs_ref[p, rows, :]
            dprobs = nt(value[rows, cols], g)
            dp_ref[rows, :] = dprobs
            value[rows, cols] = nn(probs.astype(bf16), g).astype(bf16)
            return total + fold(probs * dprobs, jnp.add)

        total = lax.fori_loop(0, chunks, first, jnp.zeros((8, 2 * T), f32))
        total = jnp.sum(total, axis=0, keepdims=True)

        def second(i):
            rows = at(i, CH)
            ds = (probs_ref[p, rows, :] * (dp_ref[rows, :] - total)).astype(bf16)
            low_probs[rows, :] = ds
            key[rows, cols] = (nn(ds, q) * scale).astype(bf16)

        loop(chunks, second)
        dq = nn(turned[cols, :], low_probs[...])
        ycat[CROSS_Q, 0:T, cols] = (unstacked(dq) * scale).astype(bf16)

    loop(PAIRS, cross_back)
    exchange_start(4, lambda j: nt(ycat[CROSS_Q, 0:T, :], r.cross_q_v[at(j, 256), :]))
    copy_y(CROSS_Q).start()
    sm[0, 10:11, 0:HL] = col_sum(ycat[CROSS_Q, 0:T, :].astype(f32))

    def memory_term(i):
        other = at((1 - m) * 4 + i, CH)
        own = at(m * 4 + i, CH)
        for j in range(D // 256):
            cols = pl.ds(j * 256, 256)
            for half, to in ((other, r.gm_out), (own, r.gm_own)):
                x = nt(key[half, :], r.wkv_v[0, cols, :]) + nt(value[half, :], r.wkv_v[1, cols, :])
                to[i, :, cols] = x.astype(bf16)
        gm_copy(i).start()

    def gm_copy(i):
        return remote("gm", i, 4, r.gm_out.at[i], r.gm_in.at[i], to_mp)

    def copy_kvc(v):
        return remote("kvc", v, 2, r.kvc_out.at[v], r.kvc_in.at[v], to_c)

    def copy_kvy(v):
        return remote("kvy", v, 2, r.kvy_out.at[v], r.kvy_in.at[v], to_y)

    def kv_stage_a(v):
        pair = key if v == 0 else value
        for h in range(2):
            cols = pl.ds(h * 256, 256)

            def step(b, cols=cols, h=h):
                r.kvc_out[v, at(b, 128), cols] = nn(r.memory_t[at((1 - c) * 4 + b, 128), :], pair[:, cols]).astype(bf16)
                r.memory_v[at(b, 128), pl.ds(v * W + h * 256, 256)] = nn(
                    r.memory_t[at(c * 4 + b, 128), :], pair[:, cols]
                ).astype(bf16)

            loop(4, step)
        copy_kvc(v).start()

    def kv_stage_y(v):
        copy_kvc(v).wait_recv()
        rows = at(1 - y, 256)
        r.kvy_out[v] = (r.memory_v[rows, pl.ds(v * W, W)].astype(f32) + r.kvc_in[v, rows, :].astype(f32)).astype(bf16)
        copy_kvy(v).start()

    stage_a(X_SECOND, FC_IN, 4)
    stage_a(X_CROSS, CROSS_OUT, 1)
    stage_b(FC_IN, 4)
    stage_b(CROSS_OUT, 1)
    stage_c(FC_OUT, 4)
    exchange_wait(4)
    copy_x(X_CROSS).wait_send()
    grad_rows(0, 4, r.unit0)
    send_x(X_SELF, low)

    def self_mixed_grad(j):
        load_mixed[:, at(j, 256)] = nt(low[...], r.self_out_v[at(j, 256), :]).astype(bf16)

    loop(HL // 256, self_mixed_grad)

    def self_back(p):
        cols = at(p, 128)
        q, k, v = (r.packed[i, :, cols] for i in range(3))
        probs = r.self_probs[p]
        g = stacked(load_mixed[:, cols])
        dprobs = nt(v, g)
        ycat[QKV + 2, 0:T, cols] = nn(probs.astype(bf16), g).astype(bf16)
        ds = (probs * (dprobs - jnp.sum(probs * dprobs, axis=0, keepdims=True))).astype(bf16)
        ycat[QKV + 1, 0:T, cols] = (nn(ds, stacked(q)) * scale).astype(bf16)
        dq = nn(k.astype(f32).T.astype(bf16), ds)
        ycat[QKV, 0:T, cols] = (unstacked(dq) * scale).astype(bf16)

    loop(PAIRS, self_back)

    def packed_term(j):
        rows = at(j, 256)
        total = nt(ycat[QKV, 0:T, :], r.wqkv_v[0, rows, :])
        for b in range(1, 3):
            total = total + nt(ycat[QKV + b, 0:T, :], r.wqkv_v[b, rows, :])
        return total

    for b in range(3):
        copy_y(QKV + b).start()
    exchange_start(5, packed_term)
    sm[0, 9:10, 0:HL] = col_sum(ycat[QKV, 0:T, :].astype(f32))
    sm[0, 9:10, HL : 2 * HL] = col_sum(ycat[QKV + 2, 0:T, :].astype(f32))
    sm[0, 10:11, HL : 2 * HL] = col_sum(value[...].astype(f32))
    sm[0, 13:16, :] = jnp.zeros((3, D), f32)

    partners = (to_c, to_y, to_z1, to_z2)

    def small_copy(k):
        return remote(("small", k), 0, 1, sm.at[k], r.sm_in.at[k], partners[k])

    def small_step(k):
        small_copy(k).wait_recv()
        sm[k + 1] = sm[k] + r.sm_in[k]

    small_copy(0).start()
    stage_a(X_FIRST, CROSS_Q, 1)
    stage_a(X_SELF, SELF_OUT, 1)
    kv_stage_a(0)
    small_step(0)
    small_copy(1).start()
    kv_stage_a(1)
    stage_b(CROSS_Q, 2)
    kv_stage_y(0)
    kv_stage_y(1)
    stage_a(X_TOKENS, QKV, 3)
    small_step(1)
    small_copy(2).start()
    loop(4, memory_term)
    stage_b(QKV, 3)
    stage_b(KV, 2, kv_sum, KV, lambda i: copy_kvy(i).wait_recv())
    small_step(2)
    small_copy(3).start()
    exchange_wait(5)

    def token_rows(i):
        rows = at(i, 16)
        r.tokens_g[rows, :] = (r.grad[rows, :] + exchanged(5, rows)).astype(bf16)

    loop(T // 16, token_rows)
    token_copy = local("tokens_g", r.tokens_g, r.grad_tokens)
    token_copy.start()
    stage_d(FC_OUT, 4)
    stage_c(FC_IN, 4)
    stage_c(CROSS_OUT, 3)
    stage_c(QKV, 3)
    stage_c(KV, 2, kv_sum, KV)

    def memory_sum(i):
        gm_copy(i).wait()
        r.gm_own[i] = (r.gm_own[i].astype(f32) + r.gm_in[i].astype(f32)).astype(bf16)
        gm_store(i).start()

    def gm_store(i):
        return local("gm_store", r.gm_own.at[i], r.grad_memory.at[at(i, CH), :], i, 4)

    loop(4, memory_sum)
    stage_d(FC_IN, 4)
    stage_d(CROSS_OUT, 1)
    stage_d(CROSS_Q, 1)
    stage_d(SELF_OUT, 1)
    stage_d(QKV, 3)
    stage_d(KV, 2, kv_sum, KV)
    small_step(3)
    sm_copy = local("sm", sm.at[4], r.sums)
    sm_copy.start()

    for w in (X_TOKENS, X_FIRST, X_FFN, X_SELF):
        copy_x(w).wait_send()
    loop(KV, lambda u: copy_y(u).wait_send())
    loop(KV, lambda u: copy_core(u).wait_send())
    loop(2, lambda v: copy_kvc(v).wait_send())
    loop(2, lambda v: copy_kvy(v).wait_send())
    loop(UNITS, lambda u: copy_z1(u).wait_send())
    loop(UNITS, lambda u: copy_z2(u).wait_send())
    for k in range(4):
        small_copy(k).wait_send()
    for u0, count in ((FC_OUT, 4), (FC_IN, 4), (CROSS_OUT, 1), (CROSS_Q, 1), (SELF_OUT, 1), (QKV, 3), (KV, 2)):
        loop(count, lambda i, u0=u0: out_copy(u0, i).wait())
    loop(4, lambda i: gm_store(i).wait())
    layer_copy.wait()
    token_copy.wait()
    sm_copy.wait()
    refs_at.update(remote=sum(n for _, n in given.values()), local=sum(n for _, n in local_given.values()))


REMOTE_SEMS = 140
LOCAL_SEMS = 40


def layer(tokens, memory, mem_len, dec_len, cotangent, wqkv, self_qv_bias, self_out, cross_q, wkv, cross_qv_bias, cross_out, fc_in, fc_in_bias, fc_out, out_bias, norm_gain, norm_bias):
    T, D = tokens.shape
    ML = memory.shape[0]
    HL = self_out.shape[0]
    FL = fc_out.shape[0]
    R = D // GROUP
    W = 512
    PAIRS = HL // 128
    anywhere = pl.BlockSpec(memory_space=pl.ANY)
    in_vmem = pl.BlockSpec(memory_space=pltpu.VMEM)
    in_smem = pl.BlockSpec(memory_space=pltpu.SMEM)
    big = dict(tokens=tokens, memory=memory, cotangent=cotangent, wqkv=wqkv, self_out=self_out, cross_q=cross_q, wkv=wkv,
               cross_out=cross_out, fc_in=fc_in, fc_out=fc_out)
    small = dict(self_qv_bias=self_qv_bias, cross_qv_bias=cross_qv_bias, fc_in_bias=fc_in_bias, out_bias=out_bias,
                 norm_gain=norm_gain, norm_bias=norm_bias)
    scalars = dict(mem_len=mem_len, dec_len=dec_len)
    outs = dict(
        layer_out=((T, D), bf16),
        grad_tokens=((T, D), bf16),
        grad_memory=((ML // 2, D), bf16),
        g_qkv=((3, R, HL), f32),
        g_self_out=((R, HL), f32),
        g_cross_q=((R, HL), f32),
        g_kv=((2, R, HL), f32),
        g_cross_out=((R, HL), f32),
        g_fc_in=((R, FL), f32),
        g_fc_out=((R, FL), f32),
        sums=((16, D), f32),
    )
    scratch = {name + "_v": (x.shape, x.dtype) for name, x in big.items()}
    scratch |= dict(
        packed=((3, T, HL), bf16),
        self_probs=((PAIRS, T, 2 * T), f32),
        low=((T, D), bf16),
        ycat=((KV, 2 * T, W), bf16),
        xcat=((6, 512, 256), bf16),
        xsend=((6, 512, 128), bf16),
        ex_out=((2, 4, T, 256), bf16),
        ex_in=((2, 4, T, 256), bf16),
        norm=((T, D), f32),
        unit0=((T, D), f32),
        unit1=((T, D), f32),
        inv=((2, T, 128), f32),
        grad=((T, D), f32),
        key=((ML, HL), bf16),
        value=((ML, HL), bf16),
        turned=((HL, ML), bf16),
        query=((T, HL), bf16),
        mixed_grad=((T, HL), bf16),
        probs=((PAIRS, ML, 2 * T), f32),
        low_probs=((ML, 2 * T), bf16),
        dp=((ML, 2 * T), f32),
        slope=((T, FL), f32),
        memory_t=((D, ML), bf16),
        layer_v=((T, D), bf16),
        tokens_g=((T, D), bf16),
        gm_out=((4, 128, D), bf16),
        gm_own=((4, 128, D), bf16),
        gm_in=((4, 128, D), bf16),
        core_in=((KV, 256, W), bf16),
        kvc_out=((2, 512, W), bf16),
        kvc_in=((2, 512, W), bf16),
        kvy_out=((2, 256, W), bf16),
        kvy_in=((2, 256, W), bf16),
        z1_out=((UNITS, 128, W), bf16),
        z1_in=((UNITS, 128, W), bf16),
        z2_out=((UNITS, 64, W), bf16),
        z2_in=((UNITS, 64, W), bf16),
        fin=((UNITS, 64, W), f32),
        sm=((5, 16, D), f32),
        sm_in=((4, 16, D), f32),
    )
    sems = dict(send_sem=REMOTE_SEMS, recv_sem=REMOTE_SEMS, local_sem=LOCAL_SEMS)
    names = [*big, *small, *scalars, *outs, *scratch, *sems]
    got = {}
    out = pl.pallas_call(
        functools.partial(kernel, names, got),
        out_shape=[jax.ShapeDtypeStruct(s, t) for s, t in outs.values()],
        in_specs=[anywhere] * len(big) + [in_vmem] * len(small) + [in_smem] * len(scalars),
        out_specs=[anywhere] * len(outs),
        scratch_shapes=[pltpu.VMEM(s, t) for s, t in scratch.values()]
        + [pltpu.SemaphoreType.DMA((count,)) for count in sems.values()],
        compiler_params=pltpu.CompilerParams(
            collective_id=0, has_side_effects=True, vmem_limit_bytes=63 * 2**20
        ),
        name="layer",
    )(*big.values(), *small.values(), *scalars.values())
    assert got["remote"] <= REMOTE_SEMS and got["local"] <= LOCAL_SEMS, got
    return types.SimpleNamespace(**dict(zip(outs, out)))


def per_device(tokens, memory, mem_len, dec_len, cotangent, self_qkv, self_qv_bias, self_out, cross_q, cross_kv, cross_qv_bias, cross_out, fc_in, fc_in_bias, fc_out, out_bias, norm_gain, norm_bias):
    D = tokens.shape[1]
    HL = self_out.shape[0]
    devices = lax.axis_size("dp")
    outer = devices // GROUP

    def regroup(x, axis, there):
        if outer == 1:
            return x
        sizes = (outer, GROUP) if there else (GROUP, outer)
        shape = x.shape
        x = x.reshape(shape[:axis] + sizes + (D // devices,) + shape[axis + 1 :])
        return jnp.swapaxes(x, axis, axis + 1).reshape(shape)

    tokens, memory, cotangent, self_out, cross_out, fc_out, out_bias, norm_gain, norm_bias = (
        regroup(x, 1, True)
        for x in (tokens, memory, cotangent, self_out, cross_out, fc_out, out_bias, norm_gain, norm_bias)
    )
    self_qkv, cross_q, cross_kv, fc_in = (regroup(x, 0, True) for x in (self_qkv, cross_q, cross_kv, fc_in))
    got = layer(
        tokens, memory, mem_len, dec_len, cotangent, self_qkv.transpose(1, 0, 2), self_qv_bias, self_out, cross_q,
        cross_kv.transpose(1, 0, 2), cross_qv_bias, cross_out, fc_in, fc_in_bias.reshape(1, -1), fc_out, out_bias,
        norm_gain, norm_bias,
    )
    groups = [[o * GROUP + i for o in range(outer)] for i in range(GROUP)]

    def spread(x, axis):
        if outer == 1:
            return x
        return lax.psum_scatter(x, "dp", scatter_dimension=axis, axis_index_groups=groups, tiled=True)

    sums = got.sums
    if outer > 1:
        sums = lax.psum(sums, "dp", axis_index_groups=groups)
    layer_out, grad_tokens, grad_memory = (
        regroup(x, 1, False) for x in (got.layer_out, got.grad_tokens, got.grad_memory)
    )
    return (
        layer_out,
        grad_tokens,
        grad_memory,
        spread(got.g_qkv, 1).transpose(1, 0, 2),
        sums[9].reshape(2, HL),
        spread(got.g_self_out, 0).T,
        spread(got.g_cross_q, 0),
        spread(got.g_kv, 1).transpose(1, 0, 2),
        sums[10].reshape(2, HL),
        spread(got.g_cross_out, 0).T,
        spread(got.g_fc_in, 0),
        sums[11:13].reshape(-1),
        spread(got.g_fc_out, 0).T,
        regroup(sums[0:3], 1, False),
        regroup(sums[3:6], 1, False),
        regroup(sums[6:9], 1, False),
    )


def solution(mesh):
    placed = (
        P("dp", None),
        P("dp", None),
        P("dp"),
        P("dp"),
        P("dp", None),
        P(None, None, "mp"),
        P(None, "mp"),
        P("mp", None),
        P(None, "mp"),
        P(None, None, "mp"),
        P(None, "mp"),
        P("mp", None),
        P(None, "mp"),
        P("mp"),
        P("mp", None),
        P(),
        P(),
        P(),
    )
    return jax.shard_map(
        per_device,
        mesh=mesh,
        in_specs=placed,
        out_specs=(
            P("dp", None),
            P("dp", None),
            P(("dp", "mp"), None),
            P("dp", None, "mp"),
            P(None, "mp"),
            P("mp", "dp"),
            P("dp", "mp"),
            P("dp", None, "mp"),
            P(None, "mp"),
            P("mp", "dp"),
            P("dp", "mp"),
            P("mp"),
            P("mp", "dp"),
            P(),
            P(),
            P(),
        ),
        check_vma=False,
    )
```

time: 962 us -> 177 us (0.18)
  waiting for transfers between devices: 711 us -> 0 us
  Pallas kernels: 0 us -> 154 us
  matrix products: 85.5 us -> 0 us
  blocking collectives: 65.8 us -> 0 us
  local copies, waits for them, and re-layouts: 53.4 us -> 20.2 us
  other arithmetic: 26.1 us -> 0 us
  between operations: 17.1 us -> 2 us
    reduce_scatter x6 -> x0, waiting for transfers between devices: 444 us -> none  [the longest x1 109 us: per_device(): lax.psum_scatter(grad_fc_out, 'dp', scatter_dimension=1, tiled=True)]
    pallas_call x0 -> x1, Pallas kernels: none -> 154 us  [layer(): pl.pallas_call(functools.partial(kernel, names, got), out_shape=[jax.Shap...]
    unnamed x14 -> x0, waiting for transfers between devices: 145 us -> none
    psum x6 -> x0, waiting for transfers between devices: 122 us -> none  [the longest x3 77.2 us: reduce_forward(): return lax.psum(partial_term(0, all_rows), 'mp')]
    dot_general x33 -> x0, matrix products: 85.5 us -> none  [the longest x7 24.9 us: contract_rows(): lax.dot_general(operand, other, (((0,), (0,)), ((), ())), preferred_eleme...]
    psum x1 -> x0, blocking collectives: 65.8 us -> none  [per_device(): lax.psum((grad_self_qv_bias, grad_cross_qv_bias, grad_fc_in_bias, bias_gr...]
    reduce_sum x17 -> x0, other arithmetic: 20.6 us -> none  [the longest x3 6.37 us: normalize_back(): jnp.sum(upstream * unit_rows, axis=0)]
    dot_general x2 -> x0, local copies, waits for them, and re-layouts: 16.8 us -> none  [contract_rows(): lax.dot_general(operand, other, (((0,), (0,)), ((), ())), preferred_eleme...]
  transfers between devices with their start and end apart: 13 -> 0, of which waited for: 12 -> 0; matrix products, arithmetic and copies ran while one was open for 8% -> 0% of each run, Pallas kernels for 0% -> 0%
where the time goes in v1:
time: 177 us; the launch traced here: 176 us
  Pallas kernels  154 us (87%)
  local copies, waits for them, and re-layouts  20.2 us (11%)
  between operations  2 us (1%)
    pallas_call x1, Pallas kernels, layer(): pl.pallas_call(functools.partial(kernel, names, got), out_shape=[jax.Shap...  154 us
    unnamed x25, local copies, waits for them, and re-layouts  16.6 us

profile of v1, /device:TPU:0, one launch (start us, length us, event | category | flops | bytes accessed | tf_op | source)
XLA Modules:
  0.0 176.0 jit_solution(4323394203867279351)
XLA Ops:
  1.9 3.3 %copy.39 = bf16[1024,2,512]{2,0,1:T(8,128)(2,1)} copy(bf16[1024,2,512]{2,1,0:T(2,128)(2,1)} %param.27) | data formatting | bytes 4194304 | tf_op args[9]
  5.2 153.9 %layer.1 = (bf16[128,1024]{1,0:T(8,128)(2,1)}, bf16[128,1024]{1,0:T(8,128)(2,1)}, bf16[512,1024]{1,0:T(8,128)(2,1)}, f32[3,64,512]{2,1,0:T(8,128)}, f32[64,512]{...) custom-call(bf16[128,1024]{1,0:T(8,128)(2,1)} %refs_0_.1, ...), custom_call_target="tpu_custom_call" | custom-call | tf_op jit(solution)/shard_map/layer/pallas_call | solution.py:813
  159.1 0.0 copy-start.2
  159.1 0.0 copy-start.5
  159.1 0.0 copy-start.4
  159.1 0.0 copy-start.3
  159.1 0.0 copy-start.1
  159.1 0.9 slice_bitcast_fusion
  160.0 0.6 copy.40
  160.6 0.9 slice_reduce_fusion
  161.4 1.5 fusion
  163.0 0.6 reshape_squeeze.7
  163.6 0.6 reshape_squeeze.6
  164.2 0.0 copy-start
  164.2 1.9 %copy.35 = f32[64,2,512]{2,1,0:T(2,128)} copy(f32[64,2,512]{2,0,1:T(8,128)} %bitcast.19) | data formatting | bytes 524288
  166.1 1.7 copy.52
  167.8 1.7 copy.53
  169.4 2.3 %copy.54 = bf16[512,1024]{1,0:T(8,128)(2,1)} copy(bf16[512,1024]{1,0:T(8,128)(2,1)} %get-tuple-element.77) | data formatting | bytes 2097152
  171.7 0.0 copy-done.2
  171.7 0.7 copy.55
  172.5 0.0 copy-done.5
  172.5 0.7 copy.56
  173.1 0.0 copy-done.4
  173.1 0.7 copy.57
  173.8 0.0 copy-done.3
  173.8 0.7 copy.58
  174.4 0.0 copy-done.1
  174.4 0.8 copy.59
  175.2 0.0 copy-done
  175.2 0.8 copy.60
Async XLA Ops:
  159.1 12.6 %copy-start.2 = (f32[3,64,512]{2,1,0:T(8,128)S(1)}, f32[3,64,512]{2,1,0:T(8,128)}, u32[]{:S(2)}) copy-start(f32[3,64,512]{2,1,0:T(8,128)} %get-tuple-element.30) | copy-start | bytes 1179652
  159.1 13.4 %copy-start.5 = (f32[64,512]{1,0:T(8,128)S(1)}, f32[64,512]{1,0:T(8,128)}, u32[]{:S(2)}) copy-start(f32[64,512]{1,0:T(8,128)} %get-tuple-element.32) | copy-start | bytes 393220
  159.1 14.0 %copy-start.4 = (f32[64,512]{1,0:T(8,128)S(1)}, f32[64,512]{1,0:T(8,128)}, u32[]{:S(2)}) copy-start(f32[64,512]{1,0:T(8,128)} %get-tuple-element.81) | copy-start | bytes 393220
  159.1 14.7 %copy-start.3 = (f32[64,512]{1,0:T(8,128)S(1)}, f32[64,512]{1,0:T(8,128)}, u32[]{:S(2)}) copy-start(f32[64,512]{1,0:T(8,128)} %get-tuple-element.35) | copy-start | bytes 393220
  159.1 15.3 %copy-start.1 = (f32[64,2048]{1,0:T(8,128)S(1)}, f32[64,2048]{1,0:T(8,128)}, u32[]{:S(2)}) copy-start(f32[64,2048]{1,0:T(8,128)} %get-tuple-element.85) | copy-start | bytes 1572868
  164.2 11.0 %copy-start = (f32[64,2048]{1,0:T(8,128)S(1)}, f32[64,2048]{1,0:T(8,128)}, u32[]{:S(2)}) copy-start(f32[64,2048]{1,0:T(8,128)} %get-tuple-element.37) | copy-start | bytes 1572868

commit v2 on v1

v2 whole, which is shorter than its diff:
```python
import functools
import types

import jax
import jax.numpy as jnp
from jax import lax
from jax.experimental import pallas as pl
from jax.experimental.pallas import tpu as pltpu
from jax.sharding import PartitionSpec as P

HEAD = 64
LOG2E = 1.4426950408889634
GROUP = 16
epsilon = 1e-05
MESH = pl.DeviceIdType.MESH
f32, bf16 = jnp.float32, jnp.bfloat16

FC_OUT, FC_IN, CROSS_OUT, CROSS_Q, SELF_OUT, QKV, KV = 0, 4, 8, 9, 10, 11, 14
UNITS = 16
X_TOKENS, X_FIRST, X_SECOND, X_FFN, X_CROSS, X_SELF = range(6)


AXIS_Y, AXIS_Z = 0, 1


def axis_of(unit):
    return AXIS_Z if unit < FC_IN or unit == CROSS_OUT else AXIS_Y


def x_axis(x):
    return AXIS_Z if x in (X_FFN, X_CROSS) else AXIS_Y


def x_of(unit):
    return ((X_FFN,) * 4 + (X_SECOND,) * 4 + (X_CROSS, X_FIRST, X_SELF) + (X_TOKENS,) * 3)[unit]


def nn(a, b):
    return lax.dot_general(a, b, (((1,), (0,)), ((), ())), preferred_element_type=f32)


def nt(a, b):
    return lax.dot_general(a, b, (((1,), (1,)), ((), ())), preferred_element_type=f32)


def loop(count, body, unroll=1):
    def step(i, carry):
        for j in range(unroll):
            body(i * unroll + j)
        return carry

    if unroll == count:
        step(0, 0)
    else:
        lax.fori_loop(0, count // unroll, step, 0)


def at(index, size):
    return pl.ds(index * size if isinstance(index, int) else pl.multiple_of(index * size, size), size)


def kernel(names, refs_at, *refs):
    r = types.SimpleNamespace(**dict(zip(names, refs)))
    T, D = r.tokens.shape
    ML = r.memory.shape[0]
    HL = r.self_out.shape[0]
    FL = r.fc_out.shape[0]
    W = 512
    PAIRS = HL // 128
    CH = 128
    scale = HEAD**-0.5

    d, m = lax.axis_index("dp"), lax.axis_index("mp")
    c, y = lax.rem(d, 2), lax.rem(d // 2, 2)
    zl, zh = lax.rem(d // 4, 2), lax.rem(d // 8, 2)
    to_mp = (d, 1 - m)
    to_c = (d + 1 - 2 * c, m)
    to_y = (d + 2 - 4 * y, m)
    to_z1 = (d + 4 - 8 * zl, m)
    to_z2 = (d + 8 - 16 * zh, m)

    bits, partners_of = (y, zl), (to_y, to_z1)

    barrier = pltpu.get_barrier_semaphore()
    for partner in (to_mp, to_c, to_y, to_z1, to_z2):
        pl.semaphore_signal(barrier, inc=1, device_id=partner, device_id_type=MESH)

    given = {}
    local_given = {}

    def slot(key, count=1):
        if key not in given:
            given[key] = sum(n for _, n in given.values()), count
        return given[key][0]

    def remote(key, index, count, src, dst, partner):
        base = slot(key, count) + index
        return pltpu.make_async_remote_copy(
            src_ref=src,
            dst_ref=dst,
            send_sem=r.send_sem.at[base],
            recv_sem=r.recv_sem.at[base],
            device_id=partner,
            device_id_type=MESH,
        )

    def local(key, src, dst, index=0, count=1):
        if key not in local_given:
            local_given[key] = sum(n for _, n in local_given.values()), count
        return pltpu.make_async_copy(src, dst, r.local_sem.at[local_given[key][0] + index])

    def load(src):
        name = next(k for k, v in vars(r).items() if v is src)
        return local(name, src, getattr(r, name + "_v"))

    def load_qkv(part):
        return local("qkv", r.wqkv.at[part], r.wqkv_v.at[part], part, 3)

    load(r.tokens).start()
    for part in range(3):
        load_qkv(part).start()
    for src in (r.self_out, r.memory, r.cross_kv, r.cross_q, r.cross_out, r.fc_in, r.fc_out, r.cotangent):
        load(src).start()

    dec_len = r.dec_len[0]
    mem_len = r.mem_len[0]
    gain, shift, out_bias = r.norm_gain, r.norm_bias, r.out_bias
    sm = r.sm
    ycat, xcat, xsend = r.ycat, r.xcat, r.xsend
    low = r.low
    lane_low = lax.broadcasted_iota(jnp.int32, (T, 128), 1) < HEAD

    def stacked(pair):
        wide = pair.astype(f32)
        return jnp.concatenate(
            [jnp.where(lane_low, wide, 0.0).astype(bf16), jnp.where(lane_low, 0.0, wide).astype(bf16)], axis=0
        )

    def unstacked(wide):
        return jnp.concatenate([wide[:HEAD, :T], wide[HEAD:, T:]], axis=0).T

    def col_sum(x):
        return jnp.sum(x, axis=0, keepdims=True)

    def send_x(w, src):
        g = x_axis(w)

        def block(q):
            high, o = q // 2, lax.rem(q, 2)
            row = o * 128 + high * 64
            for own in (True, False):
                side = bits[g] if own else 1 - bits[g]
                from_block = high * 4 + (o * 2 + side if g == AXIS_Y else side * 2 + o)
                t = src[:, at(from_block, 128)].astype(f32).T.astype(bf16)
                for half in range(2):
                    rows = pl.ds(pl.multiple_of(half * 256 + row, 64), 64)
                    piece = t[half * 64 : (half + 1) * 64]
                    if own:
                        xcat[w, rows, 0:128] = piece
                    else:
                        xsend[w, rows, :] = piece

        loop(4, block, 2)
        copy_x(w).start()

    def copy_x(w):
        return remote(("x", w), 0, 1, xsend.at[w], xcat.at[w, :, pl.ds(128, 128)], partners_of[x_axis(w)])

    def copy_y(u):
        to = partners_of[axis_of(u)]
        return remote("gather", u, KV, ycat.at[u, pl.ds(0, T), :], ycat.at[u, pl.ds(T, T), :], to)

    def exchange_copy(k, j):
        s = k % 2
        return remote(("ex", k), j, 4, r.ex_out.at[s, j], r.ex_in.at[s, j], to_mp)

    def exchange_start(k, term):
        def step(j):
            r.ex_out[k % 2, j] = term(j).astype(bf16)
            exchange_copy(k, j).start()

        loop(4, step, 4)

    def exchange_wait(k):
        def step(j):
            exchange_copy(k, j).wait()

        loop(4, step)

    def exchanged(k, rows):
        s = k % 2
        return jnp.concatenate(
            [r.ex_out[s, j, rows, :].astype(f32) + r.ex_in[s, j, rows, :].astype(f32) for j in range(4)], axis=1
        )

    def kept(u):
        return r.fc_out_v.at[at(u % 8, 256), at(u // 8, W)]

    def core_out(u):
        return r.fc_in_v.at[at(u % 4, 256), at(u // 4, W)]

    def copy_core(u):
        return remote("core", u, KV, core_out(u), r.core_in.at[u], to_c)

    def copy_half(u):
        return remote("half", u, UNITS, r.half_out.at[u], r.half_in.at[u], partners_of[1 - axis_of(u)])

    def copy_last(u):
        return remote("last", u, UNITS, r.last_out.at[u], r.last_in.at[u], to_z2)

    def kvc_copy(v):
        return remote("kvc", v, 2, r.kvc_out.at[v], r.kvc_in.at[v], to_c)

    def kvy_copy(v):
        return remote("kvy", v, 2, r.kvy_out.at[v], r.kvy_in.at[v], to_y)

    arrived = set()

    def product(u):
        w = x_of(u)
        if w not in arrived:
            arrived.add(w)
            copy_x(w).wait_recv()
        copy_y(u).wait_recv()
        for h in range(W // 256):
            cols = pl.ds(h * 256, 256)
            rhs = ycat[u, :, cols]
            core_out(u)[:, cols] = nn(xcat[w, at(1 - c, 256), :], rhs).astype(bf16)
            kept(u)[:, cols] = nn(xcat[w, at(c, 256), :], rhs).astype(bf16)
        copy_core(u).start()

    def local_sum(u, rows):
        if u < KV:
            return kept(u)[rows, :].astype(f32) + r.core_in[u, rows, :].astype(f32)
        v = u - KV
        wide = pl.ds(pl.multiple_of(y * 256 + rows.start, 64), rows.size)
        mine = r.memory_v[wide, pl.ds(v * W, W)].astype(f32) + r.kvc_in[v, wide, :].astype(f32)
        return mine + r.kvy_in[v, rows, :].astype(f32)

    def halve(u):
        if u < KV:
            copy_core(u).wait_recv()
        else:
            kvy_copy(u - KV).wait_recv()
        r.half_out[u] = local_sum(u, at(1 - bits[1 - axis_of(u)], 128)).astype(bf16)
        copy_half(u).start()

    def part_rows(u, high):
        return pl.ds(pl.multiple_of(bits[1 - axis_of(u)] * 128 + high * 64, 64), 64)

    def halve_last(u):
        copy_half(u).wait_recv()
        got = r.half_in[u, at(1 - zh, 64), :].astype(f32)
        r.last_out[u] = (local_sum(u, part_rows(u, 1 - zh)) + got).astype(bf16)
        copy_last(u).start()

    def out_copy(u):
        if u < FC_IN:
            to = r.g_fc_out.at[:, at(u, W)]
        elif u < CROSS_OUT:
            to = r.g_fc_in.at[:, at(u - FC_IN, W)]
        elif u < QKV:
            to = (r.g_cross_out, r.g_cross_q, r.g_self_out)[u - CROSS_OUT]
        elif u < KV:
            to = r.g_qkv.at[u - QKV]
        else:
            to = r.g_kv.at[u - KV]
        return local("unit", r.fin.at[u], to, u, UNITS)

    def total(u):
        copy_last(u).wait_recv()
        got = r.half_in[u, at(zh, 64), :].astype(f32) + r.last_in[u].astype(f32)
        r.fin[u] = local_sum(u, part_rows(u, zh)) + got
        out_copy(u).start()

    def project():
        load(r.tokens).wait()
        for part in range(3):
            load_qkv(part).wait()

            def packed(j, part=part):
                cols = at(j, 256)
                x = nn(r.tokens_v[...], r.wqkv_v[part, :, cols])
                if part == 0:
                    x = x + r.self_qv_bias[0:1, cols]
                if part == 2:
                    x = x + r.self_qv_bias[1:2, cols]
                r.packed[part, :, cols] = x.astype(bf16)

            loop(HL // 256, packed, 2)

    key_row = lax.broadcasted_iota(jnp.int32, (T, 2 * T), 0)
    query_row = lax.rem(lax.broadcasted_iota(jnp.int32, (T, 2 * T), 1), T)

    def self_pair(p):
        cols = at(p, 128)
        q, k, v = (r.packed[i, :, cols] for i in range(3))
        s = nt(k, stacked(q)) * scale
        s = jnp.where((key_row <= query_row) & (key_row < dec_len), s, -1e30)
        w = jnp.exp(s - jnp.max(s, axis=0, keepdims=True))
        probs = w / jnp.sum(w, axis=0, keepdims=True)
        r.self_probs[p] = probs
        mixed = nn(v.astype(f32).T.astype(bf16), probs.astype(bf16))
        ycat[SELF_OUT, 0:T, cols] = unstacked(mixed).astype(bf16)

    def self_attention():
        loop(PAIRS, self_pair, 4)

    def send_first():
        load(r.self_out).wait()
        pl.semaphore_wait(barrier, 5)
        exchange_start(0, lambda j: nn(ycat[SELF_OUT, 0:T, :], r.self_out_v[:, at(j, 256)]))
        copy_y(SELF_OUT).start()

    key, value, turned = r.key, r.value, r.turned
    odd = lax.broadcasted_iota(jnp.int32, (256, 256), 0)
    odd = jnp.where(odd < 128, 2 * odd, 2 * odd - 255)
    select = (lax.broadcasted_iota(jnp.int32, (256, 256), 1) == odd).astype(f32).astype(bf16)

    def part_weights(i):
        rows = at(i, CH)
        x = nn(select, r.cross_kv_v[rows].reshape(2 * CH, HL)).astype(bf16)
        r.wkv_v[0, rows, :] = x[:CH]
        r.wkv_v[1, rows, :] = x[CH:]

    def pair_rows(i):
        rows = at(i, CH)
        x = r.memory_v[rows, :]
        for j in range(HL // 256):
            cols = pl.ds(j * 256, 256)
            key[rows, cols] = nn(x, r.wkv_v[0, :, cols]).astype(bf16)
            val = (nn(x, r.wkv_v[1, :, cols]) + r.cross_qv_bias[1:2, cols]).astype(bf16)
            value[rows, cols] = val

    def turn(src):
        def step(i):
            rows = at(i, CH)
            for j in range(HL // 128):
                turned[pl.ds(j * 128, 128), rows] = src[rows, pl.ds(j * 128, 128)].astype(f32).T.astype(bf16)

        loop(ML // CH, step, 2)

    def memory_pair():
        load(r.cross_kv).wait()
        loop(D // CH, part_weights, 2)
        load(r.memory).wait()
        loop(ML // CH, pair_rows, 2)
        turn(value)

    def turn_memory(i):
        rows = at(i, CH)

        def block(b):
            t = r.memory_v[rows, at(b, 128)].astype(f32).T.astype(bf16)
            side, zlow, zhigh = lax.rem(b, 2), lax.rem(b // 2, 2), b // 4
            for half in range(2):
                to = half * 512 + side * 256 + zlow * 128 + zhigh * 64
                r.memory_t[pl.ds(pl.multiple_of(to, 64), 64), rows] = t[half * 64 : (half + 1) * 64]

        loop(D // 128, block, 4)

    def normalize(v, k):
        mean = jnp.mean(v, axis=-1, keepdims=True)
        centred = v - mean
        inv = lax.rsqrt(jnp.mean(centred * centred, axis=-1, keepdims=True) + epsilon)
        unit = centred * inv
        return unit * gain[k : k + 1, :] + shift[k : k + 1, :], unit, inv

    def norm_back(g, unit, inv, k):
        w = g * gain[k : k + 1, :]
        return inv * (w - jnp.mean(w, axis=-1, keepdims=True) - unit * jnp.mean(w * unit, axis=-1, keepdims=True))

    def norm_rows(k, base, unit_ref):
        def body(i):
            rows = at(i, 16)
            v = base[rows, :].astype(f32) + (exchanged(k, rows) + out_bias[k : k + 1, :])
            norm, unit, inv = normalize(v, k)
            r.norm[rows, :] = norm
            unit_ref[rows, :] = unit
            r.inv[k, rows, :] = jnp.broadcast_to(inv, (16, 128))
            low[rows, :] = norm.astype(bf16)

        exchange_wait(k)
        loop(T // 16, body, T // 16)

    def first_norm():
        norm_rows(0, r.tokens_v, r.unit0)

    def cross_query(j):
        cols = at(j, 256)
        x = nn(low[...], r.cross_q_v[:, cols]) + r.cross_qv_bias[0:1, cols]
        r.query[:, cols] = x.astype(bf16)

    probs_ref = r.probs
    low_probs = r.low_probs
    mem_row = lax.broadcasted_iota(jnp.int32, (CH, 2 * T), 0)
    chunks = ML // CH

    def fold(x, op):
        total = x[0:8]
        for i in range(1, x.shape[0] // 8):
            total = op(total, x[8 * i : 8 * i + 8])
        return total

    def cross_pair(p):
        cols = at(p, 128)
        q = stacked(r.query[:, cols])
        top = jnp.full((8, 2 * T), -1e30, f32)
        for i in range(chunks):
            rows = at(i, CH)
            s = nt(key[rows, cols], q) * (scale * LOG2E)
            s = jnp.where(mem_row < mem_len - i * CH, s, -1e30)
            probs_ref[p, rows, :] = s
            top = jnp.maximum(top, fold(s, jnp.maximum))
        top = jnp.max(top, axis=0, keepdims=True)
        total = jnp.zeros((8, 2 * T), f32)
        for i in range(chunks):
            rows = at(i, CH)
            w = jnp.exp2(probs_ref[p, rows, :] - top)
            probs_ref[p, rows, :] = w
            low_probs[rows, :] = w.astype(bf16)
            total = total + fold(w, jnp.add)
        part = 1.0 / jnp.sum(total, axis=0, keepdims=True)
        r.part[p] = jnp.broadcast_to(part, (8, 2 * T))
        mixed = nn(turned[cols, :], low_probs[...]) * part
        ycat[CROSS_OUT, 0:T, cols] = unstacked(mixed).astype(bf16)

    def cross_attention():
        load(r.cross_q).wait()
        loop(HL // 256, cross_query, 2)
        loop(PAIRS, cross_pair)

    def send_second():
        load(r.cross_out).wait()
        exchange_start(1, lambda j: nn(ycat[CROSS_OUT, 0:T, :], r.cross_out_v[:, at(j, 256)]))
        copy_y(CROSS_OUT).start()

    def second_norm():
        norm_rows(1, r.norm, r.unit1)

    def ffn(j):
        cols = at(j, 256)
        h = nn(low[...], r.fc_in_v[:, cols]) + r.fc_in_bias[:, cols]
        phi = 0.5 * (1.0 + lax.erf(h * 0.7071067811865476))
        slope = phi + h * jnp.exp(-0.5 * h * h) * 0.3989422804014327
        r.slope[:, cols] = slope
        ycat[FC_OUT + j // 2, 0:T, at(lax.rem(j, 2), 256)] = (h * phi).astype(bf16)

    def hidden_units():
        load(r.fc_in).wait()
        for b in range(FL // W):
            ffn(2 * b)
            ffn(2 * b + 1)
            copy_y(FC_OUT + b).start()

    def ffn_term(j):
        cols = at(j, 256)
        total = nn(ycat[FC_OUT, 0:T, :], r.fc_out_v[pl.ds(0, W), cols])
        for b in range(1, FL // W):
            total = total + nn(ycat[FC_OUT + b, 0:T, :], r.fc_out_v[pl.ds(b * W, W), cols])
        return total

    def send_third():
        load(r.fc_out).wait()
        exchange_start(2, ffn_term)

    row16 = lax.broadcasted_iota(jnp.int32, (16, D), 0)
    zero8 = jnp.zeros((8, D), f32)

    def sums_of(body, k):
        def step(i, carry):
            g, unit, rounded = body(i)
            return (
                carry[0] + fold(rounded, jnp.add),
                carry[1] + fold(g * unit, jnp.add),
                carry[2] + fold(g, jnp.add),
            )

        carry = (zero8, zero8, zero8)
        for i in range(T // 16):
            carry = step(i, carry)
        bias, gains, shifts = carry
        sm[k : k + 1, :] = col_sum(bias)
        sm[3 + k : 4 + k, :] = col_sum(gains)
        sm[6 + k : 7 + k, :] = col_sum(shifts)

    def output_rows(i):
        rows = at(i, 16)
        v = r.norm[rows, :] + (exchanged(2, rows) + out_bias[2:3, :])
        norm, unit, inv = normalize(v, 2)
        r.layer_v[rows, :] = norm.astype(bf16)
        g = jnp.where(row16 + i * 16 < dec_len, r.cotangent_v[rows, :].astype(f32), 0.0)
        grad = norm_back(g, unit, inv, 2)
        r.grad[rows, :] = grad
        rounded = grad.astype(bf16)
        low[rows, :] = rounded
        return g, unit, rounded.astype(f32)

    def layer_copy():
        return local("layer", r.layer_v, r.layer_out)

    def output_norm():
        load(r.cotangent).wait()
        exchange_wait(2)
        sums_of(output_rows, 2)
        layer_copy().start()

    def hidden_grad(j):
        cols = at(j, 256)
        g = nt(low[...], r.fc_out_v[at(j, 256), :]) * r.slope[:, cols]
        rounded = g.astype(bf16)
        ycat[FC_IN + j // 2, 0:T, at(j % 2, 256)] = rounded
        sm[pl.ds(11 + j // 4, 1), at(j % 4, 256)] = col_sum(rounded.astype(f32))

    def hidden_grads():
        for b in range(FL // W):
            hidden_grad(2 * b)
            hidden_grad(2 * b + 1)
            copy_y(FC_IN + b).start()

    def hidden_term(j):
        rows = at(j, 256)
        total = nt(ycat[FC_IN, 0:T, :], r.fc_in_v[rows, pl.ds(0, W)])
        for b in range(1, FL // W):
            total = total + nt(ycat[FC_IN + b, 0:T, :], r.fc_in_v[rows, pl.ds(b * W, W)])
        return total

    def send_fourth():
        exchange_start(3, hidden_term)

    def grad_rows(k, e, unit_ref):
        def body(i):
            rows = at(i, 16)
            g = r.grad[rows, :] + exchanged(e, rows)
            unit = unit_ref[rows, :]
            grad = norm_back(g, unit, r.inv[k, rows, 0:1], k)
            r.grad[rows, :] = grad
            rounded = grad.astype(bf16)
            low[rows, :] = rounded
            return g, unit, rounded.astype(f32)

        exchange_wait(e)
        sums_of(body, k)

    mixed_grad = r.mixed_grad

    def second_back():
        grad_rows(1, 3, r.unit1)

    def mixed_from(weights):
        for j in range(HL // 256):
            mixed_grad[:, at(j, 256)] = nt(low[...], weights[at(j, 256), :]).astype(bf16)

    def cross_mixed_grad():
        mixed_from(r.cross_out_v)

    dp_ref = r.dp

    def cross_back(p):
        cols = at(p, 128)
        q = stacked(r.query[:, cols])
        g = stacked(mixed_grad[:, cols])
        part = r.part[p, 0:1, :]
        total = jnp.zeros((8, 2 * T), f32)
        for i in range(chunks):
            rows = at(i, CH)
            probs = probs_ref[p, rows, :] * part
            dprobs = nt(value[rows, cols], g)
            dp_ref[rows, :] = dprobs
            probs_ref[p, rows, :] = probs
            value[rows, cols] = nn(probs.astype(bf16), g).astype(bf16)
            total = total + fold(probs * dprobs, jnp.add)
        total = jnp.sum(total, axis=0, keepdims=True)
        for i in range(chunks):
            rows = at(i, CH)
            ds = (probs_ref[p, rows, :] * (dp_ref[rows, :] - total)).astype(bf16)
            low_probs[rows, :] = ds
            key[rows, cols] = (nn(ds, q) * scale).astype(bf16)
        dq = nn(turned[cols, :], low_probs[...])
        ycat[CROSS_Q, 0:T, cols] = (unstacked(dq) * scale).astype(bf16)

    def send_fifth():
        exchange_start(4, lambda j: nt(ycat[CROSS_Q, 0:T, :], r.cross_q_v[at(j, 256), :]))
        copy_y(CROSS_Q).start()
        sm[10:11, 0:HL] = col_sum(ycat[CROSS_Q, 0:T, :].astype(f32))
        sm[10:11, HL : 2 * HL] = col_sum(value[...].astype(f32))

    def gm_copy(i):
        return remote("gm", i, 4, r.gm_out.at[i], r.gm_in.at[i], to_mp)

    def memory_term(i):
        for half, to in (((1 - m) * 4 + i, r.gm_out), (m * 4 + i, r.gm_own)):
            rows = at(half, CH)
            for j in range(D // 256):
                cols = pl.ds(j * 256, 256)
                x = nt(key[rows, :], r.wkv_v[0, cols, :]) + nt(value[rows, :], r.wkv_v[1, cols, :])
                to[i, :, cols] = x.astype(bf16)
        gm_copy(i).start()

    def gm_store(i):
        return local("gm_store", r.gm_own.at[i], r.grad_memory.at[at(i, CH), :], i, 4)

    def memory_sum(i):
        gm_copy(i).wait()
        r.gm_own[i] = (r.gm_own[i].astype(f32) + r.gm_in[i].astype(f32)).astype(bf16)
        gm_store(i).start()

    def pair_product(v):
        pair = key if v == 0 else value
        for h in range(2):
            cols = pl.ds(h * 256, 256)

            def step(b, cols=cols, h=h):
                rows = at(b, 128)
                other, own = r.memory_t[at((1 - c) * 4 + b, 128), :], r.memory_t[at(c * 4 + b, 128), :]
                r.kvc_out[v, rows, cols] = nn(other, pair[:, cols]).astype(bf16)
                r.memory_v[rows, pl.ds(v * W + h * 256, 256)] = nn(own, pair[:, cols]).astype(bf16)

            loop(4, step)
        kvc_copy(v).start()

    def pair_halve(v):
        kvc_copy(v).wait_recv()
        rows = at(1 - y, 256)
        mine = r.memory_v[rows, pl.ds(v * W, W)].astype(f32)
        r.kvy_out[v] = (mine + r.kvc_in[v, rows, :].astype(f32)).astype(bf16)
        kvy_copy(v).start()

    def first_back():
        grad_rows(0, 4, r.unit0)

    def self_back(p):
        cols = at(p, 128)
        q, k, v = (r.packed[i, :, cols] for i in range(3))
        probs = r.self_probs[p]
        g = stacked(mixed_grad[:, cols])
        dprobs = nt(v, g)
        ycat[QKV + 2, 0:T, cols] = nn(probs.astype(bf16), g).astype(bf16)
        ds = (probs * (dprobs - jnp.sum(probs * dprobs, axis=0, keepdims=True))).astype(bf16)
        ycat[QKV + 1, 0:T, cols] = (nn(ds, stacked(q)) * scale).astype(bf16)
        dq = nn(k.astype(f32).T.astype(bf16), ds)
        ycat[QKV, 0:T, cols] = (unstacked(dq) * scale).astype(bf16)

    def self_grads():
        mixed_from(r.self_out_v)
        loop(PAIRS, self_back, 4)
        for b in range(3):
            copy_y(QKV + b).start()
        sm[9:10, 0:HL] = col_sum(ycat[QKV, 0:T, :].astype(f32))
        sm[9:10, HL : 2 * HL] = col_sum(ycat[QKV + 2, 0:T, :].astype(f32))
        sm[13:16, :] = jnp.zeros((3, D), f32)

    def packed_term(j):
        rows = at(j, 256)
        total = nt(ycat[QKV, 0:T, :], r.wqkv_v[0, rows, :])
        for b in range(1, 3):
            total = total + nt(ycat[QKV + b, 0:T, :], r.wqkv_v[b, rows, :])
        return total

    def send_sixth():
        exchange_start(5, packed_term)

    def token_copy():
        return local("tokens_g", r.tokens_g, r.grad_tokens)

    def token_grads():
        def body(i):
            rows = at(i, 16)
            r.tokens_g[rows, :] = (r.grad[rows, :] + exchanged(5, rows)).astype(bf16)

        exchange_wait(5)
        loop(T // 16, body, 2)
        token_copy().start()

    doubling = (to_c, to_y, to_z1, to_z2)

    def small_copy(k):
        return remote("small", k, 4, r.sm_out.at[k], r.sm_in.at[k], doubling[k])

    def sums_copy():
        return local("sums", sm, r.sums)

    def small_step(k):
        if k > 0:
            small_copy(k - 1).wait()
            sm[...] = r.sm_out[k - 1].astype(f32) + r.sm_in[k - 1].astype(f32)
        if k < 4:
            r.sm_out[k] = sm[...].astype(bf16)
            small_copy(k).start()
        else:
            sums_copy().start()

    def each(step, *indices):
        for i in indices:
            step(i)

    project()
    self_attention()
    send_first()
    memory_pair()
    send_x(X_TOKENS, r.tokens_v)
    each(turn_memory, 4, 3, 1)
    first_norm()
    cross_attention()
    send_second()
    send_x(X_FIRST, low)
    turn(key)
    each(turn_memory, 0, 6, 2, 5, 7)
    second_norm()
    send_x(X_SECOND, low)
    hidden_units()
    send_third()
    output_norm()
    send_x(X_FFN, low)
    hidden_grads()
    send_fourth()
    each(product, 4)
    each(halve, 4)
    each(product, 0, 3, 2, 1, 5)
    each(halve, 0)
    second_back()
    send_x(X_CROSS, low)
    cross_mixed_grad()
    each(halve, 3, 2, 1)
    each(cross_back, 0)
    each(halve_last, 4)
    each(product, 6)
    each(cross_back, 1, 2)
    each(halve, 6)
    each(product, 7)
    each(halve, 5)
    each(cross_back, 3)
    each(product, 8)
    send_fifth()
    each(halve_last, 0)
    each(halve, 7)
    each(memory_term, 0)
    each(halve, 8)
    each(memory_term, 3)
    each(halve_last, 3, 6)
    each(pair_product, 1)
    each(halve_last, 2)
    first_back()
    each(halve_last, 5)
    each(memory_term, 1)
    each(total, 4)
    send_x(X_SELF, low)
    self_grads()
    each(halve_last, 7, 1)
    send_sixth()
    each(memory_sum, 0)
    each(small_step, 0)
    each(product, 9)
    each(total, 3, 0)
    each(pair_product, 0)
    each(halve_last, 8)
    each(small_step, 1)
    each(total, 6)
    each(halve, 9)
    each(pair_halve, 1)
    each(memory_term, 2)
    each(memory_sum, 3)
    each(product, 10)
    each(pair_halve, 0)
    each(total, 2)
    each(halve, 10)
    each(product, 11)
    each(total, 5)
    each(memory_sum, 1)
    each(halve, 11)
    each(halve_last, 9)
    each(product, 12)
    each(total, 7)
    each(halve, 12)
    each(halve_last, 10)
    each(product, 13)
    each(small_step, 2)
    each(total, 1)
    token_grads()
    each(halve, 13)
    each(halve_last, 11)
    each(total, 8)
    each(halve_last, 12)
    each(memory_sum, 2)
    each(halve, 15)
    each(total, 9)
    each(small_step, 3)
    each(total, 10)
    each(halve_last, 13)
    each(halve, 14)
    each(total, 11)
    each(halve_last, 15)
    each(total, 12)
    each(small_step, 4)
    each(total, 13)
    each(halve_last, 14)
    each(total, 15, 14)
    for w in range(6):
        copy_x(w).wait_send()
    for u in range(UNITS):
        if u < KV:
            copy_y(u).wait_send()
            copy_core(u).wait_send()
        copy_half(u).wait_send()
        copy_last(u).wait_send()
        out_copy(u).wait()
    for v in range(2):
        kvc_copy(v).wait_send()
        kvy_copy(v).wait_send()
    for i in range(4):
        gm_store(i).wait()
    layer_copy().wait()
    token_copy().wait()
    sums_copy().wait()
    refs_at.update(remote=sum(n for _, n in given.values()), local=sum(n for _, n in local_given.values()))


REMOTE_SEMS = 144
LOCAL_SEMS = 40


def layer(tokens, memory, mem_len, dec_len, cotangent, wqkv, self_qv_bias, self_out, cross_q, cross_kv, cross_qv_bias, cross_out, fc_in, fc_in_bias, fc_out, out_bias, norm_gain, norm_bias):
    T, D = tokens.shape
    ML = memory.shape[0]
    HL = self_out.shape[0]
    FL = fc_out.shape[0]
    R = D // GROUP
    W = 512
    PAIRS = HL // 128
    anywhere = pl.BlockSpec(memory_space=pl.ANY)
    in_vmem = pl.BlockSpec(memory_space=pltpu.VMEM)
    in_smem = pl.BlockSpec(memory_space=pltpu.SMEM)
    big = dict(tokens=tokens, memory=memory, cotangent=cotangent, wqkv=wqkv, self_out=self_out, cross_q=cross_q, cross_kv=cross_kv,
               cross_out=cross_out, fc_in=fc_in, fc_out=fc_out)
    small = dict(self_qv_bias=self_qv_bias, cross_qv_bias=cross_qv_bias, fc_in_bias=fc_in_bias, out_bias=out_bias,
                 norm_gain=norm_gain, norm_bias=norm_bias)
    scalars = dict(mem_len=mem_len, dec_len=dec_len)
    outs = dict(
        layer_out=((T, D), bf16),
        grad_tokens=((T, D), bf16),
        grad_memory=((ML // 2, D), bf16),
        g_qkv=((3, R, HL), f32),
        g_self_out=((R, HL), f32),
        g_cross_q=((R, HL), f32),
        g_kv=((2, R, HL), f32),
        g_cross_out=((R, HL), f32),
        g_fc_in=((R, FL), f32),
        g_fc_out=((R, FL), f32),
        sums=((16, D), f32),
    )
    scratch = {name + "_v": (x.shape, x.dtype) for name, x in big.items()}
    scratch |= dict(
        wkv_v=((2, D, HL), bf16),
        packed=((3, T, HL), bf16),
        self_probs=((PAIRS, T, 2 * T), f32),
        low=((T, D), bf16),
        ycat=((KV, 2 * T, W), bf16),
        xcat=((6, 512, 256), bf16),
        xsend=((6, 512, 128), bf16),
        ex_out=((2, 4, T, 256), bf16),
        ex_in=((2, 4, T, 256), bf16),
        norm=((T, D), f32),
        unit0=((T, D), f32),
        unit1=((T, D), f32),
        inv=((2, T, 128), f32),
        grad=((T, D), f32),
        key=((ML, HL), bf16),
        value=((ML, HL), bf16),
        turned=((HL, ML), bf16),
        query=((T, HL), bf16),
        mixed_grad=((T, HL), bf16),
        probs=((PAIRS, ML, 2 * T), f32),
        part=((PAIRS, 8, 2 * T), f32),
        low_probs=((ML, 2 * T), bf16),
        dp=((ML, 2 * T), f32),
        slope=((T, FL), f32),
        memory_t=((D, ML), bf16),
        layer_v=((T, D), bf16),
        tokens_g=((T, D), bf16),
        gm_out=((4, 128, D), bf16),
        gm_own=((4, 128, D), bf16),
        gm_in=((4, 128, D), bf16),
        core_in=((KV, 256, W), bf16),
        kvc_out=((2, 512, W), bf16),
        kvc_in=((2, 512, W), bf16),
        kvy_out=((2, 256, W), bf16),
        kvy_in=((2, 256, W), bf16),
        half_out=((UNITS, 128, W), bf16),
        half_in=((UNITS, 128, W), bf16),
        last_out=((UNITS, 64, W), bf16),
        last_in=((UNITS, 64, W), bf16),
        fin=((UNITS, 64, W), f32),
        sm=((16, D), f32),
        sm_out=((4, 16, D), bf16),
        sm_in=((4, 16, D), bf16),
    )
    sems = dict(send_sem=REMOTE_SEMS, recv_sem=REMOTE_SEMS, local_sem=LOCAL_SEMS)
    names = [*big, *small, *scalars, *outs, *scratch, *sems]
    got = {}
    out = pl.pallas_call(
        functools.partial(kernel, names, got),
        out_shape=[jax.ShapeDtypeStruct(s, t) for s, t in outs.values()],
        in_specs=[anywhere] * len(big) + [in_vmem] * len(small) + [in_smem] * len(scalars),
        out_specs=[anywhere] * len(outs),
        scratch_shapes=[pltpu.VMEM(s, t) for s, t in scratch.values()]
        + [pltpu.SemaphoreType.DMA((count,)) for count in sems.values()],
        compiler_params=pltpu.CompilerParams(
            collective_id=0, has_side_effects=True, vmem_limit_bytes=63 * 2**20
        ),
        name="layer",
    )(*big.values(), *small.values(), *scalars.values())
    assert got["remote"] <= REMOTE_SEMS and got["local"] <= LOCAL_SEMS, got
    return types.SimpleNamespace(**dict(zip(outs, out)))


def finish_kernel(count, *refs):
    ins, outs, scratch = refs[: count + 2], refs[count + 2 : 2 * count + 9], refs[2 * count + 9 :]
    held, turned, in_sem, out_sem = scratch[: count + 1], *scratch[count + 1 :]
    loads = [pltpu.make_async_copy(a, b, in_sem.at[i]) for i, (a, b) in enumerate(zip(ins, held))]
    stores = [
        pltpu.make_async_copy(a, b, out_sem.at[i]) for i, (a, b) in enumerate(zip((*held[:count], turned), outs))
    ]
    for load in loads:
        load.start()
    sums = ins[count + 1]
    self_bias, cross_bias, hidden_bias, out_bias, gains, shifts = outs[count + 1 :]
    width = self_bias.shape[1]
    for row, to in ((9, self_bias), (10, cross_bias)):
        for part in range(2):
            to[part : part + 1, :] = sums[row : row + 1, part * width : (part + 1) * width]
    features = sums.shape[1]
    for part in range(hidden_bias.shape[1] // features):
        hidden_bias[:, part * features : (part + 1) * features] = sums[11 + part : 12 + part, :]
    for first, to in ((0, out_bias), (3, gains), (6, shifts)):
        to[...] = sums[first : first + 3, :]
    for i in range(count):
        loads[i].wait()
        stores[i].start()
    loads[count].wait()
    for part in range(2):
        turned[:, part, :] = held[count][part]
    stores[count].start()
    for store in stores:
        store.wait()


def finish(whole, kv, sums):
    R, HL = kv.shape[1:]
    D = sums.shape[1]
    anywhere = pl.BlockSpec(memory_space=pl.ANY)
    in_vmem = pl.BlockSpec(memory_space=pltpu.VMEM)
    small = [(2, HL), (2, HL), (1, 4 * HL), (3, D), (3, D), (3, D)]
    return pl.pallas_call(
        functools.partial(finish_kernel, len(whole)),
        out_shape=[jax.ShapeDtypeStruct(x.shape, x.dtype) for x in whole]
        + [jax.ShapeDtypeStruct((R, 2, HL), f32)]
        + [jax.ShapeDtypeStruct(shape, f32) for shape in small],
        in_specs=[anywhere] * (len(whole) + 1) + [in_vmem],
        out_specs=[anywhere] * (len(whole) + 1) + [in_vmem] * len(small),
        scratch_shapes=[pltpu.VMEM(x.shape, x.dtype) for x in (*whole, kv)]
        + [pltpu.VMEM((R, 2, HL), f32)]
        + [pltpu.SemaphoreType.DMA((len(whole) + 1,))] * 2,
        compiler_params=pltpu.CompilerParams(vmem_limit_bytes=63 * 2**20),
        name="finish",
    )(*whole, kv, sums)


def per_device(tokens, memory, mem_len, dec_len, cotangent, self_qkv, self_qv_bias, self_out, cross_q, cross_kv, cross_qv_bias, cross_out, fc_in, fc_in_bias, fc_out, out_bias, norm_gain, norm_bias):
    D = tokens.shape[1]
    devices = lax.axis_size("dp")
    outer = devices // GROUP

    def regroup(x, axis, there):
        if outer == 1:
            return x
        sizes = (outer, GROUP) if there else (GROUP, outer)
        shape = x.shape
        x = x.reshape(shape[:axis] + sizes + (D // devices,) + shape[axis + 1 :])
        return jnp.swapaxes(x, axis, axis + 1).reshape(shape)

    tokens, memory, cotangent, self_out, cross_out, fc_out, out_bias, norm_gain, norm_bias = (
        regroup(x, 1, True)
        for x in (tokens, memory, cotangent, self_out, cross_out, fc_out, out_bias, norm_gain, norm_bias)
    )
    self_qkv, cross_q, cross_kv, fc_in = (regroup(x, 0, True) for x in (self_qkv, cross_q, cross_kv, fc_in))
    got = layer(
        tokens, memory, mem_len, dec_len, cotangent, self_qkv.transpose(1, 0, 2), self_qv_bias, self_out, cross_q,
        cross_kv, cross_qv_bias, cross_out, fc_in, fc_in_bias.reshape(1, -1), fc_out, out_bias,
        norm_gain, norm_bias,
    )
    groups = [[o * GROUP + i for o in range(outer)] for i in range(GROUP)]

    def spread(x, axis):
        if outer == 1:
            return x
        return lax.psum_scatter(x, "dp", scatter_dimension=axis, axis_index_groups=groups, tiled=True)

    sums = got.sums
    if outer > 1:
        sums = lax.psum(sums, "dp", axis_index_groups=groups)
    (
        layer_out, grad_tokens, grad_memory, qkv, self_out, cross_q, cross_out, fc_in, fc_out, kv,
        self_bias, cross_bias, hidden_bias, out_bias, gains, shifts,
    ) = finish(
        (
            got.layer_out, got.grad_tokens, got.grad_memory, got.g_qkv, got.g_self_out, got.g_cross_q, got.g_cross_out,
            got.g_fc_in, got.g_fc_out,
        ),
        got.g_kv,
        sums,
    )
    return (
        regroup(layer_out, 1, False),
        regroup(grad_tokens, 1, False),
        regroup(grad_memory, 1, False),
        spread(qkv, 1).transpose(1, 0, 2),
        self_bias,
        spread(self_out, 0).T,
        spread(cross_q, 0),
        spread(kv, 0),
        cross_bias,
        spread(cross_out, 0).T,
        spread(fc_in, 0),
        hidden_bias.reshape(-1),
        spread(fc_out, 0).T,
        regroup(out_bias, 1, False),
        regroup(gains, 1, False),
        regroup(shifts, 1, False),
    )


def solution(mesh):
    placed = (
        P("dp", None),
        P("dp", None),
        P("dp"),
        P("dp"),
        P("dp", None),
        P(None, None, "mp"),
        P(None, "mp"),
        P("mp", None),
        P(None, "mp"),
        P(None, None, "mp"),
        P(None, "mp"),
        P("mp", None),
        P(None, "mp"),
        P("mp"),
        P("mp", None),
        P(),
        P(),
        P(),
    )
    return jax.shard_map(
        per_device,
        mesh=mesh,
        in_specs=placed,
        out_specs=(
            P("dp", None),
            P("dp", None),
            P(("dp", "mp"), None),
            P("dp", None, "mp"),
            P(None, "mp"),
            P("mp", "dp"),
            P("dp", "mp"),
            P("dp", None, "mp"),
            P(None, "mp"),
            P("mp", "dp"),
            P("dp", "mp"),
            P("mp"),
            P("mp", "dp"),
            P(),
            P(),
            P(),
        ),
        check_vma=False,
    )
```

time: 177 us -> 123 us (0.69)
  Pallas kernels: 154 us -> 120 us
  local copies, waits for them, and re-layouts: 20.2 us -> 0 us
    pallas_call x1, Pallas kernels: 154 us -> 115 us  [layer(): pl.pallas_call(functools.partial(kernel, names, got), out_shape=[jax.Shap...]
    unnamed x25 -> x0, local copies, waits for them, and re-layouts: 16.6 us -> none
    pallas_call x0 -> x1, Pallas kernels: none -> 4.7 us  [finish(): pl.pallas_call(functools.partial(finish_kernel, len(whole)), out_shape=[j...]
    slice x2 -> x0, local copies, waits for them, and re-layouts: 2.4 us -> none  [the longest x1 1.54 us: per_device(): sums[6:9]]
where the time goes in v2:
time: 123 us; the launch traced here: 122 us
  Pallas kernels  120 us (98%)
  between operations  2.13 us (2%)
    pallas_call x1, Pallas kernels, layer(): pl.pallas_call(functools.partial(kernel, names, got), out_shape=[jax.Shap...  115 us
    pallas_call x1, Pallas kernels, finish(): pl.pallas_call(functools.partial(finish_kernel, len(whole)), out_shape=[j...  4.7 us

profile of v2, /device:TPU:0, one launch (start us, length us, event | category | flops | bytes accessed | tf_op | source)
XLA Modules:
  0.0 122.3 jit_solution(915800315386389633)
XLA Ops:
  1.9 115.4 %layer.1 = (bf16[128,1024]{1,0:T(8,128)(2,1)}, bf16[128,1024]{1,0:T(8,128)(2,1)}, bf16[512,1024]{1,0:T(8,128)(2,1)}, f32[3,64,512]{2,1,0:T(8,128)}, f32[64,512]{...) custom-call(bf16[128,1024]{1,0:T(8,128)(2,1)} %refs_0_.1, ...), custom_call_target="tpu_custom_call" | custom-call | tf_op jit(solution)/shard_map/layer/pallas_call | solution.py:900
  117.4 4.7 %finish.1 = (bf16[128,1024]{1,0:T(8,128)(2,1)}, bf16[128,1024]{1,0:T(8,128)(2,1)}, bf16[512,1024]{1,0:T(8,128)(2,1)}, f32[3,64,512]{2,1,0:T(8,128)}, f32[64,512]...) custom-call(bf16[128,1024]{1,0:T(8,128)(2,1)} %get-tuple-element.43., ...), custom_call_target="tpu_custom_call" | custom-call | tf_op jit(solution)/shard_map/finish/pallas_call | solution.py:953

commit v3 on v2

--- a/solution.py
+++ b/solution.py
@@ -24,11 +24,11 @@
 
 
 def axis_of(unit):
-    return AXIS_Z if unit < FC_IN or unit == CROSS_OUT else AXIS_Y
+    return AXIS_Z if unit < FC_IN or unit in (CROSS_OUT, SELF_OUT) else AXIS_Y
 
 
 def x_axis(x):
-    return AXIS_Z if x in (X_FFN, X_CROSS) else AXIS_Y
+    return AXIS_Z if x in (X_FFN, X_CROSS, X_SELF) else AXIS_Y
 
 
 def x_of(unit):
@@ -116,15 +116,17 @@
     def load_qkv(part):
         return local("qkv", r.wqkv.at[part], r.wqkv_v.at[part], part, 3)
 
+    first = (r.dec_len, r.mem_len, r.self_qv_bias, r.cross_qv_bias, r.fc_in_bias, r.out_bias, r.norm_gain, r.norm_bias)
     load(r.tokens).start()
-    for part in range(3):
-        load_qkv(part).start()
+    load_qkv(0).start()
+    for src in first:
+        load(src).start()
+    load_qkv(1).start()
+    load_qkv(2).start()
     for src in (r.self_out, r.memory, r.cross_kv, r.cross_q, r.cross_out, r.fc_in, r.fc_out, r.cotangent):
         load(src).start()
 
-    dec_len = r.dec_len[0]
-    mem_len = r.mem_len[0]
-    gain, shift, out_bias = r.norm_gain, r.norm_bias, r.out_bias
+    gain, shift, out_bias = r.norm_gain_v, r.norm_bias_v, r.out_bias_v
     sm = r.sm
     ycat, xcat, xsend = r.ycat, r.xcat, r.xsend
     low = r.low
@@ -164,7 +166,18 @@
         copy_x(w).start()
 
     def copy_x(w):
-        return remote(("x", w), 0, 1, xsend.at[w], xcat.at[w, :, pl.ds(128, 128)], partners_of[x_axis(w)])
+        rows = pl.ds(0, 512) if x_axis(w) == AXIS_Y else at(m, 256)
+        return remote(
+            ("x", w), 0, 1, xsend.at[w, rows, :], xcat.at[w, rows, pl.ds(128, 128)], partners_of[x_axis(w)]
+        )
+
+    def copy_shared(w, side):
+        held = xcat.at[w, at(side, 256), pl.ds(128, 128)]
+        return remote(("shared", w), 0, 1, held, held, to_mp)
+
+    def share_x(w):
+        copy_x(w).wait_recv()
+        copy_shared(w, m).start()
 
     def copy_y(u):
         to = partners_of[axis_of(u)]
@@ -220,7 +233,7 @@
         w = x_of(u)
         if w not in arrived:
             arrived.add(w)
-            copy_x(w).wait_recv()
+            (copy_x(w) if x_axis(w) == AXIS_Y else copy_shared(w, 1 - m)).wait_recv()
         copy_y(u).wait_recv()
         for h in range(W // 256):
             cols = pl.ds(h * 256, 256)
@@ -277,14 +290,17 @@
         load(r.tokens).wait()
         for part in range(3):
             load_qkv(part).wait()
+            if part == 0:
+                for src in first:
+                    load(src).wait()
 
             def packed(j, part=part):
                 cols = at(j, 256)
                 x = nn(r.tokens_v[...], r.wqkv_v[part, :, cols])
                 if part == 0:
-                    x = x + r.self_qv_bias[0:1, cols]
+                    x = x + r.self_qv_bias_v[0:1, cols]
                 if part == 2:
-                    x = x + r.self_qv_bias[1:2, cols]
+                    x = x + r.self_qv_bias_v[1:2, cols]
                 r.packed[part, :, cols] = x.astype(bf16)
 
             loop(HL // 256, packed, 2)
@@ -296,7 +312,7 @@
         cols = at(p, 128)
         q, k, v = (r.packed[i, :, cols] for i in range(3))
         s = nt(k, stacked(q)) * scale
-        s = jnp.where((key_row <= query_row) & (key_row < dec_len), s, -1e30)
+        s = jnp.where((key_row <= query_row) & (key_row < r.dec_len_v[0]), s, -1e30)
         w = jnp.exp(s - jnp.max(s, axis=0, keepdims=True))
         probs = w / jnp.sum(w, axis=0, keepdims=True)
         r.self_probs[p] = probs
@@ -311,6 +327,7 @@
         pl.semaphore_wait(barrier, 5)
         exchange_start(0, lambda j: nn(ycat[SELF_OUT, 0:T, :], r.self_out_v[:, at(j, 256)]))
         copy_y(SELF_OUT).start()
+        load(r.memory).wait()
 
     key, value, turned = r.key, r.value, r.turned
     odd = lax.broadcasted_iota(jnp.int32, (256, 256), 0)
@@ -329,7 +346,7 @@
         for j in range(HL // 256):
             cols = pl.ds(j * 256, 256)
             key[rows, cols] = nn(x, r.wkv_v[0, :, cols]).astype(bf16)
-            val = (nn(x, r.wkv_v[1, :, cols]) + r.cross_qv_bias[1:2, cols]).astype(bf16)
+            val = (nn(x, r.wkv_v[1, :, cols]) + r.cross_qv_bias_v[1:2, cols]).astype(bf16)
             value[rows, cols] = val
 
     def turn(src):
@@ -343,7 +360,6 @@
     def memory_pair():
         load(r.cross_kv).wait()
         loop(D // CH, part_weights, 2)
-        load(r.memory).wait()
         loop(ML // CH, pair_rows, 2)
         turn(value)
 
@@ -388,7 +404,7 @@
 
     def cross_query(j):
         cols = at(j, 256)
-        x = nn(low[...], r.cross_q_v[:, cols]) + r.cross_qv_bias[0:1, cols]
+        x = nn(low[...], r.cross_q_v[:, cols]) + r.cross_qv_bias_v[0:1, cols]
         r.query[:, cols] = x.astype(bf16)
 
     probs_ref = r.probs
@@ -409,7 +425,7 @@
         for i in range(chunks):
             rows = at(i, CH)
             s = nt(key[rows, cols], q) * (scale * LOG2E)
-            s = jnp.where(mem_row < mem_len - i * CH, s, -1e30)
+            s = jnp.where(mem_row < r.mem_len_v[0] - i * CH, s, -1e30)
             probs_ref[p, rows, :] = s
             top = jnp.maximum(top, fold(s, jnp.maximum))
         top = jnp.max(top, axis=0, keepdims=True)
@@ -440,7 +456,7 @@
 
     def ffn(j):
         cols = at(j, 256)
-        h = nn(low[...], r.fc_in_v[:, cols]) + r.fc_in_bias[:, cols]
+        h = nn(low[...], r.fc_in_v[:, cols]) + r.fc_in_bias_v[:, cols]
         phi = 0.5 * (1.0 + lax.erf(h * 0.7071067811865476))
         slope = phi + h * jnp.exp(-0.5 * h * h) * 0.3989422804014327
         r.slope[:, cols] = slope
@@ -489,7 +505,7 @@
         v = r.norm[rows, :] + (exchanged(2, rows) + out_bias[2:3, :])
         norm, unit, inv = normalize(v, 2)
         r.layer_v[rows, :] = norm.astype(bf16)
-        g = jnp.where(row16 + i * 16 < dec_len, r.cotangent_v[rows, :].astype(f32), 0.0)
+        g = jnp.where(row16 + i * 16 < r.dec_len_v[0], r.cotangent_v[rows, :].astype(f32), 0.0)
         grad = norm_back(g, unit, inv, 2)
         r.grad[rows, :] = grad
         rounded = grad.astype(bf16)
@@ -697,106 +713,112 @@
     project()
     self_attention()
     send_first()
+    each(turn_memory, 6, 0)
     memory_pair()
+    each(turn_memory, 5)
     send_x(X_TOKENS, r.tokens_v)
-    each(turn_memory, 4, 3, 1)
+    each(turn_memory, 7)
     first_norm()
     cross_attention()
     send_second()
     send_x(X_FIRST, low)
     turn(key)
-    each(turn_memory, 0, 6, 2, 5, 7)
+    each(turn_memory, 4, 1, 2, 3)
     second_norm()
-    send_x(X_SECOND, low)
     hidden_units()
     send_third()
+    send_x(X_SECOND, low)
     output_norm()
     send_x(X_FFN, low)
     hidden_grads()
     send_fourth()
     each(product, 4)
+    share_x(X_FFN)
     each(halve, 4)
-    each(product, 0, 3, 2, 1, 5)
-    each(halve, 0)
+    each(product, 5)
     second_back()
+    each(halve, 5)
     send_x(X_CROSS, low)
     cross_mixed_grad()
-    each(halve, 3, 2, 1)
-    each(cross_back, 0)
+    each(cross_back, 0, 1)
+    each(product, 3, 1, 6, 7)
     each(halve_last, 4)
-    each(product, 6)
-    each(cross_back, 1, 2)
-    each(halve, 6)
-    each(product, 7)
-    each(halve, 5)
+    each(cross_back, 2)
+    each(halve, 3, 6, 1)
+    each(halve_last, 5)
+    each(product, 0)
+    each(halve, 7)
+    each(product, 2)
+    share_x(X_CROSS)
     each(cross_back, 3)
+    send_fifth()
+    each(halve, 0, 2)
+    each(memory_term, 3)
+    each(total, 4)
     each(product, 8)
-    send_fifth()
-    each(halve_last, 0)
-    each(halve, 7)
+    each(halve_last, 3)
     each(memory_term, 0)
+    each(halve_last, 6)
+    each(pair_product, 0)
+    first_back()
+    send_x(X_SELF, low)
+    each(halve_last, 1, 7)
     each(halve, 8)
-    each(memory_term, 3)
-    each(halve_last, 3, 6)
-    each(pair_product, 1)
-    each(halve_last, 2)
-    first_back()
-    each(halve_last, 5)
-    each(memory_term, 1)
-    each(total, 4)
-    send_x(X_SELF, low)
     self_grads()
-    each(halve_last, 7, 1)
-    send_sixth()
-    each(memory_sum, 0)
     each(small_step, 0)
     each(product, 9)
-    each(total, 3, 0)
-    each(pair_product, 0)
-    each(halve_last, 8)
+    each(pair_halve, 0)
+    send_sixth()
     each(small_step, 1)
+    each(total, 3)
+    share_x(X_SELF)
+    each(halve, 9)
+    each(memory_sum, 3)
+    each(halve_last, 0)
+    each(total, 5)
+    each(memory_term, 1)
     each(total, 6)
-    each(halve, 9)
+    each(halve_last, 2)
+    each(memory_term, 2)
+    each(pair_product, 1)
+    each(halve_last, 8, 9)
+    each(memory_sum, 0)
+    each(total, 1, 7)
+    each(product, 11)
     each(pair_halve, 1)
-    each(memory_term, 2)
-    each(memory_sum, 3)
+    each(halve, 11)
+    each(total, 0)
+    each(product, 12)
+    token_grads()
+    each(halve, 12)
     each(product, 10)
-    each(pair_halve, 0)
     each(total, 2)
-    each(halve, 10)
-    each(product, 11)
-    each(total, 5)
-    each(memory_sum, 1)
-    each(halve, 11)
-    each(halve_last, 9)
-    each(product, 12)
-    each(total, 7)
-    each(halve, 12)
-    each(halve_last, 10)
     each(product, 13)
-    each(small_step, 2)
-    each(total, 1)
-    token_grads()
-    each(halve, 13)
     each(halve_last, 11)
+    each(halve, 10, 13)
     each(total, 8)
     each(halve_last, 12)
+    each(memory_sum, 1)
+    each(total, 9)
+    each(halve, 14)
+    each(small_step, 2)
+    each(halve_last, 13)
+    each(total, 11)
     each(memory_sum, 2)
+    each(total, 12)
+    each(halve_last, 14)
     each(halve, 15)
-    each(total, 9)
     each(small_step, 3)
-    each(total, 10)
-    each(halve_last, 13)
-    each(halve, 14)
-    each(total, 11)
+    each(halve_last, 10)
+    each(total, 13)
     each(halve_last, 15)
-    each(total, 12)
+    each(total, 14)
     each(small_step, 4)
-    each(total, 13)
-    each(halve_last, 14)
-    each(total, 15, 14)
+    each(total, 10, 15)
     for w in range(6):
         copy_x(w).wait_send()
+        if x_axis(w) == AXIS_Z:
+            copy_shared(w, m).wait_send()
     for u in range(UNITS):
         if u < KV:
             copy_y(u).wait_send()
@@ -816,7 +838,7 @@
 
 
 REMOTE_SEMS = 144
-LOCAL_SEMS = 40
+LOCAL_SEMS = 64
 
 
 def layer(tokens, memory, mem_len, dec_len, cotangent, wqkv, self_qv_bias, self_out, cross_q, cross_kv, cross_qv_bias, cross_out, fc_in, fc_in_bias, fc_out, out_bias, norm_gain, norm_bias):
@@ -828,8 +850,6 @@
     W = 512
     PAIRS = HL // 128
     anywhere = pl.BlockSpec(memory_space=pl.ANY)
-    in_vmem = pl.BlockSpec(memory_space=pltpu.VMEM)
-    in_smem = pl.BlockSpec(memory_space=pltpu.SMEM)
     big = dict(tokens=tokens, memory=memory, cotangent=cotangent, wqkv=wqkv, self_out=self_out, cross_q=cross_q, cross_kv=cross_kv,
                cross_out=cross_out, fc_in=fc_in, fc_out=fc_out)
     small = dict(self_qv_bias=self_qv_bias, cross_qv_bias=cross_qv_bias, fc_in_bias=fc_in_bias, out_bias=out_bias,
@@ -848,7 +868,7 @@
         g_fc_out=((R, FL), f32),
         sums=((16, D), f32),
     )
-    scratch = {name + "_v": (x.shape, x.dtype) for name, x in big.items()}
+    scratch = {name + "_v": (x.shape, x.dtype) for name, x in (big | small).items()}
     scratch |= dict(
         wkv_v=((2, D, HL), bf16),
         packed=((3, T, HL), bf16),
@@ -895,14 +915,16 @@
         sm_in=((4, 16, D), bf16),
     )
     sems = dict(send_sem=REMOTE_SEMS, recv_sem=REMOTE_SEMS, local_sem=LOCAL_SEMS)
-    names = [*big, *small, *scalars, *outs, *scratch, *sems]
+    lengths = {name + "_v": pltpu.SMEM((1,), jnp.int32) for name in scalars}
+    names = [*big, *small, *scalars, *outs, *scratch, *lengths, *sems]
     got = {}
     out = pl.pallas_call(
         functools.partial(kernel, names, got),
         out_shape=[jax.ShapeDtypeStruct(s, t) for s, t in outs.values()],
-        in_specs=[anywhere] * len(big) + [in_vmem] * len(small) + [in_smem] * len(scalars),
+        in_specs=[anywhere] * (len(big) + len(small) + len(scalars)),
         out_specs=[anywhere] * len(outs),
         scratch_shapes=[pltpu.VMEM(s, t) for s, t in scratch.values()]
+        + [*lengths.values()]
         + [pltpu.SemaphoreType.DMA((count,)) for count in sems.values()],
         compiler_params=pltpu.CompilerParams(
             collective_id=0, has_side_effects=True, vmem_limit_bytes=63 * 2**20
@@ -913,17 +935,18 @@
     return types.SimpleNamespace(**dict(zip(outs, out)))
 
 
-def finish_kernel(count, *refs):
-    ins, outs, scratch = refs[: count + 2], refs[count + 2 : 2 * count + 9], refs[2 * count + 9 :]
-    held, turned, in_sem, out_sem = scratch[: count + 1], *scratch[count + 1 :]
+def finish_kernel(count, small, *refs):
+    ins, outs, scratch = refs[: count + 2], refs[count + 2 : 2 * count + 3 + small], refs[2 * count + 3 + small :]
+    held, turned, made, (in_sem, out_sem) = scratch[: count + 2], scratch[count + 2], scratch[count + 3 : -2], scratch[-2:]
     loads = [pltpu.make_async_copy(a, b, in_sem.at[i]) for i, (a, b) in enumerate(zip(ins, held))]
     stores = [
-        pltpu.make_async_copy(a, b, out_sem.at[i]) for i, (a, b) in enumerate(zip((*held[:count], turned), outs))
+        pltpu.make_async_copy(a, b, out_sem.at[i]) for i, (a, b) in enumerate(zip((*held[:count], turned, *made), outs))
     ]
-    for load in loads:
+    for load in loads[::-1]:
         load.start()
-    sums = ins[count + 1]
-    self_bias, cross_bias, hidden_bias, out_bias, gains, shifts = outs[count + 1 :]
+    loads[count + 1].wait()
+    sums = held[count + 1]
+    self_bias, cross_bias, hidden_bias, out_bias, gains, shifts = made
     width = self_bias.shape[1]
     for row, to in ((9, self_bias), (10, cross_bias)):
         for part in range(2):
@@ -933,13 +956,15 @@
         hidden_bias[:, part * features : (part + 1) * features] = sums[11 + part : 12 + part, :]
     for first, to in ((0, out_bias), (3, gains), (6, shifts)):
         to[...] = sums[first : first + 3, :]
-    for i in range(count):
-        loads[i].wait()
-        stores[i].start()
+    for i in range(small):
+        stores[count + 1 + i].start()
     loads[count].wait()
     for part in range(2):
         turned[:, part, :] = held[count][part]
     stores[count].start()
+    for i in range(count):
+        loads[i].wait()
+        stores[i].start()
     for store in stores:
         store.wait()
 
@@ -948,18 +973,17 @@
     R, HL = kv.shape[1:]
     D = sums.shape[1]
     anywhere = pl.BlockSpec(memory_space=pl.ANY)
-    in_vmem = pl.BlockSpec(memory_space=pltpu.VMEM)
     small = [(2, HL), (2, HL), (1, 4 * HL), (3, D), (3, D), (3, D)]
     return pl.pallas_call(
-        functools.partial(finish_kernel, len(whole)),
+        functools.partial(finish_kernel, len(whole), len(small)),
         out_shape=[jax.ShapeDtypeStruct(x.shape, x.dtype) for x in whole]
         + [jax.ShapeDtypeStruct((R, 2, HL), f32)]
         + [jax.ShapeDtypeStruct(shape, f32) for shape in small],
-        in_specs=[anywhere] * (len(whole) + 1) + [in_vmem],
-        out_specs=[anywhere] * (len(whole) + 1) + [in_vmem] * len(small),
-        scratch_shapes=[pltpu.VMEM(x.shape, x.dtype) for x in (*whole, kv)]
-        + [pltpu.VMEM((R, 2, HL), f32)]
-        + [pltpu.SemaphoreType.DMA((len(whole) + 1,))] * 2,
+        in_specs=[anywhere] * (len(whole) + 2),
+        out_specs=[anywhere] * (len(whole) + 1 + len(small)),
+        scratch_shapes=[pltpu.VMEM(x.shape, x.dtype) for x in (*whole, kv, sums)]
+        + [pltpu.VMEM(shape, f32) for shape in [(R, 2, HL), *small]]
+        + [pltpu.SemaphoreType.DMA((len(whole) + 2,)), pltpu.SemaphoreType.DMA((len(whole) + 1 + len(small),))],
         compiler_params=pltpu.CompilerParams(vmem_limit_bytes=63 * 2**20),
         name="finish",
     )(*whole, kv, sums)

time: 123 us -> 117 us (0.951)
  Pallas kernels: 120 us -> 115 us
    pallas_call x1, Pallas kernels: 115 us -> 111 us  [layer(): pl.pallas_call(functools.partial(kernel, names, got), out_shape=[jax.Shap...]
where the time goes in v3:
time: 117 us
  Pallas kernels  115 us (98%)
  between operations  2.13 us (2%)
    pallas_call x1, Pallas kernels, layer(): pl.pallas_call(functools.partial(kernel, names, got), out_shape=[jax.Shap...  111 us
    pallas_call x1, Pallas kernels, finish(): pl.pallas_call(functools.partial(finish_kernel, len(whole), len(small)),...  4.13 us

profile of v3, /device:TPU:0, one launch (start us, length us, event | category | flops | bytes accessed | tf_op | source)
XLA Modules:
  0.0 117.0 jit_solution(8254362475332304533)
XLA Ops:
  1.9 110.7 %layer.1 = (bf16[128,1024]{1,0:T(8,128)(2,1)}, bf16[128,1024]{1,0:T(8,128)(2,1)}, bf16[512,1024]{1,0:T(8,128)(2,1)}, f32[3,64,512]{2,1,0:T(8,128)}, f32[64,512]{...) custom-call(bf16[128,1024]{1,0:T(8,128)(2,1)} %refs_0_.1, ...), custom_call_target="tpu_custom_call" | custom-call | tf_op jit(solution)/shard_map/layer/pallas_call | solution.py:921
  112.7 4.1 %finish.1 = (bf16[128,1024]{1,0:T(8,128)(2,1)}, bf16[128,1024]{1,0:T(8,128)(2,1)}, bf16[512,1024]{1,0:T(8,128)(2,1)}, f32[3,64,512]{2,1,0:T(8,128)}, f32[64,512]...) custom-call(bf16[128,1024]{1,0:T(8,128)(2,1)} %get-tuple-element.43., ...), custom_call_target="tpu_custom_call" | custom-call | tf_op jit(solution)/shard_map/finish/pallas_call | solution.py:977

commit v4 on v3

--- a/solution.py
+++ b/solution.py
@@ -140,6 +140,20 @@
 
     def unstacked(wide):
         return jnp.concatenate([wide[:HEAD, :T], wide[HEAD:, T:]], axis=0).T
+
+    quad_lane = lax.broadcasted_iota(jnp.int32, (T // 2, 256), 1) // HEAD
+
+    def stacked_quad(quad):
+        wide = quad.astype(f32)
+        return jnp.concatenate([jnp.where(quad_lane == h, wide, 0.0).astype(bf16) for h in range(4)], axis=0)
+
+    def unstacked_quad(wide):
+        parts = []
+        for b in range(2):
+            span = slice(b * 128, (b + 1) * 128)
+            t = wide[span, span].T
+            parts.append(jnp.where(lane_low[: T // 2], t[: T // 2], t[T // 2 :]))
+        return jnp.concatenate(parts, axis=1)
 
     def col_sum(x):
         return jnp.sum(x, axis=0, keepdims=True)
@@ -179,32 +193,45 @@
         copy_x(w).wait_recv()
         copy_shared(w, m).start()
 
+    def copy_y_half(u, half):
+        rows, there = pl.ds(half * (T // 2), T // 2), pl.ds(T + half * (T // 2), T // 2)
+        return remote(("half", half), u, 4, ycat.at[u, rows, :], ycat.at[u, there, :], partners_of[axis_of(FC_OUT)])
+
+    def gathers(u):
+        return [copy_y_half(u, half) for half in range(2)] if u < FC_IN else [copy_y(u)]
+
     def copy_y(u):
         to = partners_of[axis_of(u)]
         return remote("gather", u, KV, ycat.at[u, pl.ds(0, T), :], ycat.at[u, pl.ds(T, T), :], to)
 
+    HALF = T // 2
+
+    def exchange_part(k, j):
+        return (at(j, HALF), pl.ds(0, D)) if k < 3 else (pl.ds(0, T), at(j, 256))
+
     def exchange_copy(k, j):
-        s = k % 2
-        return remote(("ex", k), j, 4, r.ex_out.at[s, j], r.ex_in.at[s, j], to_mp)
+        rows, cols = exchange_part(k, j)
+        return remote(
+            ("ex", k), j, 4, r.ex_out.at[k % 2, rows, cols], r.ex_in.at[k % 2, rows, cols], to_mp
+        )
+
+    def exchange_half(k, half, term):
+        for j in range(D // 256):
+            cols = pl.ds(j * 256, 256)
+            r.ex_out[k % 2, at(half, HALF), cols] = term(at(half, HALF), cols).astype(bf16)
+        exchange_copy(k, half).start()
 
     def exchange_start(k, term):
-        def step(j):
-            r.ex_out[k % 2, j] = term(j).astype(bf16)
+        for j in range(D // 256):
+            r.ex_out[k % 2, :, pl.ds(j * 256, 256)] = term(j).astype(bf16)
             exchange_copy(k, j).start()
 
-        loop(4, step, 4)
-
     def exchange_wait(k):
-        def step(j):
+        for j in range(4):
             exchange_copy(k, j).wait()
 
-        loop(4, step)
-
     def exchanged(k, rows):
-        s = k % 2
-        return jnp.concatenate(
-            [r.ex_out[s, j, rows, :].astype(f32) + r.ex_in[s, j, rows, :].astype(f32) for j in range(4)], axis=1
-        )
+        return r.ex_out[k % 2, rows, :].astype(f32) + r.ex_in[k % 2, rows, :].astype(f32)
 
     def kept(u):
         return r.fc_out_v.at[at(u % 8, 256), at(u // 8, W)]
@@ -234,7 +261,8 @@
         if w not in arrived:
             arrived.add(w)
             (copy_x(w) if x_axis(w) == AXIS_Y else copy_shared(w, 1 - m)).wait_recv()
-        copy_y(u).wait_recv()
+        for copy in gathers(u):
+            copy.wait_recv()
         for h in range(W // 256):
             cols = pl.ds(h * 256, 256)
             rhs = ycat[u, :, cols]
@@ -325,7 +353,8 @@
     def send_first():
         load(r.self_out).wait()
         pl.semaphore_wait(barrier, 5)
-        exchange_start(0, lambda j: nn(ycat[SELF_OUT, 0:T, :], r.self_out_v[:, at(j, 256)]))
+        for half in range(2):
+            exchange_half(0, half, lambda rows, cols: nn(ycat[SELF_OUT, rows, :], r.self_out_v[:, cols]))
         copy_y(SELF_OUT).start()
         load(r.memory).wait()
 
@@ -386,9 +415,10 @@
         w = g * gain[k : k + 1, :]
         return inv * (w - jnp.mean(w, axis=-1, keepdims=True) - unit * jnp.mean(w * unit, axis=-1, keepdims=True))
 
-    def norm_rows(k, base, unit_ref):
-        def body(i):
-            rows = at(i, 16)
+    def norm_rows(k, half, base, unit_ref):
+        exchange_copy(k, half).wait()
+        for i in range(HALF // 16):
+            rows = pl.ds(half * HALF + i * 16, 16)
             v = base[rows, :].astype(f32) + (exchanged(k, rows) + out_bias[k : k + 1, :])
             norm, unit, inv = normalize(v, k)
             r.norm[rows, :] = norm
@@ -396,18 +426,11 @@
             r.inv[k, rows, :] = jnp.broadcast_to(inv, (16, 128))
             low[rows, :] = norm.astype(bf16)
 
-        exchange_wait(k)
-        loop(T // 16, body, T // 16)
-
-    def first_norm():
-        norm_rows(0, r.tokens_v, r.unit0)
-
-    def cross_query(j):
-        cols = at(j, 256)
-        x = nn(low[...], r.cross_q_v[:, cols]) + r.cross_qv_bias_v[0:1, cols]
-        r.query[:, cols] = x.astype(bf16)
+    def first_norm(half):
+        norm_rows(0, half, r.tokens_v, r.unit0)
 
     probs_ref = r.probs
+    dp_ref = r.dp
     low_probs = r.low_probs
     mem_row = lax.broadcasted_iota(jnp.int32, (CH, 2 * T), 0)
     chunks = ML // CH
@@ -418,67 +441,78 @@
             total = op(total, x[8 * i : 8 * i + 8])
         return total
 
-    def cross_pair(p):
-        cols = at(p, 128)
-        q = stacked(r.query[:, cols])
+    def cross_quad(half, g):
+        cols, rows_q, index = pl.ds(g * 256, 256), pl.ds(half * HALF, HALF), half * (HL // 256) + g
+        q = stacked_quad(r.query[rows_q, cols])
         top = jnp.full((8, 2 * T), -1e30, f32)
         for i in range(chunks):
             rows = at(i, CH)
             s = nt(key[rows, cols], q) * (scale * LOG2E)
             s = jnp.where(mem_row < r.mem_len_v[0] - i * CH, s, -1e30)
-            probs_ref[p, rows, :] = s
+            probs_ref[index, rows, :] = s
             top = jnp.maximum(top, fold(s, jnp.maximum))
         top = jnp.max(top, axis=0, keepdims=True)
         total = jnp.zeros((8, 2 * T), f32)
         for i in range(chunks):
             rows = at(i, CH)
-            w = jnp.exp2(probs_ref[p, rows, :] - top)
-            probs_ref[p, rows, :] = w
-            low_probs[rows, :] = w.astype(bf16)
+            w = jnp.exp2(probs_ref[index, rows, :] - top)
+            probs_ref[index, rows, :] = w
+            low_probs[g, rows, :] = w.astype(bf16)
             total = total + fold(w, jnp.add)
         part = 1.0 / jnp.sum(total, axis=0, keepdims=True)
-        r.part[p] = jnp.broadcast_to(part, (8, 2 * T))
-        mixed = nn(turned[cols, :], low_probs[...]) * part
-        ycat[CROSS_OUT, 0:T, cols] = unstacked(mixed).astype(bf16)
-
-    def cross_attention():
-        load(r.cross_q).wait()
-        loop(HL // 256, cross_query, 2)
-        loop(PAIRS, cross_pair)
-
-    def send_second():
-        load(r.cross_out).wait()
-        exchange_start(1, lambda j: nn(ycat[CROSS_OUT, 0:T, :], r.cross_out_v[:, at(j, 256)]))
-        copy_y(CROSS_OUT).start()
-
-    def second_norm():
-        norm_rows(1, r.norm, r.unit1)
-
-    def ffn(j):
-        cols = at(j, 256)
-        h = nn(low[...], r.fc_in_v[:, cols]) + r.fc_in_bias_v[:, cols]
-        phi = 0.5 * (1.0 + lax.erf(h * 0.7071067811865476))
-        slope = phi + h * jnp.exp(-0.5 * h * h) * 0.3989422804014327
-        r.slope[:, cols] = slope
-        ycat[FC_OUT + j // 2, 0:T, at(lax.rem(j, 2), 256)] = (h * phi).astype(bf16)
-
-    def hidden_units():
-        load(r.fc_in).wait()
-        for b in range(FL // W):
-            ffn(2 * b)
-            ffn(2 * b + 1)
-            copy_y(FC_OUT + b).start()
-
-    def ffn_term(j):
-        cols = at(j, 256)
-        total = nn(ycat[FC_OUT, 0:T, :], r.fc_out_v[pl.ds(0, W), cols])
+        r.part[index] = jnp.broadcast_to(part, (8, 2 * T))
+        mixed = nn(turned[cols, :], low_probs[g]) * part
+        ycat[CROSS_OUT, rows_q, cols] = unstacked_quad(mixed).astype(bf16)
+
+    def cross_attention(half):
+        if half == 0:
+            load(r.cross_q).wait()
+        rows = pl.ds(half * HALF, HALF)
+        for j in range(HL // 256):
+            cols = pl.ds(j * 256, 256)
+            x = nn(low[rows, :], r.cross_q_v[:, cols]) + r.cross_qv_bias_v[0:1, cols]
+            r.query[rows, cols] = x.astype(bf16)
+        for g in range(HL // 256):
+            cross_quad(half, g)
+
+    def send_second(half):
+        if half == 0:
+            load(r.cross_out).wait()
+        exchange_half(1, half, lambda rows, cols: nn(ycat[CROSS_OUT, rows, :], r.cross_out_v[:, cols]))
+        if half == 1:
+            copy_y(CROSS_OUT).start()
+
+    def second_norm(half):
+        norm_rows(1, half, r.norm, r.unit1)
+
+    def hidden_units(half):
+        if half == 0:
+            load(r.fc_in).wait()
+        rows = pl.ds(half * HALF, HALF)
+
+        def unit(b):
+            for part in range(2):
+                j = 2 * b + part
+                cols = at(j, 256)
+                h = nn(low[rows, :], r.fc_in_v[:, cols]) + r.fc_in_bias_v[:, cols]
+                phi = 0.5 * (1.0 + lax.erf(h * 0.7071067811865476))
+                slope = phi + h * jnp.exp(-0.5 * h * h) * 0.3989422804014327
+                dp_ref[1, pl.ds(pl.multiple_of(j * T + half * HALF, HALF), HALF), :] = slope
+                ycat[FC_OUT + b, rows, pl.ds(part * 256, 256)] = (h * phi).astype(bf16)
+            copy_y_half(FC_OUT + b, half).start()
+
+        loop(FL // W, unit)
+
+    def ffn_term(rows, cols):
+        total = nn(ycat[FC_OUT, rows, :], r.fc_out_v[pl.ds(0, W), cols])
         for b in range(1, FL // W):
-            total = total + nn(ycat[FC_OUT + b, 0:T, :], r.fc_out_v[pl.ds(b * W, W), cols])
+            total = total + nn(ycat[FC_OUT + b, rows, :], r.fc_out_v[pl.ds(b * W, W), cols])
         return total
 
-    def send_third():
-        load(r.fc_out).wait()
-        exchange_start(2, ffn_term)
+    def send_third(half):
+        if half == 0:
+            load(r.fc_out).wait()
+        exchange_half(2, half, ffn_term)
 
     row16 = lax.broadcasted_iota(jnp.int32, (16, D), 0)
     zero8 = jnp.zeros((8, D), f32)
@@ -517,13 +551,14 @@
 
     def output_norm():
         load(r.cotangent).wait()
-        exchange_wait(2)
+        for half in range(2):
+            exchange_copy(2, half).wait()
         sums_of(output_rows, 2)
         layer_copy().start()
 
     def hidden_grad(j):
         cols = at(j, 256)
-        g = nt(low[...], r.fc_out_v[at(j, 256), :]) * r.slope[:, cols]
+        g = nt(low[...], r.fc_out_v[at(j, 256), :]) * dp_ref[1, at(j, T), :]
         rounded = g.astype(bf16)
         ycat[FC_IN + j // 2, 0:T, at(j % 2, 256)] = rounded
         sm[pl.ds(11 + j // 4, 1), at(j % 4, 256)] = col_sum(rounded.astype(f32))
@@ -570,30 +605,39 @@
     def cross_mixed_grad():
         mixed_from(r.cross_out_v)
 
-    dp_ref = r.dp
-
-    def cross_back(p):
-        cols = at(p, 128)
-        q = stacked(r.query[:, cols])
-        g = stacked(mixed_grad[:, cols])
-        part = r.part[p, 0:1, :]
-        total = jnp.zeros((8, 2 * T), f32)
+    def cross_back(g):
+        cols = pl.ds(g * 256, 256)
+        halves = [pl.ds(half * HALF, HALF) for half in range(2)]
+        index = [half * (HL // 256) + g for half in range(2)]
+        gs = [stacked_quad(mixed_grad[rows, cols]) for rows in halves]
+        part = [r.part[i, 0:1, :] for i in index]
+        total = [jnp.zeros((8, 2 * T), f32)] * 2
+        both = jnp.concatenate(gs, axis=0)
         for i in range(chunks):
             rows = at(i, CH)
-            probs = probs_ref[p, rows, :] * part
-            dprobs = nt(value[rows, cols], g)
-            dp_ref[rows, :] = dprobs
-            probs_ref[p, rows, :] = probs
-            value[rows, cols] = nn(probs.astype(bf16), g).astype(bf16)
-            total = total + fold(probs * dprobs, jnp.add)
-        total = jnp.sum(total, axis=0, keepdims=True)
+            v = value[rows, cols]
+            lows = []
+            for half in range(2):
+                probs = probs_ref[index[half], rows, :] * part[half]
+                dprobs = nt(v, gs[half])
+                dp_ref[half, rows, :] = dprobs
+                probs_ref[index[half], rows, :] = probs
+                total[half] = total[half] + fold(probs * dprobs, jnp.add)
+                lows.append(probs.astype(bf16))
+            value[rows, cols] = nn(jnp.concatenate(lows, axis=1), both).astype(bf16)
+        total = [jnp.sum(x, axis=0, keepdims=True) for x in total]
+        both = jnp.concatenate([stacked_quad(r.query[rows, cols]) for rows in halves], axis=0)
         for i in range(chunks):
             rows = at(i, CH)
-            ds = (probs_ref[p, rows, :] * (dp_ref[rows, :] - total)).astype(bf16)
-            low_probs[rows, :] = ds
-            key[rows, cols] = (nn(ds, q) * scale).astype(bf16)
-        dq = nn(turned[cols, :], low_probs[...])
-        ycat[CROSS_Q, 0:T, cols] = (unstacked(dq) * scale).astype(bf16)
+            lows = []
+            for half in range(2):
+                ds = (probs_ref[index[half], rows, :] * (dp_ref[half, rows, :] - total[half])).astype(bf16)
+                low_probs[half, rows, :] = ds
+                lows.append(ds)
+            key[rows, cols] = (nn(jnp.concatenate(lows, axis=1), both) * scale).astype(bf16)
+        for half in range(2):
+            dq = nn(turned[cols, :], low_probs[half])
+            ycat[CROSS_Q, halves[half], cols] = (unstacked_quad(dq) * scale).astype(bf16)
 
     def send_fifth():
         exchange_start(4, lambda j: nt(ycat[CROSS_Q, 0:T, :], r.cross_q_v[at(j, 256), :]))
@@ -713,115 +757,119 @@
     project()
     self_attention()
     send_first()
-    each(turn_memory, 6, 0)
     memory_pair()
-    each(turn_memory, 5)
-    send_x(X_TOKENS, r.tokens_v)
-    each(turn_memory, 7)
-    first_norm()
-    cross_attention()
-    send_second()
+    first_norm(0)
+    cross_attention(0)
+    send_second(0)
+    first_norm(1)
+    cross_attention(1)
+    send_second(1)
     send_x(X_FIRST, low)
+    each(turn_memory, 6)
     turn(key)
-    each(turn_memory, 4, 1, 2, 3)
-    second_norm()
-    hidden_units()
-    send_third()
+    second_norm(0)
+    hidden_units(0)
+    send_third(0)
+    second_norm(1)
+    hidden_units(1)
+    send_third(1)
     send_x(X_SECOND, low)
     output_norm()
-    send_x(X_FFN, low)
     hidden_grads()
     send_fourth()
+    send_x(X_FFN, low)
     each(product, 4)
-    share_x(X_FFN)
+    send_x(X_TOKENS, r.tokens_v)
     each(halve, 4)
     each(product, 5)
+    share_x(X_FFN)
     second_back()
     each(halve, 5)
+    cross_mixed_grad()
+    each(product, 6)
     send_x(X_CROSS, low)
-    cross_mixed_grad()
-    each(cross_back, 0, 1)
-    each(product, 3, 1, 6, 7)
+    each(product, 0)
     each(halve_last, 4)
-    each(cross_back, 2)
-    each(halve, 3, 6, 1)
+    each(cross_back, 0)
+    each(halve, 6, 0)
+    each(cross_back, 1)
     each(halve_last, 5)
-    each(product, 0)
+    send_fifth()
+    share_x(X_CROSS)
+    each(product, 7, 3)
+    each(turn_memory, 5, 0)
     each(halve, 7)
+    each(product, 1)
+    each(turn_memory, 3)
+    each(halve_last, 0)
+    each(turn_memory, 7)
     each(product, 2)
-    share_x(X_CROSS)
-    each(cross_back, 3)
-    send_fifth()
-    each(halve, 0, 2)
+    each(turn_memory, 4)
+    each(halve_last, 6)
+    each(halve, 3)
+    each(product, 9)
+    first_back()
+    self_grads()
+    each(halve, 2)
+    send_x(X_SELF, low)
+    each(halve, 1)
+    each(turn_memory, 2)
     each(memory_term, 3)
-    each(total, 4)
+    each(halve, 9)
+    each(turn_memory, 1)
+    each(halve_last, 7)
     each(product, 8)
     each(halve_last, 3)
-    each(memory_term, 0)
-    each(halve_last, 6)
+    each(product, 11)
     each(pair_product, 0)
-    first_back()
-    send_x(X_SELF, low)
-    each(halve_last, 1, 7)
-    each(halve, 8)
-    self_grads()
+    each(product, 12)
+    share_x(X_SELF)
+    each(total, 6)
     each(small_step, 0)
-    each(product, 9)
+    each(halve, 11)
+    each(product, 13)
+    each(halve_last, 9)
+    each(memory_term, 1)
     each(pair_halve, 0)
-    send_sixth()
-    each(small_step, 1)
-    each(total, 3)
-    share_x(X_SELF)
-    each(halve, 9)
-    each(memory_sum, 3)
-    each(halve_last, 0)
-    each(total, 5)
-    each(memory_term, 1)
-    each(total, 6)
-    each(halve_last, 2)
-    each(memory_term, 2)
-    each(pair_product, 1)
-    each(halve_last, 8, 9)
-    each(memory_sum, 0)
-    each(total, 1, 7)
-    each(product, 11)
-    each(pair_halve, 1)
-    each(halve, 11)
-    each(total, 0)
-    each(product, 12)
-    token_grads()
     each(halve, 12)
     each(product, 10)
-    each(total, 2)
-    each(product, 13)
+    each(memory_sum, 3)
+    each(memory_term, 0)
     each(halve_last, 11)
-    each(halve, 10, 13)
-    each(total, 8)
-    each(halve_last, 12)
+    each(halve, 8, 13)
+    each(small_step, 1)
+    each(pair_product, 1)
+    each(total, 9)
+    each(memory_term, 2)
+    each(halve_last, 1, 12)
+    send_sixth()
     each(memory_sum, 1)
-    each(total, 9)
-    each(halve, 14)
+    each(total, 7, 4, 3)
+    each(pair_halve, 1)
+    each(halve, 10, 14)
+    each(halve_last, 8, 2, 13)
+    each(memory_sum, 2)
     each(small_step, 2)
-    each(halve_last, 13)
-    each(total, 11)
-    each(memory_sum, 2)
+    each(halve, 15)
+    each(memory_sum, 0)
+    each(total, 5)
+    each(halve_last, 10, 14)
     each(total, 12)
-    each(halve_last, 14)
-    each(halve, 15)
     each(small_step, 3)
-    each(halve_last, 10)
-    each(total, 13)
+    each(total, 10, 2)
     each(halve_last, 15)
-    each(total, 14)
+    token_grads()
+    each(total, 8, 1, 13)
     each(small_step, 4)
-    each(total, 10, 15)
+    each(total, 0, 11, 14, 15)
     for w in range(6):
         copy_x(w).wait_send()
         if x_axis(w) == AXIS_Z:
             copy_shared(w, m).wait_send()
     for u in range(UNITS):
         if u < KV:
-            copy_y(u).wait_send()
+            for copy in gathers(u):
+                copy.wait_send()
             copy_core(u).wait_send()
         copy_half(u).wait_send()
         copy_last(u).wait_send()
@@ -837,7 +885,7 @@
     refs_at.update(remote=sum(n for _, n in given.values()), local=sum(n for _, n in local_given.values()))
 
 
-REMOTE_SEMS = 144
+REMOTE_SEMS = 160
 LOCAL_SEMS = 64
 
 
@@ -877,8 +925,8 @@
         ycat=((KV, 2 * T, W), bf16),
         xcat=((6, 512, 256), bf16),
         xsend=((6, 512, 128), bf16),
-        ex_out=((2, 4, T, 256), bf16),
-        ex_in=((2, 4, T, 256), bf16),
+        ex_out=((2, T, D), bf16),
+        ex_in=((2, T, D), bf16),
         norm=((T, D), f32),
         unit0=((T, D), f32),
         unit1=((T, D), f32),
@@ -891,9 +939,8 @@
         mixed_grad=((T, HL), bf16),
         probs=((PAIRS, ML, 2 * T), f32),
         part=((PAIRS, 8, 2 * T), f32),
-        low_probs=((ML, 2 * T), bf16),
-        dp=((ML, 2 * T), f32),
-        slope=((T, FL), f32),
+        low_probs=((2, ML, 2 * T), bf16),
+        dp=((2, ML, 2 * T), f32),
         memory_t=((D, ML), bf16),
         layer_v=((T, D), bf16),
         tokens_g=((T, D), bf16),

time: 117 us -> 109 us (0.932)
  Pallas kernels: 115 us -> 107 us
    pallas_call x1, Pallas kernels: 111 us -> 103 us  [layer(): pl.pallas_call(functools.partial(kernel, names, got), out_shape=[jax.Shap...]
where the time goes in v4:
time: 109 us
  Pallas kernels  107 us (98%)
  between operations  2.13 us (2%)
    pallas_call x1, Pallas kernels, layer(): pl.pallas_call(functools.partial(kernel, names, got), out_shape=[jax.Shap...  103 us
    pallas_call x1, Pallas kernels, finish(): pl.pallas_call(functools.partial(finish_kernel, len(whole), len(small)),...  4.13 us

profile of v4, /device:TPU:0, one launch (start us, length us, event | category | flops | bytes accessed | tf_op | source)
XLA Modules:
  0.0 109.1 jit_solution(6736323421767841221)
XLA Ops:
  1.9 102.8 %layer.1 = (bf16[128,1024]{1,0:T(8,128)(2,1)}, bf16[128,1024]{1,0:T(8,128)(2,1)}, bf16[512,1024]{1,0:T(8,128)(2,1)}, f32[3,64,512]{2,1,0:T(8,128)}, f32[64,512]{...) custom-call(bf16[128,1024]{1,0:T(8,128)(2,1)} %refs_0_.1, ...), custom_call_target="tpu_custom_call" | custom-call | tf_op jit(solution)/shard_map/layer/pallas_call | solution.py:968
  104.8 4.1 %finish.1 = (bf16[128,1024]{1,0:T(8,128)(2,1)}, bf16[128,1024]{1,0:T(8,128)(2,1)}, bf16[512,1024]{1,0:T(8,128)(2,1)}, f32[3,64,512]{2,1,0:T(8,128)}, f32[64,512]...) custom-call(bf16[128,1024]{1,0:T(8,128)(2,1)} %get-tuple-element.43., ...), custom_call_target="tpu_custom_call" | custom-call | tf_op jit(solution)/shard_map/finish/pallas_call | solution.py:1024

commit v5 on v4

--- a/solution.py
+++ b/solution.py
@@ -295,24 +295,20 @@
         r.last_out[u] = (local_sum(u, part_rows(u, 1 - zh)) + got).astype(bf16)
         copy_last(u).start()
 
-    def out_copy(u):
-        if u < FC_IN:
-            to = r.g_fc_out.at[:, at(u, W)]
-        elif u < CROSS_OUT:
-            to = r.g_fc_in.at[:, at(u - FC_IN, W)]
-        elif u < QKV:
-            to = (r.g_cross_out, r.g_cross_q, r.g_self_out)[u - CROSS_OUT]
-        elif u < KV:
-            to = r.g_qkv.at[u - QKV]
-        else:
-            to = r.g_kv.at[u - KV]
-        return local("unit", r.fin.at[u], to, u, UNITS)
-
     def total(u):
         copy_last(u).wait_recv()
         got = r.half_in[u, at(zh, 64), :].astype(f32) + r.last_in[u].astype(f32)
-        r.fin[u] = local_sum(u, part_rows(u, zh)) + got
-        out_copy(u).start()
+        x = local_sum(u, part_rows(u, zh)) + got
+        if u < FC_IN:
+            r.g_fc_out[:, at(u, W)] = x
+        elif u < CROSS_OUT:
+            r.g_fc_in[:, at(u - FC_IN, W)] = x
+        elif u < QKV:
+            (r.g_cross_out, r.g_cross_q, r.g_self_out)[u - CROSS_OUT][...] = x
+        elif u < KV:
+            r.g_qkv[u - QKV] = x
+        else:
+            r.g_kv[u - KV] = x
 
     def project():
         load(r.tokens).wait()
@@ -369,14 +365,19 @@
         r.wkv_v[0, rows, :] = x[:CH]
         r.wkv_v[1, rows, :] = x[CH:]
 
+    BIG = 512
+
     def pair_rows(i):
-        rows = at(i, CH)
-        x = r.memory_v[rows, :]
+        rows = at(i, BIG)
         for j in range(HL // 256):
             cols = pl.ds(j * 256, 256)
-            key[rows, cols] = nn(x, r.wkv_v[0, :, cols]).astype(bf16)
-            val = (nn(x, r.wkv_v[1, :, cols]) + r.cross_qv_bias_v[1:2, cols]).astype(bf16)
-            value[rows, cols] = val
+            key[rows, cols] = nn(r.memory_v[rows, :], r.wkv_v[0, :, cols]).astype(bf16)
+            x = nn(r.memory_v[rows, :], r.wkv_v[1, :, cols]) + r.cross_qv_bias_v[1:2, cols]
+            value[rows, cols] = x.astype(bf16)
+            for b in range(BIG // 128):
+                for h in range(2):
+                    block = x[b * 128 : (b + 1) * 128, h * 128 : (h + 1) * 128].T
+                    turned[pl.ds(j * 256 + h * 128, 128), pl.ds(pl.multiple_of(i * BIG + b * 128, 128), 128)] = block.astype(bf16)
 
     def turn(src):
         def step(i):
@@ -389,8 +390,7 @@
     def memory_pair():
         load(r.cross_kv).wait()
         loop(D // CH, part_weights, 2)
-        loop(ML // CH, pair_rows, 2)
-        turn(value)
+        loop(ML // BIG, pair_rows)
 
     def turn_memory(i):
         rows = at(i, CH)
@@ -445,23 +445,25 @@
         cols, rows_q, index = pl.ds(g * 256, 256), pl.ds(half * HALF, HALF), half * (HL // 256) + g
         q = stacked_quad(r.query[rows_q, cols])
         top = jnp.full((8, 2 * T), -1e30, f32)
-        for i in range(chunks):
-            rows = at(i, CH)
-            s = nt(key[rows, cols], q) * (scale * LOG2E)
-            s = jnp.where(mem_row < r.mem_len_v[0] - i * CH, s, -1e30)
-            probs_ref[index, rows, :] = s
-            top = jnp.maximum(top, fold(s, jnp.maximum))
+        for b in range(ML // BIG):
+            scores = nt(key[pl.ds(b * BIG, BIG), cols], q)
+            for i in range(BIG // CH):
+                first = b * BIG + i * CH
+                s = scores[i * CH : (i + 1) * CH] * (scale * LOG2E)
+                s = jnp.where(mem_row < r.mem_len_v[0] - first, s, -1e30)
+                probs_ref[index, pl.ds(first, CH), :] = s
+                top = jnp.maximum(top, fold(s, jnp.maximum))
         top = jnp.max(top, axis=0, keepdims=True)
         total = jnp.zeros((8, 2 * T), f32)
         for i in range(chunks):
             rows = at(i, CH)
             w = jnp.exp2(probs_ref[index, rows, :] - top)
             probs_ref[index, rows, :] = w
-            low_probs[g, rows, :] = w.astype(bf16)
+            low_probs[rows, cols] = w.astype(bf16)
             total = total + fold(w, jnp.add)
         part = 1.0 / jnp.sum(total, axis=0, keepdims=True)
         r.part[index] = jnp.broadcast_to(part, (8, 2 * T))
-        mixed = nn(turned[cols, :], low_probs[g]) * part
+        mixed = nn(turned[cols, :], low_probs[:, cols]) * part
         ycat[CROSS_OUT, rows_q, cols] = unstacked_quad(mixed).astype(bf16)
 
     def cross_attention(half):
@@ -485,6 +487,9 @@
     def second_norm(half):
         norm_rows(1, half, r.norm, r.unit1)
 
+    def normal_share(h):
+        return 0.5 * (1.0 + lax.erf(h * 0.7071067811865476))
+
     def hidden_units(half):
         if half == 0:
             load(r.fc_in).wait()
@@ -495,13 +500,16 @@
                 j = 2 * b + part
                 cols = at(j, 256)
                 h = nn(low[rows, :], r.fc_in_v[:, cols]) + r.fc_in_bias_v[:, cols]
-                phi = 0.5 * (1.0 + lax.erf(h * 0.7071067811865476))
-                slope = phi + h * jnp.exp(-0.5 * h * h) * 0.3989422804014327
-                dp_ref[1, pl.ds(pl.multiple_of(j * T + half * HALF, HALF), HALF), :] = slope
-                ycat[FC_OUT + b, rows, pl.ds(part * 256, 256)] = (h * phi).astype(bf16)
+                dp_ref[1, pl.ds(j * T + half * HALF, HALF), :] = h
+                ycat[FC_OUT + b, rows, pl.ds(part * 256, 256)] = (h * normal_share(h)).astype(bf16)
             copy_y_half(FC_OUT + b, half).start()
 
-        loop(FL // W, unit)
+        for b in range(FL // W):
+            unit(b)
+
+    def slopes(j):
+        h = dp_ref[1, at(j, T), :]
+        dp_ref[1, at(j, T), :] = normal_share(h) + h * jnp.exp(-0.5 * h * h) * 0.3989422804014327
 
     def ffn_term(rows, cols):
         total = nn(ycat[FC_OUT, rows, :], r.fc_out_v[pl.ds(0, W), cols])
@@ -538,7 +546,7 @@
         rows = at(i, 16)
         v = r.norm[rows, :] + (exchanged(2, rows) + out_bias[2:3, :])
         norm, unit, inv = normalize(v, 2)
-        r.layer_v[rows, :] = norm.astype(bf16)
+        r.layer_out[rows, :] = norm.astype(bf16)
         g = jnp.where(row16 + i * 16 < r.dec_len_v[0], r.cotangent_v[rows, :].astype(f32), 0.0)
         grad = norm_back(g, unit, inv, 2)
         r.grad[rows, :] = grad
@@ -546,15 +554,11 @@
         low[rows, :] = rounded
         return g, unit, rounded.astype(f32)
 
-    def layer_copy():
-        return local("layer", r.layer_v, r.layer_out)
-
     def output_norm():
         load(r.cotangent).wait()
         for half in range(2):
             exchange_copy(2, half).wait()
         sums_of(output_rows, 2)
-        layer_copy().start()
 
     def hidden_grad(j):
         cols = at(j, 256)
@@ -613,30 +617,32 @@
         part = [r.part[i, 0:1, :] for i in index]
         total = [jnp.zeros((8, 2 * T), f32)] * 2
         both = jnp.concatenate(gs, axis=0)
-        for i in range(chunks):
-            rows = at(i, CH)
-            v = value[rows, cols]
-            lows = []
+        lanes = [pl.ds(half * 2 * T, 2 * T) for half in range(2)]
+        for b in range(ML // BIG):
+            big = pl.ds(b * BIG, BIG)
             for half in range(2):
-                probs = probs_ref[index[half], rows, :] * part[half]
-                dprobs = nt(v, gs[half])
-                dp_ref[half, rows, :] = dprobs
-                probs_ref[index[half], rows, :] = probs
-                total[half] = total[half] + fold(probs * dprobs, jnp.add)
-                lows.append(probs.astype(bf16))
-            value[rows, cols] = nn(jnp.concatenate(lows, axis=1), both).astype(bf16)
+                dbig = nt(value[big, cols], gs[half])
+                for i in range(BIG // CH):
+                    rows = pl.ds(b * BIG + i * CH, CH)
+                    probs = probs_ref[index[half], rows, :] * part[half]
+                    dprobs = dbig[i * CH : (i + 1) * CH]
+                    dp_ref[half, rows, :] = dprobs
+                    probs_ref[index[half], rows, :] = probs
+                    total[half] = total[half] + fold(probs * dprobs, jnp.add)
+                    low_probs[rows, lanes[half]] = probs.astype(bf16)
+            value[big, cols] = nn(low_probs[big, :], both).astype(bf16)
         total = [jnp.sum(x, axis=0, keepdims=True) for x in total]
         both = jnp.concatenate([stacked_quad(r.query[rows, cols]) for rows in halves], axis=0)
-        for i in range(chunks):
-            rows = at(i, CH)
-            lows = []
+        for b in range(ML // BIG):
+            big = pl.ds(b * BIG, BIG)
             for half in range(2):
-                ds = (probs_ref[index[half], rows, :] * (dp_ref[half, rows, :] - total[half])).astype(bf16)
-                low_probs[half, rows, :] = ds
-                lows.append(ds)
-            key[rows, cols] = (nn(jnp.concatenate(lows, axis=1), both) * scale).astype(bf16)
+                for i in range(BIG // CH):
+                    rows = pl.ds(b * BIG + i * CH, CH)
+                    ds = probs_ref[index[half], rows, :] * (dp_ref[half, rows, :] - total[half])
+                    low_probs[rows, lanes[half]] = ds.astype(bf16)
+            key[big, cols] = (nn(low_probs[big, :], both) * scale).astype(bf16)
         for half in range(2):
-            dq = nn(turned[cols, :], low_probs[half])
+            dq = nn(turned[cols, :], low_probs[:, lanes[half]])
             ycat[CROSS_Q, halves[half], cols] = (unstacked_quad(dq) * scale).astype(bf16)
 
     def send_fifth():
@@ -646,37 +652,29 @@
         sm[10:11, HL : 2 * HL] = col_sum(value[...].astype(f32))
 
     def gm_copy(i):
-        return remote("gm", i, 4, r.gm_out.at[i], r.gm_in.at[i], to_mp)
+        cols = at(i, 256)
+        return remote("gm", i, 4, r.gm_out.at[:, cols], r.gm_in.at[:, cols], to_mp)
 
     def memory_term(i):
-        for half, to in (((1 - m) * 4 + i, r.gm_out), (m * 4 + i, r.gm_own)):
-            rows = at(half, CH)
-            for j in range(D // 256):
-                cols = pl.ds(j * 256, 256)
-                x = nt(key[rows, :], r.wkv_v[0, cols, :]) + nt(value[rows, :], r.wkv_v[1, cols, :])
-                to[i, :, cols] = x.astype(bf16)
+        cols = pl.ds(i * 256, 256)
+        for half, to in ((1 - m, r.gm_out), (m, r.grad_memory)):
+            rows = at(half, ML // 2)
+            x = nt(key[rows, :], r.wkv_v[0, cols, :]) + nt(value[rows, :], r.wkv_v[1, cols, :])
+            to[:, cols] = x.astype(bf16)
         gm_copy(i).start()
-
-    def gm_store(i):
-        return local("gm_store", r.gm_own.at[i], r.grad_memory.at[at(i, CH), :], i, 4)
 
     def memory_sum(i):
         gm_copy(i).wait()
-        r.gm_own[i] = (r.gm_own[i].astype(f32) + r.gm_in[i].astype(f32)).astype(bf16)
-        gm_store(i).start()
+        cols = pl.ds(i * 256, 256)
+        r.grad_memory[:, cols] = (r.grad_memory[:, cols].astype(f32) + r.gm_in[:, cols].astype(f32)).astype(bf16)
 
     def pair_product(v):
         pair = key if v == 0 else value
         for h in range(2):
             cols = pl.ds(h * 256, 256)
-
-            def step(b, cols=cols, h=h):
-                rows = at(b, 128)
-                other, own = r.memory_t[at((1 - c) * 4 + b, 128), :], r.memory_t[at(c * 4 + b, 128), :]
-                r.kvc_out[v, rows, cols] = nn(other, pair[:, cols]).astype(bf16)
-                r.memory_v[rows, pl.ds(v * W + h * 256, 256)] = nn(own, pair[:, cols]).astype(bf16)
-
-            loop(4, step)
+            rhs = pair[:, cols]
+            r.kvc_out[v, :, cols] = nn(r.memory_t[at(1 - c, D // 2), :], rhs).astype(bf16)
+            r.memory_v[0 : D // 2, pl.ds(v * W + h * 256, 256)] = nn(r.memory_t[at(c, D // 2), :], rhs).astype(bf16)
         kvc_copy(v).start()
 
     def pair_halve(v):
@@ -720,35 +718,26 @@
     def send_sixth():
         exchange_start(5, packed_term)
 
-    def token_copy():
-        return local("tokens_g", r.tokens_g, r.grad_tokens)
-
     def token_grads():
         def body(i):
             rows = at(i, 16)
-            r.tokens_g[rows, :] = (r.grad[rows, :] + exchanged(5, rows)).astype(bf16)
+            r.grad_tokens[rows, :] = (r.grad[rows, :] + exchanged(5, rows)).astype(bf16)
 
         exchange_wait(5)
         loop(T // 16, body, 2)
-        token_copy().start()
 
     doubling = (to_c, to_y, to_z1, to_z2)
 
     def small_copy(k):
         return remote("small", k, 4, r.sm_out.at[k], r.sm_in.at[k], doubling[k])
-
-    def sums_copy():
-        return local("sums", sm, r.sums)
 
     def small_step(k):
         if k > 0:
             small_copy(k - 1).wait()
-            sm[...] = r.sm_out[k - 1].astype(f32) + r.sm_in[k - 1].astype(f32)
+            (sm if k < 4 else r.sums)[...] = r.sm_out[k - 1].astype(f32) + r.sm_in[k - 1].astype(f32)
         if k < 4:
             r.sm_out[k] = sm[...].astype(bf16)
             small_copy(k).start()
-        else:
-            sums_copy().start()
 
     def each(step, *indices):
         for i in indices:
@@ -761,107 +750,113 @@
     first_norm(0)
     cross_attention(0)
     send_second(0)
+    each(turn_memory, 0)
     first_norm(1)
     cross_attention(1)
     send_second(1)
     send_x(X_FIRST, low)
-    each(turn_memory, 6)
-    turn(key)
     second_norm(0)
     hidden_units(0)
     send_third(0)
     second_norm(1)
     hidden_units(1)
     send_third(1)
+    turn(key)
+    each(slopes, 7)
     send_x(X_SECOND, low)
+    each(turn_memory, 7)
+    each(slopes, 3)
+    each(turn_memory, 3)
+    each(slopes, 4, 0, 6, 5, 2, 1)
     output_norm()
     hidden_grads()
+    send_x(X_FFN, low)
     send_fourth()
-    send_x(X_FFN, low)
     each(product, 4)
     send_x(X_TOKENS, r.tokens_v)
+    share_x(X_FFN)
     each(halve, 4)
     each(product, 5)
-    share_x(X_FFN)
     second_back()
+    cross_mixed_grad()
+    send_x(X_CROSS, low)
+    each(product, 2)
+    each(turn_memory, 6)
     each(halve, 5)
-    cross_mixed_grad()
-    each(product, 6)
-    send_x(X_CROSS, low)
+    each(cross_back, 0)
+    each(product, 7)
+    each(halve_last, 4)
+    each(halve, 2)
+    each(cross_back, 1)
+    send_fifth()
+    each(halve, 7)
+    each(product, 6, 3, 1)
+    share_x(X_CROSS)
+    each(halve_last, 5)
+    each(halve, 3)
+    each(halve_last, 2)
+    each(turn_memory, 4)
+    each(halve, 6)
     each(product, 0)
-    each(halve_last, 4)
-    each(cross_back, 0)
-    each(halve, 6, 0)
-    each(cross_back, 1)
-    each(halve_last, 5)
-    send_fifth()
-    share_x(X_CROSS)
-    each(product, 7, 3)
-    each(turn_memory, 5, 0)
-    each(halve, 7)
-    each(product, 1)
-    each(turn_memory, 3)
-    each(halve_last, 0)
-    each(turn_memory, 7)
-    each(product, 2)
-    each(turn_memory, 4)
-    each(halve_last, 6)
-    each(halve, 3)
-    each(product, 9)
+    each(memory_term, 3)
+    each(halve, 1)
+    each(turn_memory, 2)
     first_back()
     self_grads()
-    each(halve, 2)
+    each(halve_last, 7)
+    each(total, 5)
+    each(halve, 0)
+    each(small_step, 0)
+    each(product, 9)
+    each(halve_last, 3)
+    each(turn_memory, 5)
+    each(product, 8)
+    each(memory_term, 2)
     send_x(X_SELF, low)
-    each(halve, 1)
-    each(turn_memory, 2)
-    each(memory_term, 3)
     each(halve, 9)
+    each(small_step, 1)
+    each(product, 11)
     each(turn_memory, 1)
-    each(halve_last, 7)
-    each(product, 8)
-    each(halve_last, 3)
-    each(product, 11)
-    each(pair_product, 0)
+    each(halve_last, 1, 6)
+    each(memory_sum, 2)
+    each(total, 3)
+    each(halve, 11)
+    each(total, 4)
+    each(pair_product, 1, 0)
     each(product, 12)
+    each(halve_last, 9)
     share_x(X_SELF)
-    each(total, 6)
-    each(small_step, 0)
-    each(halve, 11)
+    each(memory_term, 1)
     each(product, 13)
-    each(halve_last, 9)
-    each(memory_term, 1)
+    each(halve, 8)
+    each(halve_last, 0)
+    each(pair_halve, 1)
+    each(halve, 12, 13)
+    send_sixth()
+    each(small_step, 2)
     each(pair_halve, 0)
-    each(halve, 12)
     each(product, 10)
+    each(halve_last, 8, 11)
+    each(total, 2, 1, 6)
+    each(halve, 10, 15)
+    token_grads()
+    each(memory_term, 0)
+    each(halve_last, 13, 12)
+    each(total, 7)
+    each(halve, 14)
+    each(halve_last, 10)
+    each(total, 8)
+    each(small_step, 3)
+    each(halve_last, 15)
+    each(memory_sum, 1)
+    each(total, 10, 13, 9)
+    each(halve_last, 14)
+    each(memory_sum, 0)
+    each(total, 15, 11)
+    each(small_step, 4)
+    each(total, 12, 0)
     each(memory_sum, 3)
-    each(memory_term, 0)
-    each(halve_last, 11)
-    each(halve, 8, 13)
-    each(small_step, 1)
-    each(pair_product, 1)
-    each(total, 9)
-    each(memory_term, 2)
-    each(halve_last, 1, 12)
-    send_sixth()
-    each(memory_sum, 1)
-    each(total, 7, 4, 3)
-    each(pair_halve, 1)
-    each(halve, 10, 14)
-    each(halve_last, 8, 2, 13)
-    each(memory_sum, 2)
-    each(small_step, 2)
-    each(halve, 15)
-    each(memory_sum, 0)
-    each(total, 5)
-    each(halve_last, 10, 14)
-    each(total, 12)
-    each(small_step, 3)
-    each(total, 10, 2)
-    each(halve_last, 15)
-    token_grads()
-    each(total, 8, 1, 13)
-    each(small_step, 4)
-    each(total, 0, 11, 14, 15)
+    each(total, 14)
     for w in range(6):
         copy_x(w).wait_send()
         if x_axis(w) == AXIS_Z:
@@ -873,19 +868,14 @@
             copy_core(u).wait_send()
         copy_half(u).wait_send()
         copy_last(u).wait_send()
-        out_copy(u).wait()
     for v in range(2):
         kvc_copy(v).wait_send()
         kvy_copy(v).wait_send()
-    for i in range(4):
-        gm_store(i).wait()
-    layer_copy().wait()
-    token_copy().wait()
-    sums_copy().wait()
     refs_at.update(remote=sum(n for _, n in given.values()), local=sum(n for _, n in local_given.values()))
 
 
 REMOTE_SEMS = 160
+LAYER_VMEM = 59 * 2**20
 LOCAL_SEMS = 64
 
 
@@ -939,14 +929,11 @@
         mixed_grad=((T, HL), bf16),
         probs=((PAIRS, ML, 2 * T), f32),
         part=((PAIRS, 8, 2 * T), f32),
-        low_probs=((2, ML, 2 * T), bf16),
+        low_probs=((ML, 4 * T), bf16),
         dp=((2, ML, 2 * T), f32),
         memory_t=((D, ML), bf16),
-        layer_v=((T, D), bf16),
-        tokens_g=((T, D), bf16),
-        gm_out=((4, 128, D), bf16),
-        gm_own=((4, 128, D), bf16),
-        gm_in=((4, 128, D), bf16),
+        gm_out=((ML // 2, D), bf16),
+        gm_in=((ML // 2, D), bf16),
         core_in=((KV, 256, W), bf16),
         kvc_out=((2, 512, W), bf16),
         kvc_in=((2, 512, W), bf16),
@@ -956,7 +943,6 @@
         half_in=((UNITS, 128, W), bf16),
         last_out=((UNITS, 64, W), bf16),
         last_in=((UNITS, 64, W), bf16),
-        fin=((UNITS, 64, W), f32),
         sm=((16, D), f32),
         sm_out=((4, 16, D), bf16),
         sm_in=((4, 16, D), bf16),
@@ -967,14 +953,14 @@
     got = {}
     out = pl.pallas_call(
         functools.partial(kernel, names, got),
-        out_shape=[jax.ShapeDtypeStruct(s, t) for s, t in outs.values()],
+        out_shape=[pltpu.VMEM(s, t) for s, t in outs.values()],
         in_specs=[anywhere] * (len(big) + len(small) + len(scalars)),
-        out_specs=[anywhere] * len(outs),
+        out_specs=[pl.BlockSpec(memory_space=pltpu.VMEM)] * len(outs),
         scratch_shapes=[pltpu.VMEM(s, t) for s, t in scratch.values()]
         + [*lengths.values()]
         + [pltpu.SemaphoreType.DMA((count,)) for count in sems.values()],
         compiler_params=pltpu.CompilerParams(
-            collective_id=0, has_side_effects=True, vmem_limit_bytes=63 * 2**20
+            collective_id=0, has_side_effects=True, vmem_limit_bytes=LAYER_VMEM
         ),
         name="layer",
     )(*big.values(), *small.values(), *scalars.values())
@@ -984,15 +970,16 @@
 
 def finish_kernel(count, small, *refs):
     ins, outs, scratch = refs[: count + 2], refs[count + 2 : 2 * count + 3 + small], refs[2 * count + 3 + small :]
-    held, turned, made, (in_sem, out_sem) = scratch[: count + 2], scratch[count + 2], scratch[count + 3 : -2], scratch[-2:]
-    loads = [pltpu.make_async_copy(a, b, in_sem.at[i]) for i, (a, b) in enumerate(zip(ins, held))]
+    turned, made, sem = scratch[0], scratch[1:-1], scratch[-1]
     stores = [
-        pltpu.make_async_copy(a, b, out_sem.at[i]) for i, (a, b) in enumerate(zip((*held[:count], turned, *made), outs))
+        pltpu.make_async_copy(a, b, sem.at[i]) for i, (a, b) in enumerate(zip((*ins[:count], turned, *made), outs))
     ]
-    for load in loads[::-1]:
-        load.start()
-    loads[count + 1].wait()
-    sums = held[count + 1]
+    for i in range(count):
+        stores[i].start()
+    kv, sums = ins[count:]
+    for part in range(2):
+        turned[:, part, :] = kv[part]
+    stores[count].start()
     self_bias, cross_bias, hidden_bias, out_bias, gains, shifts = made
     width = self_bias.shape[1]
     for row, to in ((9, self_bias), (10, cross_bias)):
@@ -1005,13 +992,6 @@
         to[...] = sums[first : first + 3, :]
     for i in range(small):
         stores[count + 1 + i].start()
-    loads[count].wait()
-    for part in range(2):
-        turned[:, part, :] = held[count][part]
-    stores[count].start()
-    for i in range(count):
-        loads[i].wait()
-        stores[i].start()
     for store in stores:
         store.wait()
 
@@ -1020,18 +1000,18 @@
     R, HL = kv.shape[1:]
     D = sums.shape[1]
     anywhere = pl.BlockSpec(memory_space=pl.ANY)
+    in_vmem = pl.BlockSpec(memory_space=pltpu.VMEM)
     small = [(2, HL), (2, HL), (1, 4 * HL), (3, D), (3, D), (3, D)]
     return pl.pallas_call(
         functools.partial(finish_kernel, len(whole), len(small)),
         out_shape=[jax.ShapeDtypeStruct(x.shape, x.dtype) for x in whole]
         + [jax.ShapeDtypeStruct((R, 2, HL), f32)]
         + [jax.ShapeDtypeStruct(shape, f32) for shape in small],
-        in_specs=[anywhere] * (len(whole) + 2),
+        in_specs=[in_vmem] * (len(whole) + 2),
         out_specs=[anywhere] * (len(whole) + 1 + len(small)),
-        scratch_shapes=[pltpu.VMEM(x.shape, x.dtype) for x in (*whole, kv, sums)]
-        + [pltpu.VMEM(shape, f32) for shape in [(R, 2, HL), *small]]
-        + [pltpu.SemaphoreType.DMA((len(whole) + 2,)), pltpu.SemaphoreType.DMA((len(whole) + 1 + len(small),))],
-        compiler_params=pltpu.CompilerParams(vmem_limit_bytes=63 * 2**20),
+        scratch_shapes=[pltpu.VMEM(shape, f32) for shape in [(R, 2, HL), *small]]
+        + [pltpu.SemaphoreType.DMA((len(whole) + 1 + len(small),))],
+        compiler_params=pltpu.CompilerParams(vmem_limit_bytes=8 * 2**20),
         name="finish",
     )(*whole, kv, sums)
 
@@ -1066,9 +1046,6 @@
             return x
         return lax.psum_scatter(x, "dp", scatter_dimension=axis, axis_index_groups=groups, tiled=True)
 
-    sums = got.sums
-    if outer > 1:
-        sums = lax.psum(sums, "dp", axis_index_groups=groups)
     (
         layer_out, grad_tokens, grad_memory, qkv, self_out, cross_q, cross_out, fc_in, fc_out, kv,
         self_bias, cross_bias, hidden_bias, out_bias, gains, shifts,
@@ -1078,8 +1055,12 @@
             got.g_fc_in, got.g_fc_out,
         ),
         got.g_kv,
-        sums,
+        got.sums,
     )
+    small = (self_bias, cross_bias, hidden_bias, out_bias, gains, shifts)
+    if outer > 1:
+        small = lax.psum(small, "dp", axis_index_groups=groups)
+    self_bias, cross_bias, hidden_bias, out_bias, gains, shifts = small
     return (
         regroup(layer_out, 1, False),
         regroup(grad_tokens, 1, False),

time: 109 us -> 105 us (0.963)
  Pallas kernels: 107 us -> 103 us
    pallas_call x1, Pallas kernels: 4.13 us -> 1.99 us  [finish(): pl.pallas_call(functools.partial(finish_kernel, len(whole), len(small)),...]
    pallas_call x1, Pallas kernels: 103 us -> 101 us  [layer(): pl.pallas_call(functools.partial(kernel, names, got), out_shape=[pltpu.VM...]
where the time goes in v5:
time: 105 us
  Pallas kernels  103 us (98%)
  between operations  2.13 us (2%)
    pallas_call x1, Pallas kernels, layer(): pl.pallas_call(functools.partial(kernel, names, got), out_shape=[pltpu.VM...  101 us

profile of v5, /device:TPU:0, one launch (start us, length us, event | category | flops | bytes accessed | tf_op | source)
XLA Modules:
  0.0 105.2 jit_solution(15770387459922506091)
XLA Ops:
  1.9 101.1 %layer.1 = (bf16[128,1024]{1,0:T(8,128)(2,1)S(1)}, bf16[128,1024]{1,0:T(8,128)(2,1)S(1)}, bf16[512,1024]{1,0:T(8,128)(2,1)S(1)}, f32[3,64,512]{2,1,0:T(8,128)S(1...) custom-call(bf16[128,1024]{1,0:T(8,128)(2,1)} %refs_0_.1, ...), custom_call_target="tpu_custom_call" | custom-call | tf_op jit(solution)/shard_map/layer/pallas_call | solution.py:954
  103.0 2.0 %finish.1 = (bf16[128,1024]{1,0:T(8,128)(2,1)}, bf16[128,1024]{1,0:T(8,128)(2,1)}, bf16[512,1024]{1,0:T(8,128)(2,1)}, f32[3,64,512]{2,1,0:T(8,128)}, f32[64,512]...) custom-call(bf16[128,1024]{1,0:T(8,128)(2,1)S(1)} %get-tuple-element, ...), custom_call_target="tpu_custom_call" | custom-call | tf_op jit(solution)/shard_map/finish/pallas_call | solution.py:1005

commit v6 on v5

--- a/solution.py
+++ b/solution.py
@@ -207,7 +207,7 @@
     HALF = T // 2
 
     def exchange_part(k, j):
-        return (at(j, HALF), pl.ds(0, D)) if k < 3 else (pl.ds(0, T), at(j, 256))
+        return (at(j // 2, HALF), at(j % 2, D // 2)) if k < 3 else (pl.ds(0, T), at(j, 256))
 
     def exchange_copy(k, j):
         rows, cols = exchange_part(k, j)
@@ -219,7 +219,12 @@
         for j in range(D // 256):
             cols = pl.ds(j * 256, 256)
             r.ex_out[k % 2, at(half, HALF), cols] = term(at(half, HALF), cols).astype(bf16)
-        exchange_copy(k, half).start()
+            if j % 2:
+                exchange_copy(k, 2 * half + j // 2).start()
+
+    def half_wait(k, half):
+        for j in range(2):
+            exchange_copy(k, 2 * half + j).wait()
 
     def exchange_start(k, term):
         for j in range(D // 256):
@@ -416,7 +421,7 @@
         return inv * (w - jnp.mean(w, axis=-1, keepdims=True) - unit * jnp.mean(w * unit, axis=-1, keepdims=True))
 
     def norm_rows(k, half, base, unit_ref):
-        exchange_copy(k, half).wait()
+        half_wait(k, half)
         for i in range(HALF // 16):
             rows = pl.ds(half * HALF + i * 16, 16)
             v = base[rows, :].astype(f32) + (exchanged(k, rows) + out_bias[k : k + 1, :])
@@ -543,6 +548,8 @@
         sm[6 + k : 7 + k, :] = col_sum(shifts)
 
     def output_rows(i):
+        if i % (HALF // 16) == 0:
+            half_wait(2, i // (HALF // 16))
         rows = at(i, 16)
         v = r.norm[rows, :] + (exchanged(2, rows) + out_bias[2:3, :])
         norm, unit, inv = normalize(v, 2)
@@ -556,8 +563,6 @@
 
     def output_norm():
         load(r.cotangent).wait()
-        for half in range(2):
-            exchange_copy(2, half).wait()
         sums_of(output_rows, 2)
 
     def hidden_grad(j):

time: 105 us -> 104 us (level)
    pallas_call x1, Pallas kernels: 101 us -> 100 us  [layer(): pl.pallas_call(functools.partial(kernel, names, got), out_shape=[pltpu.VM...]
where the time goes in v6:
time: 104 us
  Pallas kernels  102 us (98%)
  between operations  2.13 us (2%)
    pallas_call x1, Pallas kernels, layer(): pl.pallas_call(functools.partial(kernel, names, got), out_shape=[pltpu.VM...  100 us

profile of v6, /device:TPU:0, one launch (start us, length us, event | category | flops | bytes accessed | tf_op | source)
XLA Modules:
  0.0 104.1 jit_solution(15137865005495392326)
XLA Ops:
  1.9 100.0 %layer.1 = (bf16[128,1024]{1,0:T(8,128)(2,1)S(1)}, bf16[128,1024]{1,0:T(8,128)(2,1)S(1)}, bf16[512,1024]{1,0:T(8,128)(2,1)S(1)}, f32[3,64,512]{2,1,0:T(8,128)S(1...) custom-call(bf16[128,1024]{1,0:T(8,128)(2,1)} %refs_0_.1, ...), custom_call_target="tpu_custom_call" | custom-call | tf_op jit(solution)/shard_map/layer/pallas_call | solution.py:959
  101.9 2.0 %finish.1 = (bf16[128,1024]{1,0:T(8,128)(2,1)}, bf16[128,1024]{1,0:T(8,128)(2,1)}, bf16[512,1024]{1,0:T(8,128)(2,1)}, f32[3,64,512]{2,1,0:T(8,128)}, f32[64,512]...) custom-call(bf16[128,1024]{1,0:T(8,128)(2,1)S(1)} %get-tuple-element, ...), custom_call_target="tpu_custom_call" | custom-call | tf_op jit(solution)/shard_map/finish/pallas_call | solution.py:1010

commit v7 on v6

--- a/solution.py
+++ b/solution.py
@@ -270,10 +270,11 @@
             copy.wait_recv()
         for h in range(W // 256):
             cols = pl.ds(h * 256, 256)
-            rhs = ycat[u, :, cols]
-            core_out(u)[:, cols] = nn(xcat[w, at(1 - c, 256), :], rhs).astype(bf16)
-            kept(u)[:, cols] = nn(xcat[w, at(c, 256), :], rhs).astype(bf16)
+            core_out(u)[:, cols] = nn(xcat[w, at(1 - c, 256), :], ycat[u, :, cols]).astype(bf16)
         copy_core(u).start()
+        for h in range(W // 256):
+            cols = pl.ds(h * 256, 256)
+            kept(u)[:, cols] = nn(xcat[w, at(c, 256), :], ycat[u, :, cols]).astype(bf16)
 
     def local_sum(u, rows):
         if u < KV:

time: 104 us -> 105 us (level)
  no operation moved by 1% of the time
where the time goes in v7:
time: 105 us; the launch traced here: 104 us
  Pallas kernels  102 us (97%)
  between operations  2.13 us (2%)
    pallas_call x1, Pallas kernels, layer(): pl.pallas_call(functools.partial(kernel, names, got), out_shape=[pltpu.VM...  100 us

profile of v7, /device:TPU:0, one launch (start us, length us, event | category | flops | bytes accessed | tf_op | source)
XLA Modules:
  0.0 104.4 jit_solution(3380641041618993299)
XLA Ops:
  1.9 100.3 %layer.1 = (bf16[128,1024]{1,0:T(8,128)(2,1)S(1)}, bf16[128,1024]{1,0:T(8,128)(2,1)S(1)}, bf16[512,1024]{1,0:T(8,128)(2,1)S(1)}, f32[3,64,512]{2,1,0:T(8,128)S(1...) custom-call(bf16[128,1024]{1,0:T(8,128)(2,1)} %refs_0_.1, ...), custom_call_target="tpu_custom_call" | custom-call | tf_op jit(solution)/shard_map/layer/pallas_call | solution.py:960
  102.2 2.0 %finish.1 = (bf16[128,1024]{1,0:T(8,128)(2,1)}, bf16[128,1024]{1,0:T(8,128)(2,1)}, bf16[512,1024]{1,0:T(8,128)(2,1)}, f32[3,64,512]{2,1,0:T(8,128)}, f32[64,512]...) custom-call(bf16[128,1024]{1,0:T(8,128)(2,1)S(1)} %get-tuple-element, ...), custom_call_target="tpu_custom_call" | custom-call | tf_op jit(solution)/shard_map/finish/pallas_call | solution.py:1011
